TPU v7x, 128 devices: a whole 4x4x4 slice. The times are simulated.
128 devices in a mesh: seq: 128 (over z, x, y, core).
Axes of the slice: x: 4, y: 4, z: 4, core: 2. Of those that a mesh axis runs over, the one named last changes fastest.
Arguments:
- point_feats: bfloat16 [131072, 256], P('seq'), may hold values from -6 to 6
- scene_id: int32 [131072], P('seq'), may hold values from 0 to 127, never falling along the last dimension, each value on 1 to 2048 neighbouring positions
- hilbert_rank: int32 [131072], P('seq'), may hold values from 0 to 131071, as said below
- norm_gains: float32 [2, 2, 256], replicated, may hold values from 0.1 to 1.9
- w_qkv: bfloat16 [2, 256, 768], replicated
- w_proj: bfloat16 [2, 256, 256], replicated, may hold values from -0.375 to 0.375
- w_up: bfloat16 [2, 256, 1024], replicated, may hold values from -0.375 to 0.375
- w_down: bfloat16 [2, 1024, 256], replicated, may hold values from -0.1875 to 0.1875
Outputs:
- block_out: bfloat16 [131072, 256], P('seq')
Inputs may be any that keep to these rules, and one draw needn't show every extreme that they name: `hilbert_rank`: A permutation. Positions move in aligned tiles of 32 that keep their order: a tile either stays or goes to the same place on another device. One device sends at most 96 points to each of the two devices beside it (indices one up and one down, cyclically) and at most 32 points to any other device; both bounds are reached.
All inputs are finite; a program needn't handle non-finite values.
Results may differ from a plain program's by a relative error of at most 0.039.
The roundings to bfloat16 on the way count: a program that leaves them out, or rounds other values in their place, can miss the bound.
Values may be sent and summed in bfloat16 or wider, within the bound.
No kernel may reach another device: no remote copies, remote signals or barrier semaphores. Data moves between devices by JAX's collectives and lax.ppermute only.
A program may use at most 128 MiB of HBM per device.

v0:
```python
import functools

import jax
import jax.numpy as jnp
from jax import lax
from jax.experimental import pallas as pl
from jax.experimental.pallas import tpu as pltpu
from jax.sharding import PartitionSpec as P

C = 256
HEADS = 16
HEAD = 16
ROWS = 1024
FFN = 1024
TILES = 32
TILE = 32
MOST_TILES = 3
EPSILON = 1e-05
QUERY_BLOCK = 256
WINDOW = 512
ROW_BLOCK = 256
SPLIT_SCALE = 8.0
SCORE_LIMIT = 40.0
VALUE_LIMIT = 40.0
BF16 = jnp.bfloat16
F32 = jnp.float32
F8 = jnp.float8_e4m3fn
VMEM_BYTES = 56 << 20


def dot(left, right, left_dim=1, right_dim=0):
    return lax.dot_general(
        left, right, (((left_dim,), (right_dim,)), ((), ())), preferred_element_type=F32
    )


def layer_norm(values, gain):
    center = values - jnp.mean(values, axis=-1, keepdims=True)
    spread = jnp.mean(center * center, axis=-1, keepdims=True)
    return (center * lax.rsqrt(spread + EPSILON) * gain).astype(BF16)


def split(values):
    scaled = values.astype(F32) * SPLIT_SCALE
    high = scaled.astype(F8).astype(F32)
    low = scaled - high
    return high, low


def gelu(values):
    return 0.5 * values * (1.0 + lax.erf(values * (0.5**0.5)))


class Scratch:
    names = (
        "w_qkv", "w_proj", "w_up", "w_down", "key", "query", "key_split", "query_split",
        "value", "scene_col", "mask", "attended", "normed", "result", "sems", "out_sem",
    )

    def __init__(self, refs):
        for name, ref in zip(self.names, refs, strict=True):
            setattr(self, name, ref)


def scratch_shapes():
    return [
        pltpu.VMEM((C, 3 * C), BF16),
        pltpu.VMEM((C, C), BF16),
        pltpu.VMEM((C, FFN), BF16),
        pltpu.VMEM((FFN, C), BF16),
        pltpu.VMEM((2, ROWS, 128), BF16),
        pltpu.VMEM((2, 128, ROWS), BF16),
        pltpu.VMEM((HEADS // 2, ROWS, 128), F8),
        pltpu.VMEM((HEADS, 128, ROWS), F8),
        pltpu.VMEM((HEADS, 2 * HEAD, ROWS), BF16),
        pltpu.VMEM((ROWS, 128), F32),
        pltpu.VMEM((ROWS, QUERY_BLOCK), BF16),
        pltpu.VMEM((C, ROWS), BF16),
        pltpu.VMEM((ROWS, C), BF16),
        pltpu.VMEM((ROWS, C), BF16),
        pltpu.SemaphoreType.DMA((4,)),
        pltpu.SemaphoreType.DMA,
    ]


def start_weights(block, weights, s):
    copies = [
        pltpu.make_async_copy(source.at[block], target, s.sems.at[i])
        for i, (source, target) in enumerate(
            zip(weights, (s.w_qkv, s.w_proj, s.w_up, s.w_down), strict=True)
        )
    ]
    for copy in copies:
        copy.start()
    return copies


def project(x, gain, s):
    for start in range(0, ROWS, ROW_BLOCK):
        rows = slice(start, start + ROW_BLOCK)
        s.normed[rows] = layer_norm(x[rows].astype(F32), gain)
    normed = s.normed[...]
    query = dot(s.w_qkv[:, 0:C], normed, 0, 1).astype(BF16)
    value = dot(s.w_qkv[:, 2 * C : 3 * C], normed, 0, 1).astype(BF16)
    for head in range(HEADS):
        s.value[head, 0:HEAD, :] = value[HEAD * head : HEAD * (head + 1)]
        s.value[head, HEAD:, :] = jnp.ones((HEAD, ROWS), BF16)
    s.query[0] = query[0:128]
    s.query[1] = query[128:256]
    high, low = split(query)
    for head in range(HEADS):
        part = slice(HEAD * head, HEAD * (head + 1))
        both = jnp.concatenate([high[part].astype(BF16), low[part].astype(BF16)], axis=0).astype(F8)
        own, other = 64 * (head % 2), 64 * (1 - head % 2)
        s.query_split[head, own : own + 32, :] = both
        s.query_split[head, own + 32 : own + 64, :] = both
        s.query_split[head, other : other + 64, :] = jnp.zeros((64, ROWS), F8)
    squares = query.astype(F32) * query.astype(F32)
    query_norm = jnp.max(jnp.sum(squares.reshape(HEADS, HEAD, ROWS), axis=1), axis=1, keepdims=True)

    row = lax.broadcasted_iota(jnp.int32, (64, 256), 0)
    lane = lax.broadcasted_iota(jnp.int32, (64, 256), 1)
    same = row == (lane // 64) * HEAD + lane % HEAD
    spread_high = jnp.where(same & (lane % 64 < 32), 1.0, 0.0).astype(BF16)
    spread_low = jnp.where(same & (lane % 64 >= 32), 1.0, 0.0).astype(BF16)
    spread = jnp.concatenate([spread_high, spread_low], axis=0).astype(F8)
    channel = lax.broadcasted_iota(jnp.int32, (C, 128), 0)
    column = lax.broadcasted_iota(jnp.int32, (C, 128), 1)
    head_sum = jnp.where(channel // HEAD == column, 1.0, 0.0).astype(BF16)
    key_norm = jnp.zeros((1, 128), F32)
    highest = jnp.max(jnp.abs(query.astype(F32)))
    key_high = jnp.zeros((1, C), F32)
    for start in range(0, ROWS, ROW_BLOCK):
        rows = slice(start, start + ROW_BLOCK)
        key = dot(s.normed[rows], s.w_qkv[:, C : 2 * C]).astype(BF16)
        s.key[0, rows] = key[:, 0:128]
        s.key[1, rows] = key[:, 128:256]
        wide = key.astype(F32)
        key_high = jnp.maximum(key_high, jnp.max(jnp.abs(wide), axis=0, keepdims=True))
        norms = dot((wide * wide).astype(BF16), head_sum)
        key_norm = jnp.maximum(key_norm, jnp.max(norms, axis=0, keepdims=True))
        high, low = split(key)
        for quarter in range(4):
            lanes = slice(64 * quarter, 64 * quarter + 64)
            pair = jnp.concatenate([high[:, lanes], low[:, lanes]], axis=1).astype(F8)
            expanded = dot(pair, spread).astype(F8)
            s.key_split[2 * quarter, rows] = expanded[:, 0:128]
            s.key_split[2 * quarter + 1, rows] = expanded[:, 128:256]
    largest = jnp.maximum(highest, jnp.max(key_high))
    bound = 0.25 * 1.02 * jnp.sqrt(jnp.max(query_norm) * jnp.max(key_norm))
    return bound, largest


def make_mask(keys, count, queries, scene_row, s):
    row = scene_row[:, queries].astype(F32)
    for start in range(0, count, 128):
        col = s.scene_col[pl.ds(keys + start, 128), :]
        for lane in range(0, QUERY_BLOCK, 128):
            same = col == row[:, lane : lane + 128]
            s.mask[start : start + 128, lane : lane + 128] = jnp.where(same, 1.0, 0.0).astype(BF16)


def finish(head, queries, output, s):
    start = HEAD * head if isinstance(head, int) else pl.multiple_of(HEAD * head, HEAD)
    s.attended[pl.ds(start, HEAD), queries] = (
        output[0:HEAD] * (1.0 / output[HEAD : HEAD + 1])
    ).astype(BF16)


def attend_bounded(count, first_key, scene_row, s):
    def block(index, carry):
        queries = pl.ds(pl.multiple_of(index * QUERY_BLOCK, QUERY_BLOCK), QUERY_BLOCK)
        start = first_key(index)
        keys = pl.ds(start, count)
        make_mask(start, count, queries, scene_row, s)
        mask = s.mask[0:count]
        for head in range(HEADS):
            score = dot(s.key_split[head // 2, keys, :], s.query_split[head, :, queries])
            weight = jnp.exp(score * (0.25 / SPLIT_SCALE**2)).astype(BF16) * mask
            finish(head, queries, dot(s.value[head, :, keys], weight), s)
        return carry

    lax.fori_loop(0, ROWS // QUERY_BLOCK, block, 0)


def attend_any(scene_row, s):
    lane_head = lax.broadcasted_iota(jnp.int32, (1, 128), 1) // HEAD

    def block(index, carry):
        queries = pl.ds(pl.multiple_of(index * QUERY_BLOCK, QUERY_BLOCK), QUERY_BLOCK)
        make_mask(0, ROWS, queries, scene_row, s)

        def one_head(head, carry):
            group = head // 8
            lanes = jnp.where(lane_head == head % 8, 1.0, 0.0).astype(BF16)
            score = dot(s.key[group] * lanes, s.query[group, :, queries]) * 0.25
            score = jnp.where(s.mask[...] > 0, score, F32(-1e30))
            top = jnp.max(score, axis=0, keepdims=True)
            weight = jnp.exp(score - top).astype(BF16)
            finish(head, queries, dot(s.value[head], weight), s)
            return carry

        return lax.fori_loop(0, HEADS, one_head, carry)

    lax.fori_loop(0, ROWS // QUERY_BLOCK, block, 0)


def scene_columns(scene_row, s):
    for start in range(0, ROWS, 128):
        piece = scene_row[:, start : start + 128].astype(F32)
        s.scene_col[start : start + 128, :] = jnp.transpose(jnp.broadcast_to(piece, (128, 128)))


def mlp_rows(rows, x, gain, s):
    attended = jnp.transpose(s.attended[:, rows])
    middle = (x[rows].astype(F32) + dot(attended, s.w_proj[...])).astype(BF16)
    normed = layer_norm(middle.astype(F32), gain)
    hidden = gelu(dot(normed, s.w_up[...])).astype(BF16)
    s.result[rows] = (middle.astype(F32) + dot(hidden, s.w_down[...])).astype(BF16)


def first_kernel(
    me_ref, rank_ref, x, scene_row_ref, gains, w_qkv, w_proj, w_up, w_down,
    send, up, down, local, *scratch,
):
    s = Scratch(scratch)
    copies = start_weights(0, (w_qkv, w_proj, w_up, w_down), s)
    scene_row = scene_row_ref
    scene_columns(scene_row, s)
    copies[0].wait()
    bound, largest = project(x, gains[0, 0:1], s)
    quick = (bound <= SCORE_LIMIT) & (largest <= VALUE_LIMIT)

    @pl.when(quick)
    def _():
        attend_bounded(ROWS, lambda index: 0, scene_row, s)

    @pl.when(jnp.logical_not(quick))
    def _():
        attend_any(scene_row, s)

    for copy in copies[1:]:
        copy.wait()
    me = me_ref[0]
    above, below = lax.rem(me + 1, 128), lax.rem(me + 127, 128)
    slots = (jnp.int32(0), jnp.int32(0))
    for start in range(0, ROWS, ROW_BLOCK):
        mlp_rows(slice(start, start + ROW_BLOCK), x, gains[0, 1:2], s)

        def one_tile(tile, slots):
            owner = rank_ref[tile * TILE] // ROWS
            source = s.result.at[pl.ds(pl.multiple_of(tile * TILE, TILE), TILE)]

            def put(target, index):
                place = target.at[pl.ds(pl.multiple_of(index * TILE, TILE), TILE)]
                pltpu.make_async_copy(source, place, s.out_sem).start()

            is_up, is_down, stays = owner == above, owner == below, owner == me

            @pl.when(is_up)
            def _():
                put(up, jnp.minimum(slots[0], MOST_TILES - 1))

            @pl.when(is_down)
            def _():
                put(down, jnp.minimum(slots[1], MOST_TILES - 1))

            @pl.when(stays)
            def _():
                put(local, tile)

            @pl.when(jnp.logical_not(is_up | is_down | stays))
            def _():
                put(send, owner)

            return (slots[0] + is_up.astype(jnp.int32), slots[1] + is_down.astype(jnp.int32))

        slots = lax.fori_loop(start // TILE, (start + ROW_BLOCK) // TILE, one_tile, slots)
    pltpu.make_async_copy(s.result, local, s.out_sem).wait()


def second_kernel(
    me_ref, place_ref, source_ref, scene_ref, scene_row_ref, gains, received, from_below, from_above, local,
    w_qkv, w_proj, w_up, w_down, out, x, in_sem, *scratch,
):
    s = Scratch(scratch)
    me = me_ref[0]
    above, below = lax.rem(me + 1, 128), lax.rem(me + 127, 128)

    def fetch(index, slots):
        owner = source_ref[index]
        target = x.at[pl.ds(pl.multiple_of(index * TILE, TILE), TILE)]

        def get(source, tile):
            place = source.at[pl.ds(pl.multiple_of(tile * TILE, TILE), TILE)]
            pltpu.make_async_copy(place, target, in_sem).start()

        is_up, is_down, stays = owner == above, owner == below, owner == me

        @pl.when(is_up)
        def _():
            get(from_above, jnp.minimum(slots[0], MOST_TILES - 1))

        @pl.when(is_down)
        def _():
            get(from_below, jnp.minimum(slots[1], MOST_TILES - 1))

        @pl.when(stays)
        def _():
            get(local, place_ref[index])

        @pl.when(jnp.logical_not(is_up | is_down | stays))
        def _():
            get(received, owner)

        return (slots[0] + is_up.astype(jnp.int32), slots[1] + is_down.astype(jnp.int32))

    lax.fori_loop(0, TILES, fetch, (jnp.int32(0), jnp.int32(0)))
    copies = start_weights(1, (w_qkv, w_proj, w_up, w_down), s)
    scene_row = scene_row_ref
    scene_columns(scene_row, s)
    pltpu.make_async_copy(local, x, in_sem).wait()
    copies[0].wait()
    bound, largest = project(x, gains[1, 0:1], s)
    quick = (bound <= SCORE_LIMIT) & (largest <= VALUE_LIMIT)

    def window_start(index):
        first = scene_ref[index * QUERY_BLOCK]
        start = jnp.int32(0)
        for piece in range(1, (ROWS - WINDOW) // 128 + 1):
            start = start + (scene_ref[128 * piece - 1] < first).astype(jnp.int32)
        return pl.multiple_of(start * 128, 128)

    fits = quick
    for index in range(ROWS // QUERY_BLOCK):
        last = scene_ref[(index + 1) * QUERY_BLOCK - 1]
        end = window_start(index) + WINDOW
        after = scene_ref[jnp.minimum(end, ROWS - 1)]
        fits = fits & ((end >= ROWS) | (after > last))

    @pl.when(fits)
    def _():
        attend_bounded(WINDOW, window_start, scene_row, s)

    @pl.when(quick & jnp.logical_not(fits))
    def _():
        attend_bounded(ROWS, lambda index: 0, scene_row, s)

    @pl.when(jnp.logical_not(quick))
    def _():
        attend_any(scene_row, s)

    for copy in copies[1:]:
        copy.wait()
    for start in range(0, ROWS, ROW_BLOCK):
        mlp_rows(slice(start, start + ROW_BLOCK), x, gains[1, 1:2], s)

        def one_tile(index, carry):
            source = s.result.at[pl.ds(pl.multiple_of(index * TILE, TILE), TILE)]
            place = out.at[pl.ds(pl.multiple_of(place_ref[index] * TILE, TILE), TILE)]
            pltpu.make_async_copy(source, place, s.out_sem).start()
            return carry

        lax.fori_loop(start // TILE, (start + ROW_BLOCK) // TILE, one_tile, 0)
    pltpu.make_async_copy(s.result, out, s.out_sem).wait()


SMEM = pl.BlockSpec(memory_space=pltpu.SMEM)
VMEM = pl.BlockSpec(memory_space=pltpu.VMEM)
HBM = pl.BlockSpec(memory_space=pl.ANY)


def shards(point_feats, scene_id, hilbert_rank, norm_gains, w_qkv, w_proj, w_up, w_down):
    devices = lax.axis_size("seq")
    me = lax.axis_index("seq")
    me_array = me.reshape(1).astype(jnp.int32)
    weights = (w_qkv, w_proj, w_up, w_down)
    tagged = scene_id + (hilbert_rank // ROWS) * 128
    tags = lax.all_gather(tagged, "seq", tiled=True)
    params = pltpu.CompilerParams(vmem_limit_bytes=VMEM_BYTES)
    rows = jax.ShapeDtypeStruct((ROWS, C), BF16)
    few = jax.ShapeDtypeStruct((MOST_TILES * TILE, C), BF16)
    send, up, down, local = pl.pallas_call(
        first_kernel,
        in_specs=[SMEM, SMEM, VMEM, VMEM, VMEM, HBM, HBM, HBM, HBM],
        out_specs=[HBM] * 4,
        out_shape=[jax.ShapeDtypeStruct((devices * TILE, C), BF16), few, few, rows],
        scratch_shapes=scratch_shapes(),
        compiler_params=params,
        name="first_block",
    )(me_array, hilbert_rank, point_feats, scene_id.reshape(1, ROWS), norm_gains, *weights)

    received = lax.all_to_all(send, "seq", split_axis=0, concat_axis=0, tiled=True)
    ring = range(devices)
    from_below = lax.ppermute(up, "seq", [(i, (i + 1) % devices) for i in ring])
    from_above = lax.ppermute(down, "seq", [(i, (i - 1) % devices) for i in ring])

    tags, _ = lax.optimization_barrier((tags, local))
    tags = tags.reshape(devices, ROWS)
    mine = tags // 128 == me
    scenes = jnp.sum(jnp.where(mine, tags % 128, 0), axis=0).reshape(TILES, TILE)
    source = jnp.sum(jnp.where(mine, jnp.arange(devices, dtype=jnp.int32)[:, None], 0), axis=0)
    source = source.reshape(TILES, TILE)[:, 0]
    place = jnp.arange(TILES, dtype=jnp.int32)
    order = source * TILES + place
    rank = jnp.sum((order[None, :] < order[:, None]).astype(jnp.int32), axis=1)
    chosen = rank[None, :] == place[:, None]
    place_sorted = jnp.sum(jnp.where(chosen, place[None, :], 0), axis=1)
    source_sorted = jnp.sum(jnp.where(chosen, source[None, :], 0), axis=1)
    scene_sorted = jnp.sum(jnp.where(chosen[:, :, None], scenes[None], 0), axis=1).reshape(ROWS)

    return pl.pallas_call(
        second_kernel,
        in_specs=[SMEM, SMEM, SMEM, SMEM, VMEM, VMEM] + [HBM] * 8,
        out_specs=HBM,
        out_shape=rows,
        scratch_shapes=[pltpu.VMEM((ROWS, C), BF16), pltpu.SemaphoreType.DMA] + scratch_shapes(),
        compiler_params=params,
        name="second_block",
    )(
        me_array, place_sorted, source_sorted, scene_sorted, scene_sorted.reshape(1, ROWS), norm_gains,
        received, from_below, from_above, local, *weights,
    )


def solution(mesh):
    placed = (P("seq", None), P("seq"), P("seq"), P(), P(), P(), P(), P())
    return jax.shard_map(
        shards, mesh=mesh, in_specs=placed, out_specs=P("seq", None), check_vma=False
    )
```

profile of v0, /device:TPU:0, one launch (start us, length us, event | category | flops | bytes accessed | tf_op | source)
XLA Modules:
  0.0 174.7 jit_solution(9517718427019767156)
XLA Ops:
  0.0 52.1 %first_block.1 = (bf16[4096,256]{1,0:T(8,128)(2,1)}, bf16[96,256]{1,0:T(8,128)(2,1)}, bf16[96,256]{1,0:T(8,128)(2,1)}, bf16[1024,256]{1,0:T(8,128)(2,1)}) custom-call(s32[1]{0:T(128)} %bitcast.me_ref, s32[1024]{0:T(1024)} %rank_ref.1, bf16[1024,256]{1,0:T(8,128)(2,1)} %x.1, s32[1,1024]{1,0:T(1,128)} %bitcast.6, f32[2,2,256]{2,1,0:T(2,128)} %gains.3, ...), custom_call_target="tpu_custom_call" | custom-call | tf_op jit(solution)/shard_map/first_block/pallas_call | solution.py:383
  52.1 0.0 copy-start.6
  52.1 0.0 copy-start.5
  52.1 0.0 copy-start.3
  52.1 0.0 copy-start.4
  52.2 11.1 %all-to-all-start = ((bf16[128,32,256]{2,1,0:T(8,128)(2,1)}), bf16[128,32,256]{2,1,0:T(8,128)(2,1)S(1)}, u32[]{:S(2)}, u32[]{:S(2)}) async-start(bf16[128,32,256]{2,1,0:T(8,128)(2,1)} %bitcast.5), calls=%async_computation | async-start | bytes 4194304 | tf_op jit(solution)/shard_map/all_to_all | solution.py:393
  63.3 0.0 copy-done.6
  63.3 0.1 collective-permute-start
  63.4 0.0 copy-done.5
  63.4 7.2 %collective-permute-start.1 = (bf16[96,256]{1,0:T(8,128)(2,1)S(1)}, bf16[96,256]{1,0:T(8,128)(2,1)S(1)}, u32[]{:S(2)}, u32[]{:S(2)}) collective-permute-start(bf16[96,256]{1,0:T(8,128)(2,1)S(1)} %copy-done.5), channel_id=1, source_target_pairs={{0,127},{1,0},{2,1},{3,2},{4,3},{5,4},{6,5},{7,6},{8,7},{9,8},{10,... | collective-permute-start | bytes 147464 | tf_op jit(solution)/shard_map/ppermute | solution.py:396
  70.6 0.0 copy-done.3
  70.6 0.0 copy-done.4
  70.6 47.0 %all_gather.3 = s32[131072]{0:T(1024)S(1)} all-gather(s32[1024]{0:T(1024)S(1)} %fusion.7), channel_id=1, replica_groups=mesh['seq'=128] {'seq'}, dimensions={0}, use_global_device_ids=true | all-gather | bytes 528384 | tf_op jit(solution)/shard_map/all_gather | solution.py:379
  117.6 0.1 reshape.48
  117.7 0.5 fusion.2
  118.3 0.1 broadcast_in_dim.64
  118.3 0.1 reshape.49
  118.4 0.1 add_reduce_fusion
  118.5 0.2 convert_reduce_fusion
  118.7 0.2 select_reduce_fusion
  119.0 0.7 select_reduce_fusion.2
  119.7 0.7 reshape_reshape.3.scene_row_ref
  120.3 0.7 reshape.50.scene_ref
  121.0 0.0 collective-permute-done.from_below
  121.0 0.0 copy-start.1
  121.0 0.0 collective-permute-done.1.from_above
  121.0 0.0 copy-start.2
  121.0 0.0 all-to-all-done
  121.0 0.0 copy-start
  121.1 0.6 copy-done.1
  121.6 0.0 copy-done.2
  121.6 0.7 copy-done
  122.4 52.1 %second_block.1 = bf16[1024,256]{1,0:T(8,128)(2,1)} custom-call(s32[1]{0:T(128)} %bitcast.me_ref, s32[32]{0:T(128)} %get-tuple-element.20.place_ref, s32[32]{0:T(128)} %get-tuple-element.19.source_ref, s32[1024]{0:T(1024)} %reshape.50.scene_ref, s32[1,1024]{1,0:T(1,128)} %reshape_reshape.3.scene_row_ref, f32[2,2,256]{2,1,0:T(2,128)} %gains.3, ...), custom_call_target="tpu_custom_call" | custom-call | tf_op jit(solution)/shard_map/second_block/pallas_call | solution.py:412
  (3 shorter events, 0.0 us)
Async XLA Ops:
  52.1 11.2 %copy-start.6 = (bf16[96,256]{1,0:T(8,128)(2,1)S(1)}, bf16[96,256]{1,0:T(8,128)(2,1)}, u32[]{:S(2)}) copy-start(bf16[96,256]{1,0:T(8,128)(2,1)} %get-tuple-element.13) | copy-start | bytes 147460
  52.1 11.3 %copy-start.5 = (bf16[96,256]{1,0:T(8,128)(2,1)S(1)}, bf16[96,256]{1,0:T(8,128)(2,1)}, u32[]{:S(2)}) copy-start(bf16[96,256]{1,0:T(8,128)(2,1)} %get-tuple-element.14) | copy-start | bytes 147460
  52.1 18.4 %copy-start.3 = (s32[1024]{0:T(1024)S(1)}, s32[1024]{0:T(1024)}, u32[]{:S(2)}) copy-start(s32[1024]{0:T(1024)} %param.9) | copy-start | bytes 12292
  52.1 18.4 %copy-start.4 = (s32[1024]{0:T(1024)S(1)}, s32[1024]{0:T(1024)}, u32[]{:S(2)}) copy-start(s32[1024]{0:T(1024)} %rank_ref.1) | copy-start | bytes 12292
  52.2 68.9 %all-to-all-start = ((bf16[128,32,256]{2,1,0:T(8,128)(2,1)}), bf16[128,32,256]{2,1,0:T(8,128)(2,1)S(1)}, u32[]{:S(2)}, u32[]{:S(2)}) async-start(bf16[128,32,256]{2,1,0:T(8,128)(2,1)} %bitcast.5), calls=%async_computation | async-start | bytes 4194304 | tf_op jit(solution)/shard_map/all_to_all | solution.py:393
  63.3 57.7 %collective-permute-start = (bf16[96,256]{1,0:T(8,128)(2,1)S(1)}, bf16[96,256]{1,0:T(8,128)(2,1)S(1)}, u32[]{:S(2)}, u32[]{:S(2)}) collective-permute-start(bf16[96,256]{1,0:T(8,128)(2,1)S(1)} %copy-done.6), channel_id=1, source_target_pairs={{0,1},{1,2},{2,3},{3,4},{4,5},{5,6},{6,7},{7,8},{8,9},{9,10},{10,1... | collective-permute-start | bytes 147464 | tf_op jit(solution)/shard_map/ppermute | solution.py:395
  63.4 57.6 %collective-permute-start.1 = (bf16[96,256]{1,0:T(8,128)(2,1)S(1)}, bf16[96,256]{1,0:T(8,128)(2,1)S(1)}, u32[]{:S(2)}, u32[]{:S(2)}) collective-permute-start(bf16[96,256]{1,0:T(8,128)(2,1)S(1)} %copy-done.5), channel_id=1, source_target_pairs={{0,127},{1,0},{2,1},{3,2},{4,3},{5,4},{6,5},{7,6},{8,7},{9,8},{10,... | collective-permute-start | bytes 147464 | tf_op jit(solution)/shard_map/ppermute | solution.py:396
  121.0 0.6 copy-start.1
  121.0 0.6 copy-start.2
  121.0 1.4 copy-start
where the time goes:
time: 176 us; the launch traced here: 175 us
  Pallas kernels  104 us (59%)
  blocking collectives  47 us (27%)
  starting transfers between devices  18.4 us (10%)
  local copies, waits for them, and re-layouts  2.93 us (2%)
  other arithmetic  1.81 us (1%)
    pallas_call x1, Pallas kernels, shards(): pl.pallas_call(first_kernel, in_specs=[SMEM, SMEM, VMEM, VMEM, VMEM, HBM,...  52.1 us
    pallas_call x1, Pallas kernels, shards(): pl.pallas_call(second_kernel, in_specs=[SMEM, SMEM, SMEM, SMEM, VMEM, VME...  52.1 us
    all_gather x1, blocking collectives, shards(): tags = lax.all_gather(tagged, 'seq', tiled=True)  47 us
    all_to_all x1, starting transfers between devices, shards(): lax.all_to_all(send, 'seq', split_axis=0, concat_axis=0, tiled=True)  11.1 us
    ppermute x1, starting transfers between devices, shards(): lax.ppermute(down, 'seq', [(i, (i - 1) % devices) for i in ring])  7.15 us
  transfers between devices with their start and end apart: 3, of which 0 were waited for; matrix products, arithmetic and copies ran while one was open for 2% of the time, Pallas kernels for 0%

commit v1 on v0

--- a/solution.py
+++ b/solution.py
@@ -151,12 +151,11 @@
     return bound, largest
 
 
-def make_mask(keys, count, queries, scene_row, s):
-    row = scene_row[:, queries].astype(F32)
-    for start in range(0, count, 128):
-        col = s.scene_col[pl.ds(keys + start, 128), :]
-        for lane in range(0, QUERY_BLOCK, 128):
-            same = col == row[:, lane : lane + 128]
+def make_mask(keys, count, index, scenes, s):
+    for lane in range(0, QUERY_BLOCK, 128):
+        row = scenes[pl.ds(index * (QUERY_BLOCK // 128) + lane // 128, 1), :].astype(F32)
+        for start in range(0, count, 128):
+            same = s.scene_col[pl.ds(keys + start, 128), :] == row
             s.mask[start : start + 128, lane : lane + 128] = jnp.where(same, 1.0, 0.0).astype(BF16)
 
 
@@ -167,12 +166,12 @@
     ).astype(BF16)
 
 
-def attend_bounded(count, first_key, scene_row, s):
+def attend_bounded(count, first_key, scenes, s):
     def block(index, carry):
         queries = pl.ds(pl.multiple_of(index * QUERY_BLOCK, QUERY_BLOCK), QUERY_BLOCK)
         start = first_key(index)
         keys = pl.ds(start, count)
-        make_mask(start, count, queries, scene_row, s)
+        make_mask(start, count, index, scenes, s)
         mask = s.mask[0:count]
         for head in range(HEADS):
             score = dot(s.key_split[head // 2, keys, :], s.query_split[head, :, queries])
@@ -183,12 +182,12 @@
     lax.fori_loop(0, ROWS // QUERY_BLOCK, block, 0)
 
 
-def attend_any(scene_row, s):
+def attend_any(scenes, s):
     lane_head = lax.broadcasted_iota(jnp.int32, (1, 128), 1) // HEAD
 
     def block(index, carry):
         queries = pl.ds(pl.multiple_of(index * QUERY_BLOCK, QUERY_BLOCK), QUERY_BLOCK)
-        make_mask(0, ROWS, queries, scene_row, s)
+        make_mask(0, ROWS, index, scenes, s)
 
         def one_head(head, carry):
             group = head // 8
@@ -205,9 +204,9 @@
     lax.fori_loop(0, ROWS // QUERY_BLOCK, block, 0)
 
 
-def scene_columns(scene_row, s):
+def scene_columns(scenes, s):
     for start in range(0, ROWS, 128):
-        piece = scene_row[:, start : start + 128].astype(F32)
+        piece = scenes[start // 128 : start // 128 + 1, :].astype(F32)
         s.scene_col[start : start + 128, :] = jnp.transpose(jnp.broadcast_to(piece, (128, 128)))
 
 
@@ -219,30 +218,99 @@
     s.result[rows] = (middle.astype(F32) + dot(hidden, s.w_down[...])).astype(BF16)
 
 
+def neighbours(me):
+    return lax.rem(me + 1, 128), lax.rem(me + 127, 128)
+
+
+def write_notes(me, rank_ref, scenes, notes):
+    notes[...] = jnp.zeros_like(notes)
+    above, below = neighbours(me)
+    group = lax.broadcasted_iota(jnp.int32, (1, 128), 1) // TILE
+    slots = (jnp.int32(0), jnp.int32(0))
+    for tile in range(TILES):
+        owner = rank_ref[tile * TILE] // ROWS
+        is_up, is_down = (owner == above).astype(jnp.int32), (owner == below).astype(jnp.int32)
+        slot = is_up * slots[0] + is_down * slots[1]
+        row = scenes[tile // 4 : tile // 4 + 1, (tile % 4) * TILE : (tile % 4 + 1) * TILE]
+        row = jnp.concatenate([row] * 4, axis=1) + 128 * (tile + 1)
+        notes[owner] = notes[owner] + jnp.where(group == slot, row, 0)
+        slots = (slots[0] + is_up, slots[1] + is_down)
+
+
+def plan_kernel(me_ref, rank_ref, scene_ref, notes_ref, notes, scenes, plan, scene_out):
+    me = me_ref[0]
+    group = lax.broadcasted_iota(jnp.int32, (1, 128), 1) // TILE
+    scene_out[...] = jnp.zeros_like(scene_out)
+
+    def clear(index, carry):
+        plan[index] = 0
+        return carry
+
+    lax.fori_loop(0, 4 * TILES, clear, 0)
+
+    def add(index, place, source, first, last, row, slot):
+        plan[index] = place
+        plan[TILES + index] = source
+        plan[2 * TILES + index] = first
+        plan[3 * TILES + index] = last
+        lane = lax.rem(index, 4)
+        moved = pltpu.roll(row, TILE * lax.rem(lane - slot + 4, 4), 1)
+        line = pl.ds(index // 4, 1)
+        scene_out[line, :] = jnp.where(group == lane, moved, scene_out[line, :])
+
+    def one_source(source, count):
+        def received(slot, count):
+            note = notes_ref[source, 0, slot * TILE]
+
+            @pl.when(note > 0)
+            def _():
+                last = notes_ref[source, 0, slot * TILE + TILE - 1]
+                add(count, note // 128 - 1, source, note % 128, last % 128, notes[source] % 128, slot)
+
+            return count + (note > 0).astype(jnp.int32)
+
+        def stays(tile, count):
+            keep = rank_ref[tile * TILE] // ROWS == me
+
+            @pl.when(keep)
+            def _():
+                first, last = scene_ref[tile * TILE], scene_ref[tile * TILE + TILE - 1]
+                row = scenes[pl.ds(tile // 4, 1), :]
+                add(count, tile, me, first, last, row, lax.rem(tile, 4))
+
+            return count + keep.astype(jnp.int32)
+
+        mine = source == me
+        count = lax.fori_loop(0, jnp.where(mine, 0, MOST_TILES), received, count)
+        return lax.fori_loop(0, jnp.where(mine, TILES, 0), stays, count)
+
+    lax.fori_loop(0, 128, one_source, jnp.int32(0))
+
+
 def first_kernel(
-    me_ref, rank_ref, x, scene_row_ref, gains, w_qkv, w_proj, w_up, w_down,
-    send, up, down, local, *scratch,
+    me_ref, rank_ref, x, scenes, gains, w_qkv, w_proj, w_up, w_down,
+    send, notes, up, down, local, *scratch,
 ):
     s = Scratch(scratch)
     copies = start_weights(0, (w_qkv, w_proj, w_up, w_down), s)
-    scene_row = scene_row_ref
-    scene_columns(scene_row, s)
+    write_notes(me_ref[0], rank_ref, scenes, notes)
+    scene_columns(scenes, s)
     copies[0].wait()
     bound, largest = project(x, gains[0, 0:1], s)
     quick = (bound <= SCORE_LIMIT) & (largest <= VALUE_LIMIT)
 
     @pl.when(quick)
     def _():
-        attend_bounded(ROWS, lambda index: 0, scene_row, s)
+        attend_bounded(ROWS, lambda index: 0, scenes, s)
 
     @pl.when(jnp.logical_not(quick))
     def _():
-        attend_any(scene_row, s)
+        attend_any(scenes, s)
 
     for copy in copies[1:]:
         copy.wait()
     me = me_ref[0]
-    above, below = lax.rem(me + 1, 128), lax.rem(me + 127, 128)
+    above, below = neighbours(me)
     slots = (jnp.int32(0), jnp.int32(0))
     for start in range(0, ROWS, ROW_BLOCK):
         mlp_rows(slice(start, start + ROW_BLOCK), x, gains[0, 1:2], s)
@@ -280,15 +348,15 @@
 
 
 def second_kernel(
-    me_ref, place_ref, source_ref, scene_ref, scene_row_ref, gains, received, from_below, from_above, local,
+    me_ref, plan, scenes, gains, received, from_below, from_above, local,
     w_qkv, w_proj, w_up, w_down, out, x, in_sem, *scratch,
 ):
     s = Scratch(scratch)
     me = me_ref[0]
-    above, below = lax.rem(me + 1, 128), lax.rem(me + 127, 128)
+    above, below = neighbours(me)
 
     def fetch(index, slots):
-        owner = source_ref[index]
+        owner = plan[TILES + index]
         target = x.at[pl.ds(pl.multiple_of(index * TILE, TILE), TILE)]
 
         def get(source, tile):
@@ -307,7 +375,7 @@
 
         @pl.when(stays)
         def _():
-            get(local, place_ref[index])
+            get(local, plan[index])
 
         @pl.when(jnp.logical_not(is_up | is_down | stays))
         def _():
@@ -317,38 +385,37 @@
 
     lax.fori_loop(0, TILES, fetch, (jnp.int32(0), jnp.int32(0)))
     copies = start_weights(1, (w_qkv, w_proj, w_up, w_down), s)
-    scene_row = scene_row_ref
-    scene_columns(scene_row, s)
+    scene_columns(scenes, s)
     pltpu.make_async_copy(local, x, in_sem).wait()
     copies[0].wait()
     bound, largest = project(x, gains[1, 0:1], s)
     quick = (bound <= SCORE_LIMIT) & (largest <= VALUE_LIMIT)
 
     def window_start(index):
-        first = scene_ref[index * QUERY_BLOCK]
+        first = plan[2 * TILES + index * (QUERY_BLOCK // TILE)]
         start = jnp.int32(0)
         for piece in range(1, (ROWS - WINDOW) // 128 + 1):
-            start = start + (scene_ref[128 * piece - 1] < first).astype(jnp.int32)
+            start = start + (plan[3 * TILES + 4 * piece - 1] < first).astype(jnp.int32)
         return pl.multiple_of(start * 128, 128)
 
     fits = quick
     for index in range(ROWS // QUERY_BLOCK):
-        last = scene_ref[(index + 1) * QUERY_BLOCK - 1]
+        last = plan[3 * TILES + (index + 1) * (QUERY_BLOCK // TILE) - 1]
         end = window_start(index) + WINDOW
-        after = scene_ref[jnp.minimum(end, ROWS - 1)]
+        after = plan[2 * TILES + jnp.minimum(end // TILE, TILES - 1)]
         fits = fits & ((end >= ROWS) | (after > last))
 
     @pl.when(fits)
     def _():
-        attend_bounded(WINDOW, window_start, scene_row, s)
+        attend_bounded(WINDOW, window_start, scenes, s)
 
     @pl.when(quick & jnp.logical_not(fits))
     def _():
-        attend_bounded(ROWS, lambda index: 0, scene_row, s)
+        attend_bounded(ROWS, lambda index: 0, scenes, s)
 
     @pl.when(jnp.logical_not(quick))
     def _():
-        attend_any(scene_row, s)
+        attend_any(scenes, s)
 
     for copy in copies[1:]:
         copy.wait()
@@ -357,7 +424,7 @@
 
         def one_tile(index, carry):
             source = s.result.at[pl.ds(pl.multiple_of(index * TILE, TILE), TILE)]
-            place = out.at[pl.ds(pl.multiple_of(place_ref[index] * TILE, TILE), TILE)]
+            place = out.at[pl.ds(pl.multiple_of(plan[index] * TILE, TILE), TILE)]
             pltpu.make_async_copy(source, place, s.out_sem).start()
             return carry
 
@@ -375,52 +442,52 @@
     me = lax.axis_index("seq")
     me_array = me.reshape(1).astype(jnp.int32)
     weights = (w_qkv, w_proj, w_up, w_down)
-    tagged = scene_id + (hilbert_rank // ROWS) * 128
-    tags = lax.all_gather(tagged, "seq", tiled=True)
+    scenes = scene_id.reshape(ROWS // 128, 128)
     params = pltpu.CompilerParams(vmem_limit_bytes=VMEM_BYTES)
     rows = jax.ShapeDtypeStruct((ROWS, C), BF16)
     few = jax.ShapeDtypeStruct((MOST_TILES * TILE, C), BF16)
-    send, up, down, local = pl.pallas_call(
+    send, notes, up, down, local = pl.pallas_call(
         first_kernel,
         in_specs=[SMEM, SMEM, VMEM, VMEM, VMEM, HBM, HBM, HBM, HBM],
-        out_specs=[HBM] * 4,
-        out_shape=[jax.ShapeDtypeStruct((devices * TILE, C), BF16), few, few, rows],
+        out_specs=[HBM, VMEM, HBM, HBM, HBM],
+        out_shape=[
+            jax.ShapeDtypeStruct((devices * TILE, C), BF16),
+            jax.ShapeDtypeStruct((devices, 1, 128), jnp.int32),
+            few,
+            few,
+            rows,
+        ],
         scratch_shapes=scratch_shapes(),
         compiler_params=params,
         name="first_block",
-    )(me_array, hilbert_rank, point_feats, scene_id.reshape(1, ROWS), norm_gains, *weights)
+    )(me_array, hilbert_rank, point_feats, scenes, norm_gains, *weights)
 
     received = lax.all_to_all(send, "seq", split_axis=0, concat_axis=0, tiled=True)
     ring = range(devices)
     from_below = lax.ppermute(up, "seq", [(i, (i + 1) % devices) for i in ring])
     from_above = lax.ppermute(down, "seq", [(i, (i - 1) % devices) for i in ring])
-
-    tags, _ = lax.optimization_barrier((tags, local))
-    tags = tags.reshape(devices, ROWS)
-    mine = tags // 128 == me
-    scenes = jnp.sum(jnp.where(mine, tags % 128, 0), axis=0).reshape(TILES, TILE)
-    source = jnp.sum(jnp.where(mine, jnp.arange(devices, dtype=jnp.int32)[:, None], 0), axis=0)
-    source = source.reshape(TILES, TILE)[:, 0]
-    place = jnp.arange(TILES, dtype=jnp.int32)
-    order = source * TILES + place
-    rank = jnp.sum((order[None, :] < order[:, None]).astype(jnp.int32), axis=1)
-    chosen = rank[None, :] == place[:, None]
-    place_sorted = jnp.sum(jnp.where(chosen, place[None, :], 0), axis=1)
-    source_sorted = jnp.sum(jnp.where(chosen, source[None, :], 0), axis=1)
-    scene_sorted = jnp.sum(jnp.where(chosen[:, :, None], scenes[None], 0), axis=1).reshape(ROWS)
+    notes = lax.all_to_all(notes, "seq", split_axis=0, concat_axis=0, tiled=True)
+    plan, scenes = pl.pallas_call(
+        plan_kernel,
+        in_specs=[SMEM, SMEM, SMEM, SMEM, VMEM, VMEM],
+        out_specs=[SMEM, VMEM],
+        out_shape=[
+            jax.ShapeDtypeStruct((4 * TILES,), jnp.int32),
+            jax.ShapeDtypeStruct((ROWS // 128, 128), jnp.int32),
+        ],
+        compiler_params=params,
+        name="plan",
+    )(me_array, hilbert_rank, scene_id, notes, notes, scenes)
 
     return pl.pallas_call(
         second_kernel,
-        in_specs=[SMEM, SMEM, SMEM, SMEM, VMEM, VMEM] + [HBM] * 8,
+        in_specs=[SMEM, SMEM, VMEM, VMEM] + [HBM] * 8,
         out_specs=HBM,
         out_shape=rows,
         scratch_shapes=[pltpu.VMEM((ROWS, C), BF16), pltpu.SemaphoreType.DMA] + scratch_shapes(),
         compiler_params=params,
         name="second_block",
-    )(
-        me_array, place_sorted, source_sorted, scene_sorted, scene_sorted.reshape(1, ROWS), norm_gains,
-        received, from_below, from_above, local, *weights,
-    )
+    )(me_array, plan, scenes, norm_gains, received, from_below, from_above, local, *weights)
 
 
 def solution(mesh):

time: 176 us -> 163 us (0.926)
  blocking collectives: 47 us -> 20.9 us
  Pallas kernels: 104 us -> 118 us
  waiting for transfers between devices: 0.01 us -> 10.5 us
  starting transfers between devices: 18.4 us -> 12.2 us
  other arithmetic: 1.81 us -> 0 us
    all_gather x1 -> x0, blocking collectives: 47 us -> none  [shards(): tags = lax.all_gather(tagged, 'seq', tiled=True)]
    all_to_all x0 -> x1, blocking collectives: none -> 20.9 us  [shards(): lax.all_to_all(notes, 'seq', split_axis=0, concat_axis=0, tiled=True)]
    pallas_call x1 -> x2, Pallas kernels: 52.1 us -> 64.7 us  [the longest x1 51.9 us: shards(): pl.pallas_call(second_kernel, in_specs=[SMEM, SMEM, VMEM, VMEM] + [HBM] *...]
    ppermute x1, waiting for transfers between devices: 0.01 us -> 10.5 us  [shards(): from_below = lax.ppermute(up, 'seq', [(i, (i + 1) % devices) for i in ring])]
    all_to_all x1, starting transfers between devices: 11.1 us -> 4.78 us  [shards(): lax.all_to_all(send, 'seq', split_axis=0, concat_axis=0, tiled=True)]
  transfers between devices with their start and end apart: 3 -> 3, of which waited for: 0 -> 1; matrix products, arithmetic and copies ran while one was open for 2% -> 0% of each run, Pallas kernels for 0% -> 8%
where the time goes in v1:
time: 163 us
  Pallas kernels  118 us (72%)
  blocking collectives  20.9 us (13%)
  starting transfers between devices  12.2 us (7%)
  waiting for transfers between devices  10.5 us (6%)
    pallas_call x1, Pallas kernels, shards(): pl.pallas_call(first_kernel, in_specs=[SMEM, SMEM, VMEM, VMEM, VMEM, HBM,...  53.1 us
    pallas_call x1, Pallas kernels, shards(): pl.pallas_call(second_kernel, in_specs=[SMEM, SMEM, VMEM, VMEM] + [HBM] *...  51.9 us
    all_to_all x1, blocking collectives, shards(): lax.all_to_all(notes, 'seq', split_axis=0, concat_axis=0, tiled=True)  20.9 us
    pallas_call x1, Pallas kernels, shards(): pl.pallas_call(plan_kernel, in_specs=[SMEM, SMEM, SMEM, SMEM, VMEM, VMEM]...  12.8 us
    ppermute x1, waiting for transfers between devices, shards(): from_below = lax.ppermute(up, 'seq', [(i, (i + 1) % devices) for i in ring])  10.5 us
    ppermute x1, starting transfers between devices, shards(): lax.ppermute(down, 'seq', [(i, (i - 1) % devices) for i in ring])  7.3 us
    all_to_all x1, starting transfers between devices, shards(): lax.all_to_all(send, 'seq', split_axis=0, concat_axis=0, tiled=True)  4.78 us
  transfers between devices with their start and end apart: 3, of which 1 were waited for; matrix products, arithmetic and copies ran while one was open for 0% of the time, Pallas kernels for 8%

profile of v1, /device:TPU:0, one launch (start us, length us, event | category | flops | bytes accessed | tf_op | source)
XLA Modules:
  0.0 163.0 jit_solution(12627880240469712687)
XLA Ops:
  0.0 53.1 %first_block.1 = (bf16[4096,256]{1,0:T(8,128)(2,1)}, s32[128,1,128]{2,1,0:T(1,128)}, bf16[96,256]{1,0:T(8,128)(2,1)}, bf16[96,256]{1,0:T(8,128)(2,1)}, bf16[1024,256]{1,0:T(8,128)(2,1)}) custom-call(s32[1]{0:T(128)} %bitcast.me_ref, s32[1024]{0:T(1024)} %rank_ref.3, bf16[1024,256]{1,0:T(8,128)(2,1)} %x.1, s32[8,128]{1,0:T(8,128)} %bitcast.6, ...), custom_call_target="tpu_custom_call" | custom-call | tf_op jit(solution)/shard_map/first_block/pallas_call | solution.py:449
  53.1 20.9 %all_to_all.16.notes_ref.notes = s32[128,1,128]{2,1,0:T(1,128)} all-to-all(s32[128,1,128]{2,1,0:T(1,128)} %get-tuple-element.12), channel_id=1, replica_groups=mesh['seq'=128] {'seq'}, dimensions={0} | all-to-all | bytes 131072 | tf_op jit(solution)/shard_map/all_to_all | solution.py:469
  74.0 0.0 copy-start.4
  74.0 0.0 copy-start.3
  74.0 4.8 %all-to-all-start.1 = ((bf16[128,32,256]{2,1,0:T(8,128)(2,1)}), bf16[128,32,256]{2,1,0:T(8,128)(2,1)S(1)}, u32[]{:S(2)}, u32[]{:S(2)}) async-start(bf16[128,32,256]{2,1,0:T(8,128)(2,1)} %bitcast.5), calls=%async_computation.1 | async-start | bytes 4194304 | tf_op jit(solution)/shard_map/all_to_all | solution.py:465
  78.8 0.0 copy-done.4
  78.8 0.1 collective-permute-start
  78.9 0.0 copy-done.3
  78.9 7.3 %collective-permute-start.1 = (bf16[96,256]{1,0:T(8,128)(2,1)S(1)}, bf16[96,256]{1,0:T(8,128)(2,1)S(1)}, u32[]{:S(2)}, u32[]{:S(2)}) collective-permute-start(bf16[96,256]{1,0:T(8,128)(2,1)S(1)} %copy-done.3), channel_id=1, source_target_pairs={{0,127},{1,0},{2,1},{3,2},{4,3},{5,4},{6,5},{7,6},{8,7},{9,8},{10,... | collective-permute-start | bytes 147464 | tf_op jit(solution)/shard_map/ppermute | solution.py:468
  86.2 12.8 %plan.1 = (s32[128]{0:T(128)}, s32[8,128]{1,0:T(8,128)}) custom-call(s32[1]{0:T(128)} %bitcast.me_ref, s32[1024]{0:T(1024)} %rank_ref.3, s32[1024]{0:T(1024)} %scene_ref.1, s32[128,1,128]{2,1,0:T(1,128)} %all_to_all.16.notes_ref.notes, s32[128,1,128]{2,1,0:T(1,128)} %all_to_all.16.notes_ref.notes, s32[8,128]{1,0:T(8,128)} %bitcast.7), custom_call_target="tpu_custom_call" | custom-call | tf_op jit(solution)/shard_map/plan/pallas_call | solution.py:470
  99.0 10.5 %collective-permute-done.from_below = bf16[96,256]{1,0:T(8,128)(2,1)S(1)} collective-permute-done((bf16[96,256]{1,0:T(8,128)(2,1)S(1)}, bf16[96,256]{1,0:T(8,128)(2,1)S(1)}, u32[]{:S(2)}, u32[]{:S(2)}) %collective-permute-start) | collective-permute-done | bytes 49184 | tf_op jit(solution)/shard_map/ppermute | solution.py:467
  109.5 0.0 copy-start.1
  109.5 0.0 collective-permute-done.1.from_above
  109.5 0.0 copy-start.2
  109.5 0.0 all-to-all-done.1
  109.5 0.0 copy-start
  109.5 0.6 copy-done.1
  110.1 0.0 copy-done.2
  110.2 0.7 copy-done
  110.9 51.9 %second_block.1 = bf16[1024,256]{1,0:T(8,128)(2,1)} custom-call(s32[1]{0:T(128)} %bitcast.me_ref, s32[128]{0:T(128)} %get-tuple-element.13.plan, s32[8,128]{1,0:T(8,128)} %get-tuple-element.14.scenes, f32[2,2,256]{2,1,0:T(2,128)} %gains.3, bf16[4096,256]{1,0:T(8,128)(2,1)} %bitcast.4, bf16[96,256]{1,0:T(8,128)(2,1)} %copy-done.1, bf16[96,256]{1,0:T(8,128)(2,1)} %copy-done.2, ...), custom_call_target="tpu_custom_call" | custom-call | tf_op jit(solution)/shard_map/second_block/pallas_call | solution.py:482
Async XLA Ops:
  74.0 4.8 %copy-start.4 = (bf16[96,256]{1,0:T(8,128)(2,1)S(1)}, bf16[96,256]{1,0:T(8,128)(2,1)}, u32[]{:S(2)}) copy-start(bf16[96,256]{1,0:T(8,128)(2,1)} %get-tuple-element.16) | copy-start | bytes 147460
  74.0 4.9 %copy-start.3 = (bf16[96,256]{1,0:T(8,128)(2,1)S(1)}, bf16[96,256]{1,0:T(8,128)(2,1)}, u32[]{:S(2)}) copy-start(bf16[96,256]{1,0:T(8,128)(2,1)} %get-tuple-element.17) | copy-start | bytes 147460
  74.0 35.5 %all-to-all-start.1 = ((bf16[128,32,256]{2,1,0:T(8,128)(2,1)}), bf16[128,32,256]{2,1,0:T(8,128)(2,1)S(1)}, u32[]{:S(2)}, u32[]{:S(2)}) async-start(bf16[128,32,256]{2,1,0:T(8,128)(2,1)} %bitcast.5), calls=%async_computation.1 | async-start | bytes 4194304 | tf_op jit(solution)/shard_map/all_to_all | solution.py:465
  78.8 30.7 %collective-permute-start = (bf16[96,256]{1,0:T(8,128)(2,1)S(1)}, bf16[96,256]{1,0:T(8,128)(2,1)S(1)}, u32[]{:S(2)}, u32[]{:S(2)}) collective-permute-start(bf16[96,256]{1,0:T(8,128)(2,1)S(1)} %copy-done.4), channel_id=1, source_target_pairs={{0,1},{1,2},{2,3},{3,4},{4,5},{5,6},{6,7},{7,8},{8,9},{9,10},{10,1... | collective-permute-start | bytes 147464 | tf_op jit(solution)/shard_map/ppermute | solution.py:467
  78.9 30.6 %collective-permute-start.1 = (bf16[96,256]{1,0:T(8,128)(2,1)S(1)}, bf16[96,256]{1,0:T(8,128)(2,1)S(1)}, u32[]{:S(2)}, u32[]{:S(2)}) collective-permute-start(bf16[96,256]{1,0:T(8,128)(2,1)S(1)} %copy-done.3), channel_id=1, source_target_pairs={{0,127},{1,0},{2,1},{3,2},{4,3},{5,4},{6,5},{7,6},{8,7},{9,8},{10,... | collective-permute-start | bytes 147464 | tf_op jit(solution)/shard_map/ppermute | solution.py:468
  109.5 0.6 copy-start.1
  109.5 0.6 copy-start.2
  109.5 1.4 copy-start

commit v2 on v1

--- a/solution.py
+++ b/solution.py
@@ -233,58 +233,48 @@
         slot = is_up * slots[0] + is_down * slots[1]
         row = scenes[tile // 4 : tile // 4 + 1, (tile % 4) * TILE : (tile % 4 + 1) * TILE]
         row = jnp.concatenate([row] * 4, axis=1) + 128 * (tile + 1)
-        notes[owner] = notes[owner] + jnp.where(group == slot, row, 0)
+        line = owner ^ me
+        notes[line] = notes[line] + jnp.where(group == slot, row, 0)
         slots = (slots[0] + is_up, slots[1] + is_down)
 
 
-def plan_kernel(me_ref, rank_ref, scene_ref, notes_ref, notes, scenes, plan, scene_out):
+def plan_kernel(me_ref, rank_ref, scene_ref, notes_ref, notes, scenes, plan, scene_out, found):
     me = me_ref[0]
+    stay = 4 * 128
+
+    def received(source, count):
+        for slot in range(MOST_TILES):
+            found[count] = 4 * source + slot
+            count = count + jnp.minimum(notes_ref[source ^ me, 0, slot * TILE], 1)
+        return count
+
+    def kept(tile, count):
+        found[count] = stay + tile
+        return count + (rank_ref[tile * TILE] // ROWS == me).astype(jnp.int32)
+
+    count = lax.fori_loop(0, me, received, jnp.int32(0))
+    count = lax.fori_loop(0, TILES, kept, count)
+    lax.fori_loop(me + 1, 128, received, count)
     group = lax.broadcasted_iota(jnp.int32, (1, 128), 1) // TILE
-    scene_out[...] = jnp.zeros_like(scene_out)
-
-    def clear(index, carry):
-        plan[index] = 0
-        return carry
-
-    lax.fori_loop(0, 4 * TILES, clear, 0)
-
-    def add(index, place, source, first, last, row, slot):
-        plan[index] = place
+    for index in range(TILES):
+        code = found[index]
+        keeps = code >= stay
+        tile = jnp.where(keeps, code - stay, 0)
+        source = jnp.where(keeps, me, jnp.minimum(code // 4, 127))
+        slot = jnp.where(keeps, lax.rem(tile, 4), lax.rem(code, 4))
+        start = notes_ref[source ^ me, 0, slot * TILE]
+        end = notes_ref[source ^ me, 0, slot * TILE + TILE - 1]
+        plan[index] = jnp.where(keeps, tile, start // 128 - 1)
         plan[TILES + index] = source
-        plan[2 * TILES + index] = first
-        plan[3 * TILES + index] = last
-        lane = lax.rem(index, 4)
-        moved = pltpu.roll(row, TILE * lax.rem(lane - slot + 4, 4), 1)
-        line = pl.ds(index // 4, 1)
-        scene_out[line, :] = jnp.where(group == lane, moved, scene_out[line, :])
-
-    def one_source(source, count):
-        def received(slot, count):
-            note = notes_ref[source, 0, slot * TILE]
-
-            @pl.when(note > 0)
-            def _():
-                last = notes_ref[source, 0, slot * TILE + TILE - 1]
-                add(count, note // 128 - 1, source, note % 128, last % 128, notes[source] % 128, slot)
-
-            return count + (note > 0).astype(jnp.int32)
-
-        def stays(tile, count):
-            keep = rank_ref[tile * TILE] // ROWS == me
-
-            @pl.when(keep)
-            def _():
-                first, last = scene_ref[tile * TILE], scene_ref[tile * TILE + TILE - 1]
-                row = scenes[pl.ds(tile // 4, 1), :]
-                add(count, tile, me, first, last, row, lax.rem(tile, 4))
-
-            return count + keep.astype(jnp.int32)
-
-        mine = source == me
-        count = lax.fori_loop(0, jnp.where(mine, 0, MOST_TILES), received, count)
-        return lax.fori_loop(0, jnp.where(mine, TILES, 0), stays, count)
-
-    lax.fori_loop(0, 128, one_source, jnp.int32(0))
+        plan[2 * TILES + index] = jnp.where(keeps, scene_ref[tile * TILE], lax.rem(start, 128))
+        plan[3 * TILES + index] = jnp.where(keeps, scene_ref[tile * TILE + TILE - 1], lax.rem(end, 128))
+        row = jnp.where(keeps, scenes[pl.ds(tile // 4, 1), :], notes[source ^ me] & 127)
+        moved = pltpu.roll(row, TILE * lax.rem(index % 4 - slot + 4, 4), 1)
+        line = slice(index // 4, index // 4 + 1)
+        if index % 4 == 0:
+            scene_out[line, :] = moved
+        else:
+            scene_out[line, :] = jnp.where(group == index % 4, moved, scene_out[line, :])
 
 
 def first_kernel(
@@ -435,6 +425,23 @@
 SMEM = pl.BlockSpec(memory_space=pltpu.SMEM)
 VMEM = pl.BlockSpec(memory_space=pltpu.VMEM)
 HBM = pl.BlockSpec(memory_space=pl.ANY)
+
+
+def exchange(rows, devices):
+    bits = devices.bit_length() - 1
+    lanes = rows.shape[1:]
+    shift = bits
+    while shift:
+        step = 2 if shift > 1 else 1
+        shift -= step
+        count = 1 << step
+        parts = rows.reshape((count, devices // count) + lanes)
+        pieces = [parts[0]] + [
+            lax.ppermute(parts[v], "seq", [(i, i ^ (v << shift)) for i in range(devices)])
+            for v in range(1, count)
+        ]
+        rows = jnp.stack(pieces, axis=1).reshape((devices,) + lanes)
+    return rows
 
 
 def shards(point_feats, scene_id, hilbert_rank, norm_gains, w_qkv, w_proj, w_up, w_down):
@@ -466,7 +473,7 @@
     ring = range(devices)
     from_below = lax.ppermute(up, "seq", [(i, (i + 1) % devices) for i in ring])
     from_above = lax.ppermute(down, "seq", [(i, (i - 1) % devices) for i in ring])
-    notes = lax.all_to_all(notes, "seq", split_axis=0, concat_axis=0, tiled=True)
+    notes = exchange(notes, devices)
     plan, scenes = pl.pallas_call(
         plan_kernel,
         in_specs=[SMEM, SMEM, SMEM, SMEM, VMEM, VMEM],
@@ -475,7 +482,9 @@
             jax.ShapeDtypeStruct((4 * TILES,), jnp.int32),
             jax.ShapeDtypeStruct((ROWS // 128, 128), jnp.int32),
         ],
+        scratch_shapes=[pltpu.SMEM((2 * TILES,), jnp.int32)],
         compiler_params=params,
+        cost_estimate=pl.CostEstimate(flops=1, bytes_accessed=1, transcendentals=0),
         name="plan",
     )(me_array, hilbert_rank, scene_id, notes, notes, scenes)
 

time: 163 us -> 175 us (1.074)
  starting transfers between devices: 12.2 us -> 46.4 us
  blocking collectives: 20.9 us -> 0 us
  Pallas kernels: 118 us -> 110 us
  waiting for transfers between devices: 10.5 us -> 15.5 us
    ppermute x0 -> x10, starting transfers between devices: none -> 28.1 us  [exchange(): lax.ppermute(parts[v], 'seq', [(i, i ^ v << shift) for i in range(devices)])]
    all_to_all x1 -> x0, blocking collectives: 20.9 us -> none  [shards(): lax.all_to_all(notes, 'seq', split_axis=0, concat_axis=0, tiled=True)]
    ppermute x0 -> x10, waiting for transfers between devices: none -> 15.5 us  [exchange(): lax.ppermute(parts[v], 'seq', [(i, i ^ v << shift) for i in range(devices)])]
    ppermute x1, waiting for transfers between devices: 10.5 us -> 0.01 us  [shards(): from_below = lax.ppermute(up, 'seq', [(i, (i + 1) % devices) for i in ring])]
    pallas_call x1, Pallas kernels: 12.8 us -> 4.98 us  [shards(): pl.pallas_call(plan_kernel, in_specs=[SMEM, SMEM, SMEM, SMEM, VMEM, VMEM]...]
    all_to_all x1, starting transfers between devices: 4.78 us -> 11.1 us  [shards(): lax.all_to_all(send, 'seq', split_axis=0, concat_axis=0, tiled=True)]
  transfers between devices with their start and end apart: 3 -> 13, of which waited for: 1 -> 7; matrix products, arithmetic and copies ran while one was open for 0% -> 0% of each run, Pallas kernels for 8% -> 3%
where the time goes in v2:
time: 175 us
  Pallas kernels  110 us (63%)
  starting transfers between devices  46.4 us (27%)
  waiting for transfers between devices  15.5 us (9%)
  local copies, waits for them, and re-layouts  2.13 us (1%)
    pallas_call x1, Pallas kernels, shards(): pl.pallas_call(first_kernel, in_specs=[SMEM, SMEM, VMEM, VMEM, VMEM, HBM,...  53.1 us
    pallas_call x1, Pallas kernels, shards(): pl.pallas_call(second_kernel, in_specs=[SMEM, SMEM, VMEM, VMEM] + [HBM] *...  52 us
    ppermute x10, starting transfers between devices, exchange(): lax.ppermute(parts[v], 'seq', [(i, i ^ v << shift) for i in range(devices)])  28.1 us
    ppermute x10, waiting for transfers between devices, exchange(): lax.ppermute(parts[v], 'seq', [(i, i ^ v << shift) for i in range(devices)])  15.5 us
    all_to_all x1, starting transfers between devices, shards(): lax.all_to_all(send, 'seq', split_axis=0, concat_axis=0, tiled=True)  11.1 us
    ppermute x1, starting transfers between devices, shards(): lax.ppermute(down, 'seq', [(i, (i - 1) % devices) for i in ring])  6.75 us
    pallas_call x1, Pallas kernels, shards(): pl.pallas_call(plan_kernel, in_specs=[SMEM, SMEM, SMEM, SMEM, VMEM, VMEM]...  4.98 us
  transfers between devices with their start and end apart: 13, of which 7 were waited for; matrix products, arithmetic and copies ran while one was open for 0% of the time, Pallas kernels for 3%

profile of v2, /device:TPU:0, one launch (start us, length us, event | category | flops | bytes accessed | tf_op | source)
XLA Modules:
  0.0 174.7 jit_solution(9147183356253657803)
XLA Ops:
  0.0 53.1 %first_block.1 = (bf16[4096,256]{1,0:T(8,128)(2,1)}, s32[128,1,128]{2,1,0:T(1,128)}, bf16[96,256]{1,0:T(8,128)(2,1)}, bf16[96,256]{1,0:T(8,128)(2,1)}, bf16[1024,256]{1,0:T(8,128)(2,1)}) custom-call(s32[1]{0:T(128)} %bitcast.me_ref, s32[1024]{0:T(1024)} %rank_ref.3, bf16[1024,256]{1,0:T(8,128)(2,1)} %x.1, s32[8,128]{1,0:T(8,128)} %bitcast.36, ...), custom_call_target="tpu_custom_call" | custom-call | tf_op jit(solution)/shard_map/first_block/pallas_call | solution.py:456
  53.1 0.0 copy-start.1
  53.1 0.0 copy-start.5
  53.2 0.0 copy-start.4
  53.2 11.1 %all-to-all-start = ((bf16[128,32,256]{2,1,0:T(8,128)(2,1)}), bf16[128,32,256]{2,1,0:T(8,128)(2,1)S(1)}, u32[]{:S(2)}, u32[]{:S(2)}) async-start(bf16[128,32,256]{2,1,0:T(8,128)(2,1)} %bitcast.29), calls=%async_computation | async-start | bytes 4194304 | tf_op jit(solution)/shard_map/all_to_all | solution.py:472
  64.3 0.0 copy-done.1
  64.3 1.2 collective-permute-start
  65.5 3.2 %collective-permute-start.1 = (s32[32,1,128]{2,0,1:T(8,128)S(1)}, s32[32,1,128]{2,0,1:T(8,128)S(1)}, u32[]{:S(2)}, u32[]{:S(2)}) collective-permute-start(s32[32,1,128]{2,0,1:T(8,128)S(1)} %get-tuple-element.30), channel_id=1, source_target_pairs={{0,64},{1,65},{2,66},{3,67},{4,68},{5,69},{6,70},{7,71},{8,72},{9,... | collective-permute-start | bytes 49160 | tf_op jit(solution)/shard_map/ppermute | solution.py:440
  68.7 0.4 collective-permute-start.2
  69.1 0.4 collective-permute-done
  69.5 3.9 %collective-permute-done.1 = s32[32,1,128]{2,0,1:T(8,128)S(1)} collective-permute-done((s32[32,1,128]{2,0,1:T(8,128)S(1)}, s32[32,1,128]{2,0,1:T(8,128)S(1)}, u32[]{:S(2)}, u32[]{:S(2)}) %collective-permute-start.1) | collective-permute-done | bytes 16416 | tf_op jit(solution)/shard_map/ppermute | solution.py:440
  73.4 2.6 %collective-permute-done.2 = s32[32,1,128]{2,1,0:T(1,128)S(1)} collective-permute-done((s32[32,1,128]{2,1,0:T(1,128)S(1)}, s32[32,1,128]{2,1,0:T(1,128)S(1)}, u32[]{:S(2)}, u32[]{:S(2)}) %collective-permute-start.2) | collective-permute-done | bytes 16416 | tf_op jit(solution)/shard_map/ppermute | solution.py:440
  76.1 10.4 %collective-permute-start.4 = (s32[32,1,128]{2,0,1:T(8,128)S(1)}, s32[32,1,128]{2,0,1:T(8,128)S(1)}, u32[]{:S(2)}, u32[]{:S(2)}) collective-permute-start(s32[32,1,128]{2,0,1:T(8,128)S(1)} %bitcast.40), channel_id=1, source_target_pairs={{0,16},{1,17},{2,18},{3,19},{4,20},{5,21},{6,22},{7,23},{8,24},{9,... | collective-permute-start | bytes 49160 | tf_op jit(solution)/shard_map/ppermute | solution.py:440
  86.4 4.4 %collective-permute-start.5 = (s32[32,1,128]{2,0,1:T(8,128)S(1)}, s32[32,1,128]{2,0,1:T(8,128)S(1)}, u32[]{:S(2)}, u32[]{:S(2)}) collective-permute-start(s32[32,1,128]{2,0,1:T(8,128)S(1)} %bitcast.42), channel_id=1, source_target_pairs={{0,24},{1,25},{2,26},{3,27},{4,28},{5,29},{6,30},{7,31},{8,16},{9,... | collective-permute-start | bytes 49160 | tf_op jit(solution)/shard_map/ppermute | solution.py:440
  90.8 0.0 collective-permute-start.3
  90.9 0.0 collective-permute-done.4
  90.9 1.7 collective-permute-done.5
  92.5 2.0 %collective-permute-done.3 = s32[32,1,128]{2,0,1:T(8,128)S(1)} collective-permute-done((s32[32,1,128]{2,0,1:T(8,128)S(1)}, s32[32,1,128]{2,0,1:T(8,128)S(1)}, u32[]{:S(2)}, u32[]{:S(2)}) %collective-permute-start.3) | collective-permute-done | bytes 16416 | tf_op jit(solution)/shard_map/ppermute | solution.py:440
  94.6 1.0 collective-permute-start.6
  95.6 7.4 %collective-permute-start.7 = (s32[32,1,128]{2,0,1:T(8,128)S(1)}, s32[32,1,128]{2,0,1:T(8,128)S(1)}, u32[]{:S(2)}, u32[]{:S(2)}) collective-permute-start(s32[32,1,128]{2,0,1:T(8,128)S(1)} %bitcast.43), channel_id=1, source_target_pairs={{0,4},{1,5},{2,6},{3,7},{4,0},{5,1},{6,2},{7,3},{8,12},{9,13},{10,... | collective-permute-start | bytes 49160 | tf_op jit(solution)/shard_map/ppermute | solution.py:440
  103.0 0.0 collective-permute-start.8
  103.0 0.0 collective-permute-done.6
  103.1 1.8 %collective-permute-done.7 = s32[32,1,128]{2,0,1:T(8,128)S(1)} collective-permute-done((s32[32,1,128]{2,0,1:T(8,128)S(1)}, s32[32,1,128]{2,0,1:T(8,128)S(1)}, u32[]{:S(2)}, u32[]{:S(2)}) %collective-permute-start.7) | collective-permute-done | bytes 16416 | tf_op jit(solution)/shard_map/ppermute | solution.py:440
  104.9 3.1 %collective-permute-done.8 = s32[32,1,128]{2,0,1:T(8,128)S(1)} collective-permute-done((s32[32,1,128]{2,0,1:T(8,128)S(1)}, s32[32,1,128]{2,0,1:T(8,128)S(1)}, u32[]{:S(2)}, u32[]{:S(2)}) %collective-permute-start.8) | collective-permute-done | bytes 16416 | tf_op jit(solution)/shard_map/ppermute | solution.py:440
  108.0 0.1 collective-permute-start.9
  108.1 0.0 copy-done.5
  108.1 0.5 collective-permute-start.10
  108.6 0.0 copy-done.4
  108.6 6.8 %collective-permute-start.11 = (bf16[96,256]{1,0:T(8,128)(2,1)S(1)}, bf16[96,256]{1,0:T(8,128)(2,1)S(1)}, u32[]{:S(2)}, u32[]{:S(2)}) collective-permute-start(bf16[96,256]{1,0:T(8,128)(2,1)S(1)} %copy-done.4), channel_id=1, source_target_pairs={{0,127},{1,0},{2,1},{3,2},{4,3},{5,4},{6,5},{7,6},{8,7},{9,8},{10,... | collective-permute-start | bytes 147464 | tf_op jit(solution)/shard_map/ppermute | solution.py:475
  115.4 0.0 collective-permute-done.9
  115.4 0.7 copy.43
  116.1 5.0 %plan.1 = (s32[128]{0:T(128)}, s32[8,128]{1,0:T(8,128)}) custom-call(s32[1]{0:T(128)} %bitcast.me_ref, s32[1024]{0:T(1024)} %rank_ref.3, s32[1024]{0:T(1024)} %scene_ref.1, s32[128,1,128]{2,1,0:T(1,128)} %bitcast.30, s32[128,1,128]{2,1,0:T(1,128)} %bitcast.31, s32[8,128]{1,0:T(8,128)} %bitcast.37), custom_call_target="tpu_custom_call" | custom-call | flops 1 | bytes 1 | tf_op jit(solution)/shard_map/plan/pallas_call | solution.py:477
  121.1 0.0 collective-permute-done.10.from_below
  121.1 0.0 copy-start.2
  121.1 0.0 collective-permute-done.11.from_above
  121.1 0.0 copy-start.3
  121.1 0.0 all-to-all-done
  121.1 0.0 copy-start
  121.1 0.6 copy-done.2
  121.7 0.0 copy-done.3
  121.7 0.7 copy-done
  122.5 52.0 %second_block.1 = bf16[1024,256]{1,0:T(8,128)(2,1)} custom-call(s32[1]{0:T(128)} %bitcast.me_ref, s32[128]{0:T(128)} %get-tuple-element.13.plan, s32[8,128]{1,0:T(8,128)} %get-tuple-element.14.scenes, f32[2,2,256]{2,1,0:T(2,128)} %gains.3, bf16[4096,256]{1,0:T(8,128)(2,1)} %bitcast.28, bf16[96,256]{1,0:T(8,128)(2,1)} %copy-done.2, ...), custom_call_target="tpu_custom_call" | custom-call | tf_op jit(solution)/shard_map/second_block/pallas_call | solution.py:491
  (19 shorter events, 0.1 us)
Async XLA Ops:
  53.1 11.2 %copy-start.1 = (s32[128,1,128]{2,1,0:T(1,128)S(1)}, s32[128,1,128]{2,1,0:T(1,128)}, u32[]{:S(2)}) copy-start(s32[128,1,128]{2,1,0:T(1,128)} %get-tuple-element.12) | copy-start | bytes 196612
  53.1 55.0 %copy-start.5 = (bf16[96,256]{1,0:T(8,128)(2,1)S(1)}, bf16[96,256]{1,0:T(8,128)(2,1)}, u32[]{:S(2)}) copy-start(bf16[96,256]{1,0:T(8,128)(2,1)} %get-tuple-element.16) | copy-start | bytes 147460
  53.2 55.5 %copy-start.4 = (bf16[96,256]{1,0:T(8,128)(2,1)S(1)}, bf16[96,256]{1,0:T(8,128)(2,1)}, u32[]{:S(2)}) copy-start(bf16[96,256]{1,0:T(8,128)(2,1)} %get-tuple-element.17) | copy-start | bytes 147460
  53.2 68.0 %all-to-all-start = ((bf16[128,32,256]{2,1,0:T(8,128)(2,1)}), bf16[128,32,256]{2,1,0:T(8,128)(2,1)S(1)}, u32[]{:S(2)}, u32[]{:S(2)}) async-start(bf16[128,32,256]{2,1,0:T(8,128)(2,1)} %bitcast.29), calls=%async_computation | async-start | bytes 4194304 | tf_op jit(solution)/shard_map/all_to_all | solution.py:472
  64.3 5.2 %collective-permute-start = (s32[32,1,128]{2,0,1:T(8,128)S(1)}, s32[32,1,128]{2,0,1:T(8,128)S(1)}, u32[]{:S(2)}, u32[]{:S(2)}) collective-permute-start(s32[32,1,128]{2,0,1:T(8,128)S(1)} %get-tuple-element.31), channel_id=1, source_target_pairs={{0,32},{1,33},{2,34},{3,35},{4,36},{5,37},{6,38},{7,39},{8,40},{9,... | collective-permute-start | bytes 49160 | tf_op jit(solution)/shard_map/ppermute | solution.py:440
  65.5 7.9 %collective-permute-start.1 = (s32[32,1,128]{2,0,1:T(8,128)S(1)}, s32[32,1,128]{2,0,1:T(8,128)S(1)}, u32[]{:S(2)}, u32[]{:S(2)}) collective-permute-start(s32[32,1,128]{2,0,1:T(8,128)S(1)} %get-tuple-element.30), channel_id=1, source_target_pairs={{0,64},{1,65},{2,66},{3,67},{4,68},{5,69},{6,70},{7,71},{8,72},{9,... | collective-permute-start | bytes 49160 | tf_op jit(solution)/shard_map/ppermute | solution.py:440
  68.7 7.3 %collective-permute-start.2 = (s32[32,1,128]{2,1,0:T(1,128)S(1)}, s32[32,1,128]{2,1,0:T(1,128)S(1)}, u32[]{:S(2)}, u32[]{:S(2)}) collective-permute-start(s32[32,1,128]{2,1,0:T(1,128)S(1)} %slice.59), channel_id=1, source_target_pairs={{0,96},{1,97},{2,98},{3,99},{4,100},{5,101},{6,102},{7,103},{8,104... | collective-permute-start | bytes 49160 | tf_op jit(solution)/shard_map/ppermute | solution.py:440
  76.1 14.8 %collective-permute-start.4 = (s32[32,1,128]{2,0,1:T(8,128)S(1)}, s32[32,1,128]{2,0,1:T(8,128)S(1)}, u32[]{:S(2)}, u32[]{:S(2)}) collective-permute-start(s32[32,1,128]{2,0,1:T(8,128)S(1)} %bitcast.40), channel_id=1, source_target_pairs={{0,16},{1,17},{2,18},{3,19},{4,20},{5,21},{6,22},{7,23},{8,24},{9,... | collective-permute-start | bytes 49160 | tf_op jit(solution)/shard_map/ppermute | solution.py:440
  86.4 6.1 %collective-permute-start.5 = (s32[32,1,128]{2,0,1:T(8,128)S(1)}, s32[32,1,128]{2,0,1:T(8,128)S(1)}, u32[]{:S(2)}, u32[]{:S(2)}) collective-permute-start(s32[32,1,128]{2,0,1:T(8,128)S(1)} %bitcast.42), channel_id=1, source_target_pairs={{0,24},{1,25},{2,26},{3,27},{4,28},{5,29},{6,30},{7,31},{8,16},{9,... | collective-permute-start | bytes 49160 | tf_op jit(solution)/shard_map/ppermute | solution.py:440
  90.8 3.7 %collective-permute-start.3 = (s32[32,1,128]{2,0,1:T(8,128)S(1)}, s32[32,1,128]{2,0,1:T(8,128)S(1)}, u32[]{:S(2)}, u32[]{:S(2)}) collective-permute-start(s32[32,1,128]{2,0,1:T(8,128)S(1)} %bitcast.44), channel_id=1, source_target_pairs={{0,8},{1,9},{2,10},{3,11},{4,12},{5,13},{6,14},{7,15},{8,0},{9,1},... | collective-permute-start | bytes 49160 | tf_op jit(solution)/shard_map/ppermute | solution.py:440
  94.6 8.4 %collective-permute-start.6 = (s32[32,1,128]{2,0,1:T(8,128)S(1)}, s32[32,1,128]{2,0,1:T(8,128)S(1)}, u32[]{:S(2)}, u32[]{:S(2)}) collective-permute-start(s32[32,1,128]{2,0,1:T(8,128)S(1)} %bitcast.41), channel_id=1, source_target_pairs={{0,2},{1,3},{2,0},{3,1},{4,6},{5,7},{6,4},{7,5},{8,10},{9,11},{10,... | collective-permute-start | bytes 49160 | tf_op jit(solution)/shard_map/ppermute | solution.py:440
  95.6 9.3 %collective-permute-start.7 = (s32[32,1,128]{2,0,1:T(8,128)S(1)}, s32[32,1,128]{2,0,1:T(8,128)S(1)}, u32[]{:S(2)}, u32[]{:S(2)}) collective-permute-start(s32[32,1,128]{2,0,1:T(8,128)S(1)} %bitcast.43), channel_id=1, source_target_pairs={{0,4},{1,5},{2,6},{3,7},{4,0},{5,1},{6,2},{7,3},{8,12},{9,13},{10,... | collective-permute-start | bytes 49160 | tf_op jit(solution)/shard_map/ppermute | solution.py:440
  103.0 5.0 %collective-permute-start.8 = (s32[32,1,128]{2,0,1:T(8,128)S(1)}, s32[32,1,128]{2,0,1:T(8,128)S(1)}, u32[]{:S(2)}, u32[]{:S(2)}) collective-permute-start(s32[32,1,128]{2,0,1:T(8,128)S(1)} %bitcast.45), channel_id=1, source_target_pairs={{0,6},{1,7},{2,4},{3,5},{4,2},{5,3},{6,0},{7,1},{8,14},{9,15},{10,... | collective-permute-start | bytes 49160 | tf_op jit(solution)/shard_map/ppermute | solution.py:440
  108.0 7.4 %collective-permute-start.9 = (s32[64,1,128]{2,0,1:T(8,128)S(1)}, s32[64,1,128]{2,0,1:T(8,128)S(1)}, u32[]{:S(2)}, u32[]{:S(2)}) collective-permute-start(s32[64,1,128]{2,0,1:T(8,128)S(1)} %bitcast.38), channel_id=1, source_target_pairs={{0,1},{1,0},{2,3},{3,2},{4,5},{5,4},{6,7},{7,6},{8,9},{9,8},{10,11... | collective-permute-start | bytes 98312 | tf_op jit(solution)/shard_map/ppermute | solution.py:440
  108.1 13.0 %collective-permute-start.10 = (bf16[96,256]{1,0:T(8,128)(2,1)S(1)}, bf16[96,256]{1,0:T(8,128)(2,1)S(1)}, u32[]{:S(2)}, u32[]{:S(2)}) collective-permute-start(bf16[96,256]{1,0:T(8,128)(2,1)S(1)} %copy-done.5), channel_id=1, source_target_pairs={{0,1},{1,2},{2,3},{3,4},{4,5},{5,6},{6,7},{7,8},{8,9},{9,10},{10,1... | collective-permute-start | bytes 147464 | tf_op jit(solution)/shard_map/ppermute | solution.py:474
  108.6 12.5 %collective-permute-start.11 = (bf16[96,256]{1,0:T(8,128)(2,1)S(1)}, bf16[96,256]{1,0:T(8,128)(2,1)S(1)}, u32[]{:S(2)}, u32[]{:S(2)}) collective-permute-start(bf16[96,256]{1,0:T(8,128)(2,1)S(1)} %copy-done.4), channel_id=1, source_target_pairs={{0,127},{1,0},{2,1},{3,2},{4,3},{5,4},{6,5},{7,6},{8,7},{9,8},{10,... | collective-permute-start | bytes 147464 | tf_op jit(solution)/shard_map/ppermute | solution.py:475
  121.1 0.6 copy-start.2
  121.1 0.6 copy-start.3
  121.1 1.3 copy-start

commit v3 on v2

--- a/solution.py
+++ b/solution.py
@@ -15,6 +15,8 @@
 TILES = 32
 TILE = 32
 MOST_TILES = 3
+CHIPS = 64
+STRIDE = 48
 EPSILON = 1e-05
 QUERY_BLOCK = 256
 WINDOW = 512
@@ -222,54 +224,106 @@
     return lax.rem(me + 1, 128), lax.rem(me + 127, 128)
 
 
-def write_notes(me, rank_ref, scenes, notes):
-    notes[...] = jnp.zeros_like(notes)
+def note_kernel(me_ref, rank_ref, scenes, same, other, up, down, lines):
+    me = me_ref[0]
     above, below = neighbours(me)
+    lines[...] = jnp.zeros_like(lines)
     group = lax.broadcasted_iota(jnp.int32, (1, 128), 1) // TILE
-    slots = (jnp.int32(0), jnp.int32(0))
+    ups = downs = others = jnp.int32(0)
     for tile in range(TILES):
         owner = rank_ref[tile * TILE] // ROWS
-        is_up, is_down = (owner == above).astype(jnp.int32), (owner == below).astype(jnp.int32)
-        slot = is_up * slots[0] + is_down * slots[1]
+        is_up, is_down = owner == above, owner == below
+        crosses = ((owner ^ me) & 1 == 1) & jnp.logical_not(is_up | is_down)
+        slot = jnp.where(is_up, ups, jnp.where(is_down, downs, 0))
+        line = owner // 2 + jnp.where(crosses, CHIPS, 0)
+        line = jnp.where(is_up, 2 * CHIPS, jnp.where(is_down, 2 * CHIPS + 1, line))
+        line = jnp.where(owner == me, 2 * CHIPS + 2, line)
         row = scenes[tile // 4 : tile // 4 + 1, (tile % 4) * TILE : (tile % 4 + 1) * TILE]
         row = jnp.concatenate([row] * 4, axis=1) + 128 * (tile + 1)
-        line = owner ^ me
-        notes[line] = notes[line] + jnp.where(group == slot, row, 0)
-        slots = (slots[0] + is_up, slots[1] + is_down)
-
-
-def plan_kernel(me_ref, rank_ref, scene_ref, notes_ref, notes, scenes, plan, scene_out, found):
+        lines[line] = jnp.where(group == slot, row, lines[line])
+        ups, downs = ups + is_up.astype(jnp.int32), downs + is_down.astype(jnp.int32)
+        others = others + crosses.astype(jnp.int32)
+    same[...] = jnp.where(group[None] == 3, others, lines[0:CHIPS])
+    other[...] = lines[CHIPS : 2 * CHIPS]
+    up[...] = lines[2 * CHIPS : 2 * CHIPS + 1]
+    down[...] = lines[2 * CHIPS + 1 : 2 * CHIPS + 2]
+
+
+def plan_kernel(
+    me_ref, rank_ref, scene_ref, same_ref, other_ref, below_ref, above_ref, same, other, from_below, from_above, scenes,
+    plan, scene_out, found, lines,
+):
     me = me_ref[0]
-    stay = 4 * 128
-
-    def received(source, count):
+    core = lax.rem(me, 2)
+    above, below = neighbours(me)
+    lines[0:CHIPS] = same[...]
+    lines[CHIPS : 2 * CHIPS] = other[...]
+    lines[2 * CHIPS : 2 * CHIPS + 1] = from_below[...]
+    lines[2 * CHIPS + 1 : 2 * CHIPS + 2] = from_above[...]
+    for line in range(ROWS // 128):
+        lines[2 * CHIPS + 2 + line] = scenes[line : line + 1]
+    one = jnp.int32(1)
+
+    def add(count, line, slot, source, note, last, present):
+        found[count] = 4 * line + slot
+        plan[count] = jnp.int32(note // 128 - 1)
+        plan[STRIDE + count] = source
+        plan[2 * STRIDE + count] = note & 127
+        plan[3 * STRIDE + count] = last & 127
+        return count + present
+
+    def beside(ref, line, source, count):
         for slot in range(MOST_TILES):
-            found[count] = 4 * source + slot
-            count = count + jnp.minimum(notes_ref[source ^ me, 0, slot * TILE], 1)
+            note = ref[0, 0, slot * TILE]
+            last = ref[0, 0, slot * TILE + TILE - 1]
+            count = add(count, line, slot, source, note, last, jnp.minimum(note, 1))
         return count
 
-    def kept(tile, count):
-        found[count] = stay + tile
-        return count + (rank_ref[tile * TILE] // ROWS == me).astype(jnp.int32)
-
-    count = lax.fori_loop(0, me, received, jnp.int32(0))
-    count = lax.fori_loop(0, TILES, kept, count)
-    lax.fori_loop(me + 1, 128, received, count)
+    def mine(count):
+        def kept(tile, count):
+            keeps = (rank_ref[tile * TILE] // ROWS == me).astype(jnp.int32)
+            note = scene_ref[tile * TILE] + 128 * (tile + 1)
+            last = scene_ref[tile * TILE + TILE - 1]
+            return add(count, 2 * CHIPS + 2 + tile // 4, lax.rem(tile, 4), me, note, last, keeps)
+
+        return lax.fori_loop(0, TILES, kept, count)
+
+    def chip(index, count):
+        for side in range(2):
+            source = 2 * index + side
+            own = core == side
+
+            def far(count, source=source, own=own):
+                note = jnp.where(own, same_ref[index, 0, 0], other_ref[index, 0, 0])
+                last = jnp.where(own, same_ref[index, 0, TILE - 1], other_ref[index, 0, TILE - 1])
+                line = index + jnp.where(own, 0, CHIPS)
+                return add(count, line, 0, source, note, last, jnp.minimum(note, one))
+
+            kind = jnp.where(source == me, 1, jnp.where(source == below, 2, jnp.where(source == above, 3, 0)))
+            count = lax.cond(
+                kind == 0,
+                far,
+                lambda count: lax.cond(
+                    kind == 1,
+                    mine,
+                    lambda count: lax.cond(
+                        kind == 2,
+                        lambda count: beside(below_ref, 2 * CHIPS, below, count),
+                        lambda count: beside(above_ref, 2 * CHIPS + 1, above, count),
+                        count,
+                    ),
+                    count,
+                ),
+                count,
+            )
+        return count
+
+    lax.fori_loop(0, CHIPS, chip, jnp.int32(0))
     group = lax.broadcasted_iota(jnp.int32, (1, 128), 1) // TILE
     for index in range(TILES):
         code = found[index]
-        keeps = code >= stay
-        tile = jnp.where(keeps, code - stay, 0)
-        source = jnp.where(keeps, me, jnp.minimum(code // 4, 127))
-        slot = jnp.where(keeps, lax.rem(tile, 4), lax.rem(code, 4))
-        start = notes_ref[source ^ me, 0, slot * TILE]
-        end = notes_ref[source ^ me, 0, slot * TILE + TILE - 1]
-        plan[index] = jnp.where(keeps, tile, start // 128 - 1)
-        plan[TILES + index] = source
-        plan[2 * TILES + index] = jnp.where(keeps, scene_ref[tile * TILE], lax.rem(start, 128))
-        plan[3 * TILES + index] = jnp.where(keeps, scene_ref[tile * TILE + TILE - 1], lax.rem(end, 128))
-        row = jnp.where(keeps, scenes[pl.ds(tile // 4, 1), :], notes[source ^ me] & 127)
-        moved = pltpu.roll(row, TILE * lax.rem(index % 4 - slot + 4, 4), 1)
+        row = lines[code // 4] & 127
+        moved = pltpu.roll(row, TILE * lax.rem(index % 4 - lax.rem(code, 4) + 4, 4), 1)
         line = slice(index // 4, index // 4 + 1)
         if index % 4 == 0:
             scene_out[line, :] = moved
@@ -279,11 +333,10 @@
 
 def first_kernel(
     me_ref, rank_ref, x, scenes, gains, w_qkv, w_proj, w_up, w_down,
-    send, notes, up, down, local, *scratch,
+    send, send_other, up, down, local, *scratch,
 ):
     s = Scratch(scratch)
     copies = start_weights(0, (w_qkv, w_proj, w_up, w_down), s)
-    write_notes(me_ref[0], rank_ref, scenes, notes)
     scene_columns(scenes, s)
     copies[0].wait()
     bound, largest = project(x, gains[0, 0:1], s)
@@ -327,9 +380,16 @@
             def _():
                 put(local, tile)
 
-            @pl.when(jnp.logical_not(is_up | is_down | stays))
+            far = jnp.logical_not(is_up | is_down | stays)
+            crosses = (owner ^ me) & 1 == 1
+
+            @pl.when(far & jnp.logical_not(crosses))
             def _():
-                put(send, owner)
+                put(send, owner // 2)
+
+            @pl.when(far & crosses)
+            def _():
+                put(send_other, owner // 2)
 
             return (slots[0] + is_up.astype(jnp.int32), slots[1] + is_down.astype(jnp.int32))
 
@@ -338,7 +398,7 @@
 
 
 def second_kernel(
-    me_ref, plan, scenes, gains, received, from_below, from_above, local,
+    me_ref, plan, scenes, gains, received, received_other, from_below, from_above, local,
     w_qkv, w_proj, w_up, w_down, out, x, in_sem, *scratch,
 ):
     s = Scratch(scratch)
@@ -346,7 +406,7 @@
     above, below = neighbours(me)
 
     def fetch(index, slots):
-        owner = plan[TILES + index]
+        owner = plan[STRIDE + index]
         target = x.at[pl.ds(pl.multiple_of(index * TILE, TILE), TILE)]
 
         def get(source, tile):
@@ -367,9 +427,16 @@
         def _():
             get(local, plan[index])
 
-        @pl.when(jnp.logical_not(is_up | is_down | stays))
+        far = jnp.logical_not(is_up | is_down | stays)
+        crosses = (owner ^ me) & 1 == 1
+
+        @pl.when(far & jnp.logical_not(crosses))
         def _():
-            get(received, owner)
+            get(received, owner // 2)
+
+        @pl.when(far & crosses)
+        def _():
+            get(received_other, owner // 2)
 
         return (slots[0] + is_up.astype(jnp.int32), slots[1] + is_down.astype(jnp.int32))
 
@@ -382,17 +449,17 @@
     quick = (bound <= SCORE_LIMIT) & (largest <= VALUE_LIMIT)
 
     def window_start(index):
-        first = plan[2 * TILES + index * (QUERY_BLOCK // TILE)]
+        first = plan[2 * STRIDE + index * (QUERY_BLOCK // TILE)]
         start = jnp.int32(0)
         for piece in range(1, (ROWS - WINDOW) // 128 + 1):
-            start = start + (plan[3 * TILES + 4 * piece - 1] < first).astype(jnp.int32)
+            start = start + (plan[3 * STRIDE + 4 * piece - 1] < first).astype(jnp.int32)
         return pl.multiple_of(start * 128, 128)
 
     fits = quick
     for index in range(ROWS // QUERY_BLOCK):
-        last = plan[3 * TILES + (index + 1) * (QUERY_BLOCK // TILE) - 1]
+        last = plan[3 * STRIDE + (index + 1) * (QUERY_BLOCK // TILE) - 1]
         end = window_start(index) + WINDOW
-        after = plan[2 * TILES + jnp.minimum(end // TILE, TILES - 1)]
+        after = plan[2 * STRIDE + jnp.minimum(end // TILE, TILES - 1)]
         fits = fits & ((end >= ROWS) | (after > last))
 
     @pl.when(fits)
@@ -425,23 +492,6 @@
 SMEM = pl.BlockSpec(memory_space=pltpu.SMEM)
 VMEM = pl.BlockSpec(memory_space=pltpu.VMEM)
 HBM = pl.BlockSpec(memory_space=pl.ANY)
-
-
-def exchange(rows, devices):
-    bits = devices.bit_length() - 1
-    lanes = rows.shape[1:]
-    shift = bits
-    while shift:
-        step = 2 if shift > 1 else 1
-        shift -= step
-        count = 1 << step
-        parts = rows.reshape((count, devices // count) + lanes)
-        pieces = [parts[0]] + [
-            lax.ppermute(parts[v], "seq", [(i, i ^ (v << shift)) for i in range(devices)])
-            for v in range(1, count)
-        ]
-        rows = jnp.stack(pieces, axis=1).reshape((devices,) + lanes)
-    return rows
 
 
 def shards(point_feats, scene_id, hilbert_rank, norm_gains, w_qkv, w_proj, w_up, w_down):
@@ -453,50 +503,97 @@
     params = pltpu.CompilerParams(vmem_limit_bytes=VMEM_BYTES)
     rows = jax.ShapeDtypeStruct((ROWS, C), BF16)
     few = jax.ShapeDtypeStruct((MOST_TILES * TILE, C), BF16)
-    send, notes, up, down, local = pl.pallas_call(
+    bins = jax.ShapeDtypeStruct((CHIPS * TILE, C), BF16)
+    ring = range(devices)
+    to_above = [(i, (i + 1) % devices) for i in ring]
+    to_below = [(i, (i - 1) % devices) for i in ring]
+    to_other = [(i, i ^ 1) for i in ring]
+    cores = [list(range(core, devices, 2)) for core in range(2)]
+
+    def among_chips(array):
+        return lax.all_to_all(
+            array, "seq", split_axis=0, concat_axis=0, tiled=True, axis_index_groups=cores
+        )
+
+    def note(count):
+        return jax.ShapeDtypeStruct((count, 1, 128), jnp.int32)
+
+    same, other, note_up, note_down = pl.pallas_call(
+        note_kernel,
+        in_specs=[SMEM, SMEM, VMEM],
+        out_specs=[VMEM] * 4,
+        out_shape=[note(CHIPS), note(CHIPS), note(1), note(1)],
+        scratch_shapes=[pltpu.VMEM((2 * CHIPS + 3, 1, 128), jnp.int32)],
+        compiler_params=params,
+        name="notes",
+    )(me_array, hilbert_rank, scenes)
+    same = among_chips(same)
+    note_below = lax.ppermute(note_up, "seq", to_above)
+    note_above = lax.ppermute(note_down, "seq", to_below)
+
+    send, send_other, up, down, local = pl.pallas_call(
         first_kernel,
         in_specs=[SMEM, SMEM, VMEM, VMEM, VMEM, HBM, HBM, HBM, HBM],
-        out_specs=[HBM, VMEM, HBM, HBM, HBM],
-        out_shape=[
-            jax.ShapeDtypeStruct((devices * TILE, C), BF16),
-            jax.ShapeDtypeStruct((devices, 1, 128), jnp.int32),
-            few,
-            few,
-            rows,
-        ],
+        out_specs=[HBM] * 5,
+        out_shape=[bins, bins, few, few, rows],
         scratch_shapes=scratch_shapes(),
         compiler_params=params,
         name="first_block",
     )(me_array, hilbert_rank, point_feats, scenes, norm_gains, *weights)
 
-    received = lax.all_to_all(send, "seq", split_axis=0, concat_axis=0, tiled=True)
-    ring = range(devices)
-    from_below = lax.ppermute(up, "seq", [(i, (i + 1) % devices) for i in ring])
-    from_above = lax.ppermute(down, "seq", [(i, (i - 1) % devices) for i in ring])
-    notes = exchange(notes, devices)
-    plan, scenes = pl.pallas_call(
-        plan_kernel,
-        in_specs=[SMEM, SMEM, SMEM, SMEM, VMEM, VMEM],
-        out_specs=[SMEM, VMEM],
-        out_shape=[
-            jax.ShapeDtypeStruct((4 * TILES,), jnp.int32),
-            jax.ShapeDtypeStruct((ROWS // 128, 128), jnp.int32),
-        ],
-        scratch_shapes=[pltpu.SMEM((2 * TILES,), jnp.int32)],
-        compiler_params=params,
-        cost_estimate=pl.CostEstimate(flops=1, bytes_accessed=1, transcendentals=0),
-        name="plan",
-    )(me_array, hilbert_rank, scene_id, notes, notes, scenes)
-
-    return pl.pallas_call(
-        second_kernel,
-        in_specs=[SMEM, SMEM, VMEM, VMEM] + [HBM] * 8,
-        out_specs=HBM,
-        out_shape=rows,
-        scratch_shapes=[pltpu.VMEM((ROWS, C), BF16), pltpu.SemaphoreType.DMA] + scratch_shapes(),
-        compiler_params=params,
-        name="second_block",
-    )(me_array, plan, scenes, norm_gains, received, from_below, from_above, local, *weights)
+    received = among_chips(send)
+    from_below = lax.ppermute(up, "seq", to_above)
+    from_above = lax.ppermute(down, "seq", to_below)
+    crossing = jnp.max(same[:, :, 127], axis=0, keepdims=True)
+    crossing = jnp.maximum(crossing, lax.ppermute(crossing, "seq", to_other))[0, 0] > 0
+
+    def make_plan(other):
+        return pl.pallas_call(
+            plan_kernel,
+            in_specs=[SMEM] * 7 + [VMEM] * 5,
+            out_specs=[SMEM, VMEM],
+            out_shape=[
+                jax.ShapeDtypeStruct((4 * STRIDE,), jnp.int32),
+                jax.ShapeDtypeStruct((ROWS // 128, 128), jnp.int32),
+            ],
+            scratch_shapes=[
+                pltpu.SMEM((STRIDE,), jnp.int32),
+                pltpu.VMEM((2 * CHIPS + 2 + ROWS // 128, 1, 128), jnp.int32),
+            ],
+            compiler_params=params,
+            name="plan",
+        )(
+            me_array, hilbert_rank, scene_id, same, other, note_below, note_above,
+            same, other, note_below, note_above, scenes,
+        )
+
+    def second(received, received_other, from_below, from_above, local, plan, scenes):
+        return pl.pallas_call(
+            second_kernel,
+            in_specs=[SMEM, SMEM, VMEM, VMEM] + [HBM] * 9,
+            out_specs=HBM,
+            out_shape=rows,
+            scratch_shapes=[pltpu.VMEM((ROWS, C), BF16), pltpu.SemaphoreType.DMA] + scratch_shapes(),
+            compiler_params=params,
+            name="second_block",
+        )(
+            me_array, plan, scenes, norm_gains,
+            received, received_other, from_below, from_above, local, *weights,
+        )
+
+    def with_crossing(tiles, other, received, from_below, from_above, local, plan, scenes):
+        tiles = among_chips(lax.ppermute(tiles, "seq", to_other))
+        plan, scenes = make_plan(among_chips(lax.ppermute(other, "seq", to_other)))
+        return second(received, tiles, from_below, from_above, local, plan, scenes)
+
+    def without_crossing(tiles, other, received, *rest):
+        return second(received, tiles, *rest)
+
+    plan, scenes_sorted = make_plan(jnp.zeros_like(other))
+    return lax.cond(
+        crossing, with_crossing, without_crossing,
+        send_other, other, received, from_below, from_above, local, plan, scenes_sorted,
+    )
 
 
 def solution(mesh):

time: 175 us -> 159 us (0.909); the launches traced: 175 us -> 157 us
  waiting for transfers between devices: 15.5 us -> 0.02 us
  starting transfers between devices: 46.4 us -> 35.9 us
  Pallas kernels: 110 us -> 114 us
  local copies, waits for them, and re-layouts: 2.13 us -> 4.05 us
    ppermute x12 -> x5, starting transfers between devices: 35.3 us -> 13.8 us  [the longest x1 7.17 us: shards(): from_above = lax.ppermute(down, 'seq', to_below)]
    ppermute x12 -> x5, waiting for transfers between devices: 15.5 us -> 0.01 us  [the longest x1 0.01 us: shards(): note_above = lax.ppermute(note_down, 'seq', to_below)]
    all_to_all x1 -> x2, starting transfers between devices: 11.1 us -> 22.1 us  [among_chips(): lax.all_to_all(array, 'seq', split_axis=0, concat_axis=0, tiled=True, axi...]
    pallas_call x2 -> x3, Pallas kernels: 57 us -> 62.1 us  [the longest x1 53.2 us: second(): pl.pallas_call(second_kernel, in_specs=[SMEM, SMEM, VMEM, VMEM] + [HBM] *...]
    unnamed x12 -> x24, local copies, waits for them, and re-layouts: 1.34 us -> 3.42 us
  transfers between devices with their start and end apart: 13 -> 7, of which waited for: 7 -> 0; matrix products, arithmetic and copies ran while one was open for 0% -> 1% of each run, Pallas kernels for 3% -> 38%
where the time goes in v3:
time: 159 us; the launch traced here: 157 us
  Pallas kernels  114 us (72%)
  starting transfers between devices  35.9 us (23%)
  local copies, waits for them, and re-layouts  4.05 us (3%)
    pallas_call x1, Pallas kernels, second(): pl.pallas_call(second_kernel, in_specs=[SMEM, SMEM, VMEM, VMEM] + [HBM] *...  53.2 us
    pallas_call x1, Pallas kernels, shards(): pl.pallas_call(first_kernel, in_specs=[SMEM, SMEM, VMEM, VMEM, VMEM, HBM,...  52.3 us
    all_to_all x2, starting transfers between devices, among_chips(): lax.all_to_all(array, 'seq', split_axis=0, concat_axis=0, tiled=True, axi...  22.1 us
    pallas_call x1, Pallas kernels, make_plan(): pl.pallas_call(plan_kernel, in_specs=[SMEM] * 7 + [VMEM] * 5, out_specs=[...  7.2 us
    ppermute x1, starting transfers between devices, shards(): from_above = lax.ppermute(down, 'seq', to_below)  7.17 us
    ppermute x1, starting transfers between devices, shards(): note_above = lax.ppermute(note_down, 'seq', to_below)  6.57 us
    unnamed x24, local copies, waits for them, and re-layouts  3.42 us
  transfers between devices with their start and end apart: 7, of which 0 were waited for; matrix products, arithmetic and copies ran while one was open for 1% of the time, Pallas kernels for 38%

profile of v3, /device:TPU:0, one launch (start us, length us, event | category | flops | bytes accessed | tf_op | source)
XLA Modules:
  0.0 156.9 jit_solution(2941923637088282941)
XLA Ops:
  0.0 0.0 copy-start.6
  0.0 0.0 copy-start.5
  0.0 0.7 copy-done.6
  0.7 0.0 copy-done.5
  0.7 1.8 %notes.1 = (s32[64,1,128]{2,1,0:T(1,128)}, s32[64,1,128]{2,1,0:T(1,128)}, s32[1,1,128]{2,1,0:T(1,128)}, s32[1,1,128]{2,1,0:T(1,128)}) custom-call(s32[1]{0:T(128)} %bitcast.2.me_ref, s32[1024]{0:T(1024)S(1)} %copy-done.6, s32[8,128]{1,0:T(8,128)S(1)} %bitcast.12), custom_call_target="tpu_custom_call" | custom-call | tf_op jit(solution)/shard_map/notes/pallas_call | solution.py:521
  2.5 0.0 copy-start.7
  2.5 11.6 %all-to-all-start.2 = ((s32[64,1,128]{2,1,0:T(1,128)}), s32[64,1,128]{2,1,0:T(1,128)S(1)}, u32[]{:S(2)}, u32[]{:S(2)}) async-start(s32[64,1,128]{2,1,0:T(1,128)} %get-tuple-element.114), calls=%async_computation.2 | async-start | bytes 65536 | tf_op jit(solution)/shard_map/all_to_all | solution.py:514
  14.1 0.0 copy-done.7
  14.1 0.0 copy-start.2
  14.1 52.3 %first_block.1 = (bf16[2048,256]{1,0:T(8,128)(2,1)}, bf16[2048,256]{1,0:T(8,128)(2,1)}, bf16[96,256]{1,0:T(8,128)(2,1)}, bf16[96,256]{1,0:T(8,128)(2,1)}, bf16[1024,256]{1,0:T(8,128)(2,1)}) custom-call(s32[1]{0:T(128)} %bitcast.2.me_ref, s32[1024]{0:T(1024)S(1)} %copy-done.6, bf16[1024,256]{1,0:T(8,128)(2,1)} %x.1, s32[8,128]{1,0:T(8,128)S(1)} %bitcast.13, ...), custom_call_target="tpu_custom_call" | custom-call | tf_op jit(solution)/shard_map/first_block/pallas_call | solution.py:534
  66.5 0.0 all-to-all-done.2.same_ref.same
  66.5 0.0 copy-start
  66.5 0.0 copy-start.1
  66.5 10.5 %all-to-all-start.3 = ((bf16[64,32,256]{2,1,0:T(8,128)(2,1)}), bf16[64,32,256]{2,1,0:T(8,128)(2,1)S(1)}, u32[]{:S(2)}, u32[]{:S(2)}) async-start(bf16[64,32,256]{2,1,0:T(8,128)(2,1)} %bitcast.10), calls=%async_computation.3 | async-start | bytes 2097152 | tf_op jit(solution)/shard_map/all_to_all | solution.py:514
  77.0 0.0 copy-start.13
  77.0 0.7 copy-done.13
  77.7 0.0 copy-start.12
  77.7 0.0 collective-permute-start.3
  77.7 0.6 copy-done.12
  78.3 6.6 %collective-permute-start.4 = (s32[1,1,128]{2,1,0:T(1,128)S(1)}, s32[1,1,128]{2,1,0:T(1,128)S(1)}, u32[]{:S(2)}, u32[]{:S(2)}) collective-permute-start(s32[1,1,128]{2,1,0:T(1,128)S(1)} %copy-done.12), channel_id=1, source_target_pairs={{0,127},{1,0},{2,1},{3,2},{4,3},{5,4},{6,5},{7,6},{8,7},{9,8},{10,... | collective-permute-start | bytes 1544 | tf_op jit(solution)/shard_map/ppermute | solution.py:532
  84.8 0.0 collective-permute-start.5
  84.8 7.2 %collective-permute-start.6 = (bf16[96,256]{1,0:T(8,128)(2,1)}, bf16[96,256]{1,0:T(8,128)(2,1)S(1)}, u32[]{:S(2)}, u32[]{:S(2)}) collective-permute-start(bf16[96,256]{1,0:T(8,128)(2,1)} %get-tuple-element.122), channel_id=1, source_target_pairs={{0,127},{1,0},{2,1},{3,2},{4,3},{5,4},{6,5},{7,6},{8,7},{9,8},{10,... | collective-permute-start | bytes 147464 | tf_op jit(solution)/shard_map/ppermute | solution.py:546
  92.0 0.8 slice_reduce_fusion
  92.9 0.0 collective-permute-start.2
  92.9 0.0 collective-permute-done.3.below_ref.from_below
  92.9 0.0 collective-permute-done.4.above_ref.from_above
  92.9 0.0 copy-start.8
  92.9 0.6 broadcast_in_dim.7.other_ref.other
  93.5 0.0 copy-done.8
  93.5 7.2 %plan.3 = (s32[192]{0:T(256)}, s32[8,128]{1,0:T(8,128)}) custom-call(s32[1]{0:T(128)} %bitcast.2.me_ref, s32[1024]{0:T(1024)S(1)} %copy-done.6, s32[1024]{0:T(1024)S(1)} %copy-done.5, s32[64,1,128]{2,1,0:T(1,128)S(1)} %all-to-all-done.2.same_ref.same, s32[64,1,128]{2,1,0:T(1,128)} %broadcast_in_dim.7.other_ref.other, ...), custom_call_target="tpu_custom_call" | custom-call | tf_op jit(solution)/shard_map/plan/pallas_call | solution.py:551
  100.7 0.0 collective-permute-done.2
  102.0 0.0 collective-permute-done.5
  102.0 0.0 collective-permute-done.6
  102.0 0.0 all-to-all-done.3
  102.0 0.0 copy-start.10
  102.0 0.0 copy-start.11
  102.0 0.0 copy-done.2
  102.0 0.0 copy-done
  102.0 0.0 copy-done.1
  102.1 0.6 copy-done.10
  102.7 0.0 copy-done.11
  102.7 53.4 %conditional.1 = (bf16[1024,256]{1,0:T(8,128)(2,1)S(1)}) conditional(s32[]{:T(128)} %bitcast.5, (s32[1]{0:T(128)}, s32[192]{0:T(256)S(1)}, s32[8,128]{1,0:T(8,128)S(1)}, f32[2,2,256]{2,1,0:T(2,128)S(1)}, bf16[2048,256]{1,0:T(8,128)(2,1)S(1)}, /*index=5*/bf16[2048,256]{1,0:T(8,128)(2,1)}, bf16[96,256]{1,0:T(8,128)(2,1)S(1)}, ...), branch_computations={%region_1.0_spmd, %region_2.0_spmd} | conditional | bytes 11733168 | solution.py:593
  102.7 53.2 %second_block.2 = bf16[1024,256]{1,0:T(8,128)(2,1)S(1)} custom-call(s32[1]{0:T(128)} %get-tuple-element.70.me_ref, s32[192]{0:T(256)S(1)} %get-tuple-element.71.plan, s32[8,128]{1,0:T(8,128)S(1)} %get-tuple-element.72.scenes, f32[2,2,256]{2,1,0:T(2,128)S(1)} %get-tuple-element.73.gains, bf16[2048,256]{1,0:T(8,128)(2,1)S(1)} %get-tuple-element.74.received, ...), custom_call_target="tpu_custom_call" | custom-call | tf_op jit(solution)/shard_map/cond/branch_0_fun/second_block/pallas_call | solution.py:571
  156.1 0.0 copy-start.4
  156.1 0.8 copy-done.4
Async XLA Ops:
  0.0 0.7 copy-start.6
  0.0 0.7 copy-start.5
  2.5 11.6 %copy-start.7 = (f32[2,2,256]{2,1,0:T(2,128)S(1)}, f32[2,2,256]{2,1,0:T(2,128)}, u32[]{:S(2)}) copy-start(f32[2,2,256]{2,1,0:T(2,128)} %gains.1) | copy-start | bytes 12292
  2.5 64.0 %all-to-all-start.2 = ((s32[64,1,128]{2,1,0:T(1,128)}), s32[64,1,128]{2,1,0:T(1,128)S(1)}, u32[]{:S(2)}, u32[]{:S(2)}) async-start(s32[64,1,128]{2,1,0:T(1,128)} %get-tuple-element.114), calls=%async_computation.2 | async-start | bytes 65536 | tf_op jit(solution)/shard_map/all_to_all | solution.py:514
  14.1 87.9 %copy-start.2 = (bf16[2,256,256]{2,1,0:T(8,128)(2,1)S(1)}, bf16[2,256,256]{2,1,0:T(8,128)(2,1)}, u32[]{:S(2)}) copy-start(bf16[2,256,256]{2,1,0:T(8,128)(2,1)} %w_proj.1) | copy-start | bytes 786436
  66.5 35.6 %copy-start = (bf16[2,256,1024]{2,1,0:T(8,128)(2,1)S(1)}, bf16[2,256,1024]{2,1,0:T(8,128)(2,1)}, u32[]{:S(2)}) copy-start(bf16[2,256,1024]{2,1,0:T(8,128)(2,1)} %w_up.1) | copy-start | bytes 3145732
  66.5 35.6 %copy-start.1 = (bf16[2,1024,256]{2,1,0:T(8,128)(2,1)S(1)}, bf16[2,1024,256]{2,1,0:T(8,128)(2,1)}, u32[]{:S(2)}) copy-start(bf16[2,1024,256]{2,1,0:T(8,128)(2,1)} %w_down.1) | copy-start | bytes 3145732
  66.5 35.5 %all-to-all-start.3 = ((bf16[64,32,256]{2,1,0:T(8,128)(2,1)}), bf16[64,32,256]{2,1,0:T(8,128)(2,1)S(1)}, u32[]{:S(2)}, u32[]{:S(2)}) async-start(bf16[64,32,256]{2,1,0:T(8,128)(2,1)} %bitcast.10), calls=%async_computation.3 | async-start | bytes 2097152 | tf_op jit(solution)/shard_map/all_to_all | solution.py:514
  77.0 0.7 copy-start.13
  77.7 0.6 copy-start.12
  77.7 15.2 %collective-permute-start.3 = (s32[1,1,128]{2,1,0:T(1,128)S(1)}, s32[1,1,128]{2,1,0:T(1,128)S(1)}, u32[]{:S(2)}, u32[]{:S(2)}) collective-permute-start(s32[1,1,128]{2,1,0:T(1,128)S(1)} %copy-done.13), channel_id=1, source_target_pairs={{0,1},{1,2},{2,3},{3,4},{4,5},{5,6},{6,7},{7,8},{8,9},{9,10},{10,1... | collective-permute-start | bytes 1544 | tf_op jit(solution)/shard_map/ppermute | solution.py:531
  78.3 14.6 %collective-permute-start.4 = (s32[1,1,128]{2,1,0:T(1,128)S(1)}, s32[1,1,128]{2,1,0:T(1,128)S(1)}, u32[]{:S(2)}, u32[]{:S(2)}) collective-permute-start(s32[1,1,128]{2,1,0:T(1,128)S(1)} %copy-done.12), channel_id=1, source_target_pairs={{0,127},{1,0},{2,1},{3,2},{4,3},{5,4},{6,5},{7,6},{8,7},{9,8},{10,... | collective-permute-start | bytes 1544 | tf_op jit(solution)/shard_map/ppermute | solution.py:532
  84.8 17.1 %collective-permute-start.5 = (bf16[96,256]{1,0:T(8,128)(2,1)}, bf16[96,256]{1,0:T(8,128)(2,1)S(1)}, u32[]{:S(2)}, u32[]{:S(2)}) collective-permute-start(bf16[96,256]{1,0:T(8,128)(2,1)} %get-tuple-element.121), channel_id=1, source_target_pairs={{0,1},{1,2},{2,3},{3,4},{4,5},{5,6},{6,7},{7,8},{8,9},{9,10},{10,1... | collective-permute-start | bytes 147464 | tf_op jit(solution)/shard_map/ppermute | solution.py:545
  84.8 17.1 %collective-permute-start.6 = (bf16[96,256]{1,0:T(8,128)(2,1)}, bf16[96,256]{1,0:T(8,128)(2,1)S(1)}, u32[]{:S(2)}, u32[]{:S(2)}) collective-permute-start(bf16[96,256]{1,0:T(8,128)(2,1)} %get-tuple-element.122), channel_id=1, source_target_pairs={{0,127},{1,0},{2,1},{3,2},{4,3},{5,4},{6,5},{7,6},{8,7},{9,8},{10,... | collective-permute-start | bytes 147464 | tf_op jit(solution)/shard_map/ppermute | solution.py:546
  92.9 7.9 %collective-permute-start.2 = (s32[1,1]{1,0:T(1,128)}, s32[1,1]{1,0:T(1,128)}, u32[]{:S(2)}, u32[]{:S(2)}) collective-permute-start(s32[1,1]{1,0:T(1,128)} %bitcast.4), channel_id=1, source_target_pairs={{0,1},{1,0},{2,3},{3,2},{4,5},{5,4},{6,7},{7,6},{8,9},{9,8},{10,11... | collective-permute-start | bytes 20 | tf_op jit(solution)/shard_map/ppermute | solution.py:548
  92.9 0.6 copy-start.8
  102.0 0.7 copy-start.10
  102.0 0.7 copy-start.11
  156.1 0.8 copy-start.4

commit v4 on v0

v4 whole, which is shorter than its diff:
```python
import functools

import jax
import jax.numpy as jnp
from jax import lax
from jax.experimental import pallas as pl
from jax.experimental.pallas import tpu as pltpu
from jax.sharding import PartitionSpec as P

C = 256
HEADS = 16
HEAD = 16
ROWS = 1024
FFN = 1024
TILES = 32
TILE = 32
MOST_TILES = 3
CHIPS = 64
NOTE = 8
EPSILON = 1e-05
QUERY_BLOCK = 256
WINDOW = 512
ROW_BLOCK = 256
SPLIT_SCALE = 8.0
SCORE_LIMIT = 40.0
VALUE_LIMIT = 40.0
BF16 = jnp.bfloat16
F32 = jnp.float32
F8 = jnp.float8_e4m3fn
VMEM_BYTES = 56 << 20


def dot(left, right, left_dim=1, right_dim=0):
    return lax.dot_general(
        left, right, (((left_dim,), (right_dim,)), ((), ())), preferred_element_type=F32
    )


def layer_norm(values, gain):
    center = values - jnp.mean(values, axis=-1, keepdims=True)
    spread = jnp.mean(center * center, axis=-1, keepdims=True)
    return (center * lax.rsqrt(spread + EPSILON) * gain).astype(BF16)


def split(values):
    scaled = values.astype(F32) * SPLIT_SCALE
    high = scaled.astype(F8).astype(F32)
    low = scaled - high
    return high, low


def gelu(values):
    return 0.5 * values * (1.0 + lax.erf(values * (0.5**0.5)))


class Scratch:
    names = (
        "w_qkv", "w_proj", "w_up", "w_down", "key", "query", "key_split", "query_split",
        "value", "scene_col", "mask", "attended", "normed", "sems", "out_sem",
    )

    def __init__(self, refs):
        for name, ref in zip(self.names, refs, strict=True):
            setattr(self, name, ref)


def scratch_shapes():
    return [
        pltpu.VMEM((C, 3 * C), BF16),
        pltpu.VMEM((C, C), BF16),
        pltpu.VMEM((C, FFN), BF16),
        pltpu.VMEM((FFN, C), BF16),
        pltpu.VMEM((2, ROWS, 128), BF16),
        pltpu.VMEM((2, 128, ROWS), BF16),
        pltpu.VMEM((HEADS // 2, ROWS, 128), F8),
        pltpu.VMEM((HEADS, 128, ROWS), F8),
        pltpu.VMEM((HEADS, 2 * HEAD, ROWS), BF16),
        pltpu.VMEM((ROWS, 128), F32),
        pltpu.VMEM((ROWS, QUERY_BLOCK), BF16),
        pltpu.VMEM((C, ROWS), BF16),
        pltpu.VMEM((ROWS, C), BF16),
        pltpu.SemaphoreType.DMA((4,)),
        pltpu.SemaphoreType.DMA,
    ]


def start_weights(block, weights, s):
    copies = [
        pltpu.make_async_copy(source.at[block], target, s.sems.at[i])
        for i, (source, target) in enumerate(
            zip(weights, (s.w_qkv, s.w_proj, s.w_up, s.w_down), strict=True)
        )
    ]
    for copy in copies:
        copy.start()
    return copies


def project(x, gain, s):
    for start in range(0, ROWS, ROW_BLOCK):
        rows = slice(start, start + ROW_BLOCK)
        s.normed[rows] = layer_norm(x[rows].astype(F32), gain)
    normed = s.normed[...]
    query = dot(s.w_qkv[:, 0:C], normed, 0, 1).astype(BF16)
    value = dot(s.w_qkv[:, 2 * C : 3 * C], normed, 0, 1).astype(BF16)
    for head in range(HEADS):
        s.value[head, 0:HEAD, :] = value[HEAD * head : HEAD * (head + 1)]
        s.value[head, HEAD:, :] = jnp.ones((HEAD, ROWS), BF16)
    s.query[0] = query[0:128]
    s.query[1] = query[128:256]
    high, low = split(query)
    for head in range(HEADS):
        part = slice(HEAD * head, HEAD * (head + 1))
        both = jnp.concatenate([high[part].astype(BF16), low[part].astype(BF16)], axis=0).astype(F8)
        own, other = 64 * (head % 2), 64 * (1 - head % 2)
        s.query_split[head, own : own + 32, :] = both
        s.query_split[head, own + 32 : own + 64, :] = both
        s.query_split[head, other : other + 64, :] = jnp.zeros((64, ROWS), F8)
    squares = query.astype(F32) * query.astype(F32)
    query_norm = jnp.max(jnp.sum(squares.reshape(HEADS, HEAD, ROWS), axis=1), axis=1, keepdims=True)

    row = lax.broadcasted_iota(jnp.int32, (64, 256), 0)
    lane = lax.broadcasted_iota(jnp.int32, (64, 256), 1)
    same = row == (lane // 64) * HEAD + lane % HEAD
    spread_high = jnp.where(same & (lane % 64 < 32), 1.0, 0.0).astype(BF16)
    spread_low = jnp.where(same & (lane % 64 >= 32), 1.0, 0.0).astype(BF16)
    spread = jnp.concatenate([spread_high, spread_low], axis=0).astype(F8)
    channel = lax.broadcasted_iota(jnp.int32, (C, 128), 0)
    column = lax.broadcasted_iota(jnp.int32, (C, 128), 1)
    head_sum = jnp.where(channel // HEAD == column, 1.0, 0.0).astype(BF16)
    key_norm = jnp.zeros((1, 128), F32)
    highest = jnp.max(jnp.abs(query.astype(F32)))
    key_high = jnp.zeros((1, C), F32)
    for start in range(0, ROWS, ROW_BLOCK):
        rows = slice(start, start + ROW_BLOCK)
        key = dot(s.normed[rows], s.w_qkv[:, C : 2 * C]).astype(BF16)
        s.key[0, rows] = key[:, 0:128]
        s.key[1, rows] = key[:, 128:256]
        wide = key.astype(F32)
        key_high = jnp.maximum(key_high, jnp.max(jnp.abs(wide), axis=0, keepdims=True))
        norms = dot((wide * wide).astype(BF16), head_sum)
        key_norm = jnp.maximum(key_norm, jnp.max(norms, axis=0, keepdims=True))
        high, low = split(key)
        for quarter in range(4):
            lanes = slice(64 * quarter, 64 * quarter + 64)
            pair = jnp.concatenate([high[:, lanes], low[:, lanes]], axis=1).astype(F8)
            expanded = dot(pair, spread).astype(F8)
            s.key_split[2 * quarter, rows] = expanded[:, 0:128]
            s.key_split[2 * quarter + 1, rows] = expanded[:, 128:256]
    largest = jnp.maximum(highest, jnp.max(key_high))
    bound = 0.25 * 1.02 * jnp.sqrt(jnp.max(query_norm) * jnp.max(key_norm))
    return bound, largest


def make_mask(keys, count, index, scenes, s):
    for lane in range(0, QUERY_BLOCK, 128):
        row = scenes[pl.ds(index * (QUERY_BLOCK // 128) + lane // 128, 1), :].astype(F32)
        for start in range(0, count, 128):
            same = s.scene_col[pl.ds(keys + start, 128), :] == row
            s.mask[start : start + 128, lane : lane + 128] = jnp.where(same, 1.0, 0.0).astype(BF16)


def finish(head, queries, output, s):
    start = HEAD * head if isinstance(head, int) else pl.multiple_of(HEAD * head, HEAD)
    s.attended[pl.ds(start, HEAD), queries] = (
        output[0:HEAD] * (1.0 / output[HEAD : HEAD + 1])
    ).astype(BF16)


def attend_bounded(count, first_key, scenes, s):
    def block(index, carry):
        queries = pl.ds(pl.multiple_of(index * QUERY_BLOCK, QUERY_BLOCK), QUERY_BLOCK)
        start = first_key(index)
        keys = pl.ds(start, count)
        make_mask(start, count, index, scenes, s)
        mask = s.mask[0:count]
        for head in range(HEADS):
            score = dot(s.key_split[head // 2, keys, :], s.query_split[head, :, queries])
            weight = jnp.exp(score * (0.25 / SPLIT_SCALE**2)).astype(BF16) * mask
            finish(head, queries, dot(s.value[head, :, keys], weight), s)
        return carry

    lax.fori_loop(0, ROWS // QUERY_BLOCK, block, 0)


def attend_any(scenes, s):
    lane_head = lax.broadcasted_iota(jnp.int32, (1, 128), 1) // HEAD

    def block(index, carry):
        queries = pl.ds(pl.multiple_of(index * QUERY_BLOCK, QUERY_BLOCK), QUERY_BLOCK)
        make_mask(0, ROWS, index, scenes, s)

        def one_head(head, carry):
            group = head // 8
            lanes = jnp.where(lane_head == head % 8, 1.0, 0.0).astype(BF16)
            score = dot(s.key[group] * lanes, s.query[group, :, queries]) * 0.25
            score = jnp.where(s.mask[...] > 0, score, F32(-1e30))
            top = jnp.max(score, axis=0, keepdims=True)
            weight = jnp.exp(score - top).astype(BF16)
            finish(head, queries, dot(s.value[head], weight), s)
            return carry

        return lax.fori_loop(0, HEADS, one_head, carry)

    lax.fori_loop(0, ROWS // QUERY_BLOCK, block, 0)


def scene_columns(scenes, s):
    for start in range(0, ROWS, 128):
        piece = scenes[start // 128 : start // 128 + 1, :].astype(F32)
        s.scene_col[start : start + 128, :] = jnp.transpose(jnp.broadcast_to(piece, (128, 128)))


def mlp_rows(rows, x, gain, s):
    attended = jnp.transpose(s.attended[:, rows])
    middle = (x[rows].astype(F32) + dot(attended, s.w_proj[...])).astype(BF16)
    normed = layer_norm(middle.astype(F32), gain)
    hidden = gelu(dot(normed, s.w_up[...])).astype(BF16)
    return (middle.astype(F32) + dot(hidden, s.w_down[...])).astype(BF16)


def neighbours(me):
    return lax.rem(me + 1, 128), lax.rem(me + 127, 128)


def write_notes(scenes, flag, notes):
    lane = lax.broadcasted_iota(jnp.int32, (1, 128), 1)
    flags = jnp.where(lane == TILE + 1, flag, 0)
    empty = jnp.broadcast_to(flags, (NOTE, 128)).astype(F32).astype(BF16)
    notes.empty[:, :, 0:128] = jnp.broadcast_to(empty[None], (CHIPS, NOTE, 128))
    notes.empty[:, :, 128:256] = jnp.zeros((CHIPS, NOTE, 128), BF16)
    for tile in range(TILES):
        row = scenes[tile // 4 : tile // 4 + 1, (tile % 4) * TILE : (tile % 4 + 1) * TILE]
        row = jnp.concatenate([row] * 4, axis=1)
        row = jnp.where(lane < TILE, row, jnp.where(lane == TILE, tile + 1, flags))
        row = jnp.broadcast_to(row, (NOTE, 128)).astype(F32).astype(BF16)
        notes.result[tile, TILE:, 0:128] = row
        notes.result[tile, TILE:, 128:256] = jnp.zeros((NOTE, 128), BF16)


def sort_tiles(me, entries, plan_out, scene_out):
    count = sum(notes.shape[0] for notes, _, _ in entries)
    total = -(-count // 128) * 128
    tables, sources = [], []
    for notes, first, step in entries:
        tables.append(notes[:, 0:1, :].astype(F32).reshape(notes.shape[0], 128))
        index = lax.broadcasted_iota(jnp.int32, (notes.shape[0], 1), 0)
        sources.append(first + step * index)
    if total > count:
        tables.append(jnp.zeros((total - count, 128), F32))
        sources.append(jnp.zeros((total - count, 1), jnp.int32))
    table = jnp.concatenate(tables, axis=0)
    source = jnp.concatenate(sources, axis=0)
    place = table[:, TILE : TILE + 1]
    far = F32(1 << 20)
    key = jnp.where(place > 0, source.astype(F32) * TILE + place, far)
    wide = jnp.broadcast_to(key, (total, 128))
    row = jnp.concatenate(
        [jnp.transpose(wide[start : start + 128])[0:1] for start in range(0, total, 128)], axis=1
    )
    rank = jnp.sum((key < row).astype(F32), axis=0, keepdims=True)
    rank = jnp.where(row < far, rank, -1.0)
    target = lax.broadcasted_iota(jnp.int32, (TILES, total), 0).astype(F32)
    chosen = jnp.where(rank == target, 1.0, 0.0).astype(BF16)
    lane = lax.broadcasted_iota(jnp.int32, (total, 128), 1)
    entry = lax.broadcasted_iota(jnp.int32, (total, 128), 0)
    table = jnp.where(lane == TILE + 2, entry % 128, jnp.where(lane == TILE + 3, entry // 128, table.astype(jnp.int32)))
    ordered = dot(chosen, table.astype(F32).astype(BF16)).astype(jnp.int32)
    plan_out[...] = ordered
    group = lax.broadcasted_iota(jnp.int32, (1, 128), 1) // TILE
    lines = jnp.zeros((ROWS // 128, 128), jnp.int32)
    for part in range(4):
        piece = plan_out[pl.ds(part, ROWS // 128, stride=4), :]
        piece = pltpu.roll(piece, TILE * part, 1) if part else piece
        lines = jnp.where(group == part, piece, lines)
    scene_out[...] = lines


class Notes:
    def __init__(self, empty, result):
        self.empty, self.result = empty, result


def first_kernel(
    me_ref, flag_ref, rank_ref, x, scenes, gains, w_qkv, w_proj, w_up, w_down,
    send, send_other, up, down, local, empty, result, fill_sem, *scratch,
):
    s = Scratch(scratch)
    copies = start_weights(0, (w_qkv, w_proj, w_up, w_down), s)
    write_notes(scenes, flag_ref[0], Notes(empty, result))
    fills = []
    for index, target in enumerate((send, send_other, up, down, local)):
        count = target.shape[0]
        fills.append(
            pltpu.make_async_copy(
                empty.at[0:count], target.at[:, TILE : TILE + NOTE], fill_sem.at[index]
            )
        )
        fills[-1].start()
    scene_columns(scenes, s)
    copies[0].wait()
    bound, largest = project(x, gains[0, 0:1], s)
    quick = (bound <= SCORE_LIMIT) & (largest <= VALUE_LIMIT)

    @pl.when(quick)
    def _():
        attend_bounded(ROWS, lambda index: 0, scenes, s)

    @pl.when(jnp.logical_not(quick))
    def _():
        attend_any(scenes, s)

    for copy in copies[1:] + fills:
        copy.wait()
    me = me_ref[0]
    above, below = neighbours(me)
    slots = (jnp.int32(0), jnp.int32(0))
    for start in range(0, ROWS, ROW_BLOCK):
        rows = mlp_rows(slice(start, start + ROW_BLOCK), x, gains[0, 1:2], s)
        tiles = slice(start // TILE, (start + ROW_BLOCK) // TILE)
        result[tiles, 0:TILE, :] = rows.reshape(ROW_BLOCK // TILE, TILE, C)

        def one_tile(tile, slots):
            owner = rank_ref[tile * TILE] // ROWS

            def put(target, index):
                pltpu.make_async_copy(result.at[tile], target.at[index], s.out_sem).start()

            is_up, is_down, stays = owner == above, owner == below, owner == me

            @pl.when(is_up)
            def _():
                put(up, jnp.minimum(slots[0], MOST_TILES - 1))

            @pl.when(is_down)
            def _():
                put(down, jnp.minimum(slots[1], MOST_TILES - 1))

            @pl.when(stays)
            def _():
                put(local, tile)

            far = jnp.logical_not(is_up | is_down | stays)
            crosses = (owner ^ me) & 1 == 1

            @pl.when(far & jnp.logical_not(crosses))
            def _():
                put(send, owner // 2)

            @pl.when(far & crosses)
            def _():
                put(send_other, owner // 2)

            return (slots[0] + is_up.astype(jnp.int32), slots[1] + is_down.astype(jnp.int32))

        slots = lax.fori_loop(start // TILE, (start + ROW_BLOCK) // TILE, one_tile, slots)
    pltpu.make_async_copy(result, local, s.out_sem).wait()


def second_kernel(
    me_ref, gains, *refs, sources,
):
    arrays, refs = refs[:sources], refs[sources:]
    w_qkv, w_proj, w_up, w_down, out, x, notes, plan_vmem, scenes, result, plan, note_sems, in_sem = refs[:13]
    s = Scratch(refs[13:])
    me = me_ref[0]
    core = lax.rem(me, 2)
    above, below = neighbours(me)
    firsts = ((core, 2), (1 - core, 2))[: sources - 3] + ((below, 0), (above, 0), (me, 0))
    starts, fetches = [], []
    start = 0
    for index, array in enumerate(arrays):
        count = array.shape[0]
        starts.append(start)
        fetches.append(
            pltpu.make_async_copy(
                array.at[:, TILE : TILE + NOTE, 0:128], notes.at[start : start + count], note_sems.at[index]
            )
        )
        fetches[-1].start()
        start += count
    copies = start_weights(1, (w_qkv, w_proj, w_up, w_down), s)
    for fetch in fetches:
        fetch.wait()
    ends = starts[1:] + [start]
    entries = [(notes[a:b], *first) for a, b, first in zip(starts, ends, firsts, strict=True)]
    sort_tiles(me, entries, plan_vmem, scenes)
    to_scalars = pltpu.make_async_copy(plan_vmem, plan, note_sems.at[0])
    to_scalars.start()
    to_scalars.wait()

    def fetch(index, carry):
        entry = plan[index, TILE + 2] + 128 * plan[index, TILE + 3]
        target = x.at[pl.ds(pl.multiple_of(index * TILE, TILE), TILE)]
        for array, first, end in zip(arrays, starts, ends, strict=True):

            @pl.when((entry >= first) & (entry < end))
            def _(array=array, first=first):
                pltpu.make_async_copy(array.at[entry - first, 0:TILE], target, in_sem).start()

        return carry

    lax.fori_loop(0, TILES, fetch, 0)
    scene_columns(scenes, s)
    pltpu.make_async_copy(result, x, in_sem).wait()
    copies[0].wait()
    bound, largest = project(x, gains[1, 0:1], s)
    quick = (bound <= SCORE_LIMIT) & (largest <= VALUE_LIMIT)

    def window_start(index):
        first = plan[index * (QUERY_BLOCK // TILE), 0]
        start = jnp.int32(0)
        for piece in range(1, (ROWS - WINDOW) // 128 + 1):
            start = start + (plan[4 * piece - 1, TILE - 1] < first).astype(jnp.int32)
        return pl.multiple_of(start * 128, 128)

    fits = quick
    for index in range(ROWS // QUERY_BLOCK):
        last = plan[(index + 1) * (QUERY_BLOCK // TILE) - 1, TILE - 1]
        end = window_start(index) + WINDOW
        after = plan[jnp.minimum(end // TILE, TILES - 1), 0]
        fits = fits & ((end >= ROWS) | (after > last))

    @pl.when(fits)
    def _():
        attend_bounded(WINDOW, window_start, scenes, s)

    @pl.when(quick & jnp.logical_not(fits))
    def _():
        attend_bounded(ROWS, lambda index: 0, scenes, s)

    @pl.when(jnp.logical_not(quick))
    def _():
        attend_any(scenes, s)

    for copy in copies[1:]:
        copy.wait()
    for start in range(0, ROWS, ROW_BLOCK):
        result[start : start + ROW_BLOCK] = mlp_rows(slice(start, start + ROW_BLOCK), x, gains[1, 1:2], s)

        def one_tile(index, carry):
            source = result.at[pl.ds(pl.multiple_of(index * TILE, TILE), TILE)]
            place = jnp.clip(plan[index, TILE] - 1, 0, TILES - 1)
            target = out.at[pl.ds(pl.multiple_of(place * TILE, TILE), TILE)]
            pltpu.make_async_copy(source, target, s.out_sem).start()
            return carry

        lax.fori_loop(start // TILE, (start + ROW_BLOCK) // TILE, one_tile, 0)
    pltpu.make_async_copy(result, out, s.out_sem).wait()


SMEM = pl.BlockSpec(memory_space=pltpu.SMEM)
VMEM = pl.BlockSpec(memory_space=pltpu.VMEM)
HBM = pl.BlockSpec(memory_space=pl.ANY)


def shards(point_feats, scene_id, hilbert_rank, norm_gains, w_qkv, w_proj, w_up, w_down):
    devices = lax.axis_size("seq")
    me = lax.axis_index("seq")
    me_array = me.reshape(1).astype(jnp.int32)
    weights = (w_qkv, w_proj, w_up, w_down)
    scenes = scene_id.reshape(ROWS // 128, 128)
    params = pltpu.CompilerParams(vmem_limit_bytes=VMEM_BYTES)
    rows = jax.ShapeDtypeStruct((ROWS, C), BF16)
    few = jax.ShapeDtypeStruct((MOST_TILES, TILE + NOTE, C), BF16)
    bins = jax.ShapeDtypeStruct((CHIPS, TILE + NOTE, C), BF16)
    own = jax.ShapeDtypeStruct((TILES, TILE + NOTE, C), BF16)
    ring = range(devices)
    to_above = [(i, (i + 1) % devices) for i in ring]
    to_below = [(i, (i - 1) % devices) for i in ring]
    to_other = [(i, i ^ 1) for i in ring]
    cores = [list(range(core, devices, 2)) for core in range(2)]

    def among_chips(array):
        return lax.all_to_all(
            array, "seq", split_axis=0, concat_axis=0, tiled=True, axis_index_groups=cores
        )

    owner = hilbert_rank // ROWS
    beside = (owner == (me + 1) % devices) | (owner == (me + devices - 1) % devices)
    crosses = jnp.max(jnp.where(beside, 0, (owner ^ me) & 1)).reshape(1)
    crosses = jnp.maximum(crosses, lax.ppermute(crosses, "seq", to_other))

    send, send_other, up, down, local = pl.pallas_call(
        first_kernel,
        in_specs=[SMEM, SMEM, SMEM, VMEM, VMEM, VMEM, HBM, HBM, HBM, HBM],
        out_specs=[HBM] * 5,
        out_shape=[bins, bins, few, few, own],
        scratch_shapes=[
            pltpu.VMEM((CHIPS, NOTE, C), BF16),
            pltpu.VMEM((TILES, TILE + NOTE, C), BF16),
            pltpu.SemaphoreType.DMA((5,)),
        ]
        + scratch_shapes(),
        compiler_params=params,
        name="first_block",
    )(me_array, crosses, hilbert_rank, point_feats, scenes, norm_gains, *weights)

    received = among_chips(send)
    from_below = lax.ppermute(up, "seq", to_above)
    from_above = lax.ppermute(down, "seq", to_below)

    def second(*arrays):
        noted = sum(array.shape[0] for array in arrays)
        return pl.pallas_call(
            functools.partial(second_kernel, sources=len(arrays)),
            in_specs=[SMEM, VMEM] + [HBM] * (len(arrays) + 4),
            out_specs=HBM,
            out_shape=rows,
            scratch_shapes=[
                pltpu.VMEM((ROWS, C), BF16),
                pltpu.VMEM((noted, NOTE, 128), BF16),
                pltpu.VMEM((TILES, 128), jnp.int32),
                pltpu.VMEM((ROWS // 128, 128), jnp.int32),
                pltpu.VMEM((ROWS, C), BF16),
                pltpu.SMEM((TILES, 128), jnp.int32),
                pltpu.SemaphoreType.DMA((5,)),
                pltpu.SemaphoreType.DMA,
            ]
            + scratch_shapes(),
            compiler_params=params,
            name="second_block",
        )(me_array, norm_gains, *arrays, *weights)

    def with_crossing(tiles, received, *rest):
        return second(received, among_chips(lax.ppermute(tiles, "seq", to_other)), *rest)

    def without_crossing(tiles, received, *rest):
        return second(received, *rest)

    return lax.cond(
        jnp.max(received[:, TILE, TILE + 1]) > 0, with_crossing, without_crossing,
        send_other, received, from_below, from_above, local,
    )


def solution(mesh):
    placed = (P("seq", None), P("seq"), P("seq"), P(), P(), P(), P(), P())
    return jax.shard_map(
        shards, mesh=mesh, in_specs=placed, out_specs=P("seq", None), check_vma=False
    )
```

time: 176 us -> 147 us (0.84)
  blocking collectives: 47 us -> 0 us
  waiting for transfers between devices: 0.01 us -> 16 us
  local copies, waits for them, and re-layouts: 2.93 us -> 0.81 us
  Pallas kernels: 104 us -> 106 us
    all_gather x1 -> x0, blocking collectives: 47 us -> none  [shards(): tags = lax.all_gather(tagged, 'seq', tiled=True)]
    all_to_all x1, waiting for transfers between devices: 0.01 us -> 14.7 us  [among_chips(): lax.all_to_all(array, 'seq', split_axis=0, concat_axis=0, tiled=True, axi...]
    reduce_max x0 -> x2, other arithmetic: none -> 2.13 us  [the longest x1 1.33 us: shards(): crosses = jnp.max(jnp.where(beside, 0, (owner ^ me) & 1)).reshape(1)]
    pallas_call x2, Pallas kernels: 104 us -> 106 us  [the longest x1 53.9 us: second(): pl.pallas_call(functools.partial(second_kernel, sources=len(arrays)), in_...]
    ppermute x2 -> x3, starting transfers between devices: 7.23 us -> 7.24 us  [the longest x1 7.16 us: shards(): from_above = lax.ppermute(down, 'seq', to_below)]
  transfers between devices with their start and end apart: 3 -> 4, of which waited for: 0 -> 2; matrix products, arithmetic and copies ran while one was open for 2% -> 1% of each run, Pallas kernels for 0% -> 0%
where the time goes in v4:
time: 147 us; the launch traced here: 146 us
  Pallas kernels  106 us (72%)
  starting transfers between devices  18.9 us (13%)
  waiting for transfers between devices  16 us (11%)
  other arithmetic  2.13 us (1%)
  between operations  2.01 us (1%)
    pallas_call x1, Pallas kernels, second(): pl.pallas_call(functools.partial(second_kernel, sources=len(arrays)), in_...  53.9 us
    pallas_call x1, Pallas kernels, shards(): pl.pallas_call(first_kernel, in_specs=[SMEM, SMEM, SMEM, VMEM, VMEM, VMEM...  52.4 us
    all_to_all x1, waiting for transfers between devices, among_chips(): lax.all_to_all(array, 'seq', split_axis=0, concat_axis=0, tiled=True, axi...  14.7 us
    all_to_all x1, starting transfers between devices, among_chips(): lax.all_to_all(array, 'seq', split_axis=0, concat_axis=0, tiled=True, axi...  11.6 us
    ppermute x1, starting transfers between devices, shards(): from_above = lax.ppermute(down, 'seq', to_below)  7.16 us
  transfers between devices with their start and end apart: 4, of which 2 were waited for; matrix products, arithmetic and copies ran while one was open for 1% of the time, Pallas kernels for 0%

profile of v4, /device:TPU:0, one launch (start us, length us, event | category | flops | bytes accessed | tf_op | source)
XLA Modules:
  0.0 146.5 jit_solution(16836897068053461954)
XLA Ops:
  0.0 1.3 select_reduce_fusion
  1.3 0.0 collective-permute-start.1
  1.3 1.2 collective-permute-done.1
  3.8 52.4 %first_block.1 = (bf16[64,40,256]{2,1,0:T(8,128)(2,1)}, bf16[64,40,256]{2,1,0:T(8,128)(2,1)}, bf16[3,40,256]{2,1,0:T(8,128)(2,1)}, bf16[3,40,256]{2,1,0:T(8,128)(2,1)}, bf16[32,40,256]{2,1,0:T(8,128)(2,1)}) custom-call(s32[1]{0:T(128)} %bitcast.me_ref, s32[1]{0:T(128)S(6)} %max.3.flag_ref, s32[1024]{0:T(1024)} %rank_ref.1, bf16[1024,256]{1,0:T(8,128)(2,1)} %x.1, ...), custom_call_target="tpu_custom_call" | custom-call | tf_op jit(solution)/shard_map/first_block/pallas_call | solution.py:484
  56.2 0.0 copy-start
  56.2 0.0 copy-start.1
  56.3 0.0 copy-start.6
  56.3 11.6 %all-to-all-start.1 = ((bf16[64,40,256]{2,1,0:T(8,128)(2,1)}), bf16[64,40,256]{2,1,0:T(8,128)(2,1)S(1)}, u32[]{:S(2)}, u32[]{:S(2)}) async-start(bf16[64,40,256]{2,1,0:T(8,128)(2,1)} %get-tuple-element.76), calls=%async_computation.1 | async-start | bytes 2621440 | tf_op jit(solution)/shard_map/all_to_all | solution.py:475
  67.9 0.1 collective-permute-start.2
  68.0 7.2 %collective-permute-start.3 = (bf16[3,40,256]{2,1,0:T(8,128)(2,1)}, bf16[3,40,256]{2,1,0:T(8,128)(2,1)S(1)}, u32[]{:S(2)}, u32[]{:S(2)}) collective-permute-start(bf16[3,40,256]{2,1,0:T(8,128)(2,1)} %get-tuple-element.78), channel_id=1, source_target_pairs={{0,127},{1,0},{2,1},{3,2},{4,3},{5,4},{6,5},{7,6},{8,7},{9,8},{10,... | collective-permute-start | bytes 184328 | tf_op jit(solution)/shard_map/ppermute | solution.py:501
  75.2 14.7 %all-to-all-done.1 = bf16[64,40,256]{2,1,0:T(8,128)(2,1)S(1)} async-done(((bf16[64,40,256]{2,1,0:T(8,128)(2,1)}), bf16[64,40,256]{2,1,0:T(8,128)(2,1)S(1)}, u32[]{:S(2)}, u32[]{:S(2)}) %all-to-all-start.1) | async-done | bytes 1310752 | tf_op jit(solution)/shard_map/all_to_all | solution.py:475
  89.9 0.8 slice_reduce_fusion
  91.3 0.0 collective-permute-done.2
  91.3 0.0 collective-permute-done.3
  91.3 0.0 copy-done
  91.3 0.0 copy-done.1
  91.3 0.0 copy-done.6
  91.4 54.3 %conditional.1 = (bf16[1024,256]{1,0:T(8,128)(2,1)S(1)}) conditional(s32[]{:T(128)} %convert_element_type.3, (s32[1]{0:T(128)}, f32[2,2,256]{2,1,0:T(2,128)S(1)}, bf16[64,40,256]{2,1,0:T(8,128)(2,1)S(1)}, bf16[3,40,256]{2,1,0:T(8,128)(2,1)S(1)}, bf16[3,40,256]{2,1,0:T(8,128)(2,1)S(1)}, /*index=5*/bf16[32,40,256]{2,1,0:T(8,128)(2,1)}, ...), branch_computations={%region_2.3_spmd, %region_3.4_spmd} | conditional | bytes 14680196 | solution.py:531
  91.5 53.9 %second_block.2 = bf16[1024,256]{1,0:T(8,128)(2,1)S(1)} custom-call(s32[1]{0:T(128)} %get-tuple-element.50.me_ref, f32[2,2,256]{2,1,0:T(2,128)S(1)} %get-tuple-element.51.gains, bf16[64,40,256]{2,1,0:T(8,128)(2,1)S(1)} %get-tuple-element.52.refs_0_, bf16[3,40,256]{2,1,0:T(8,128)(2,1)S(1)} %get-tuple-element.53.refs_1_, ...), custom_call_target="tpu_custom_call" | custom-call | tf_op jit(solution)/shard_map/cond/branch_0_fun/second_block/pallas_call | solution.py:505
  145.7 0.0 copy-start.5
  145.7 0.8 copy-done.5
Async XLA Ops:
  1.3 1.2 collective-permute-start.1
  56.2 35.1 %copy-start = (bf16[2,256,1024]{2,1,0:T(8,128)(2,1)S(1)}, bf16[2,256,1024]{2,1,0:T(8,128)(2,1)}, u32[]{:S(2)}) copy-start(bf16[2,256,1024]{2,1,0:T(8,128)(2,1)} %w_up.1) | copy-start | bytes 3145732
  56.2 35.1 %copy-start.1 = (bf16[2,1024,256]{2,1,0:T(8,128)(2,1)S(1)}, bf16[2,1024,256]{2,1,0:T(8,128)(2,1)}, u32[]{:S(2)}) copy-start(bf16[2,1024,256]{2,1,0:T(8,128)(2,1)} %w_down.1) | copy-start | bytes 3145732
  56.3 35.1 %copy-start.6 = (f32[2,2,256]{2,1,0:T(2,128)S(1)}, f32[2,2,256]{2,1,0:T(2,128)}, u32[]{:S(2)}) copy-start(f32[2,2,256]{2,1,0:T(2,128)} %gains.1) | copy-start | bytes 12292
  56.3 33.6 %all-to-all-start.1 = ((bf16[64,40,256]{2,1,0:T(8,128)(2,1)}), bf16[64,40,256]{2,1,0:T(8,128)(2,1)S(1)}, u32[]{:S(2)}, u32[]{:S(2)}) async-start(bf16[64,40,256]{2,1,0:T(8,128)(2,1)} %get-tuple-element.76), calls=%async_computation.1 | async-start | bytes 2621440 | tf_op jit(solution)/shard_map/all_to_all | solution.py:475
  67.9 23.4 %collective-permute-start.2 = (bf16[3,40,256]{2,1,0:T(8,128)(2,1)}, bf16[3,40,256]{2,1,0:T(8,128)(2,1)S(1)}, u32[]{:S(2)}, u32[]{:S(2)}) collective-permute-start(bf16[3,40,256]{2,1,0:T(8,128)(2,1)} %get-tuple-element.77), channel_id=1, source_target_pairs={{0,1},{1,2},{2,3},{3,4},{4,5},{5,6},{6,7},{7,8},{8,9},{9,10},{10,1... | collective-permute-start | bytes 184328 | tf_op jit(solution)/shard_map/ppermute | solution.py:500
  68.0 23.3 %collective-permute-start.3 = (bf16[3,40,256]{2,1,0:T(8,128)(2,1)}, bf16[3,40,256]{2,1,0:T(8,128)(2,1)S(1)}, u32[]{:S(2)}, u32[]{:S(2)}) collective-permute-start(bf16[3,40,256]{2,1,0:T(8,128)(2,1)} %get-tuple-element.78), channel_id=1, source_target_pairs={{0,127},{1,0},{2,1},{3,2},{4,3},{5,4},{6,5},{7,6},{8,7},{9,8},{10,... | collective-permute-start | bytes 184328 | tf_op jit(solution)/shard_map/ppermute | solution.py:501
  145.7 0.8 copy-start.5

commit v5 on v4

--- a/solution.py
+++ b/solution.py
@@ -1,4 +1,5 @@
 import functools
+import math
 
 import jax
 import jax.numpy as jnp
@@ -19,9 +20,11 @@
 NOTE = 8
 EPSILON = 1e-05
 QUERY_BLOCK = 256
-WINDOW = 512
-ROW_BLOCK = 256
+WINDOWS = (384, 512)
+ROW_BLOCK = 512
+MLP_BLOCK = 1024
 SPLIT_SCALE = 8.0
+EXPONENT_SCALE = 0.25 / SPLIT_SCALE**2 / math.log(2.0)
 SCORE_LIMIT = 40.0
 VALUE_LIMIT = 40.0
 BF16 = jnp.bfloat16
@@ -167,20 +170,29 @@
     ).astype(BF16)
 
 
-def attend_bounded(count, first_key, scenes, s):
+def attend_bounded(counts, choose, scenes, s):
     def block(index, carry):
-        queries = pl.ds(pl.multiple_of(index * QUERY_BLOCK, QUERY_BLOCK), QUERY_BLOCK)
-        start = first_key(index)
-        keys = pl.ds(start, count)
-        make_mask(start, count, index, scenes, s)
-        mask = s.mask[0:count]
-        for head in range(HEADS):
-            score = dot(s.key_split[head // 2, keys, :], s.query_split[head, :, queries])
-            weight = jnp.exp(score * (0.25 / SPLIT_SCALE**2)).astype(BF16) * mask
-            finish(head, queries, dot(s.value[head, :, keys], weight), s)
+        kind, start = choose(index)
+        for number, count in enumerate(counts):
+
+            @pl.when(kind == number)
+            def _(count=count):
+                attend_block(index, start, count, scenes, s)
+
         return carry
 
     lax.fori_loop(0, ROWS // QUERY_BLOCK, block, 0)
+
+
+def attend_block(index, start, count, scenes, s):
+    queries = pl.ds(pl.multiple_of(index * QUERY_BLOCK, QUERY_BLOCK), QUERY_BLOCK)
+    keys = pl.ds(start, count)
+    make_mask(start, count, index, scenes, s)
+    mask = s.mask[0:count]
+    for head in range(HEADS):
+        score = dot(s.key_split[head // 2, keys, :], s.query_split[head, :, queries])
+        weight = jnp.exp2(score * EXPONENT_SCALE).astype(BF16) * mask
+        finish(head, queries, dot(s.value[head, :, keys], weight), s)
 
 
 def attend_any(scenes, s):
@@ -221,6 +233,16 @@
 
 def neighbours(me):
     return lax.rem(me + 1, 128), lax.rem(me + 127, 128)
+
+
+def crossings(device, rank_ref):
+    above, below = neighbours(device)
+    flag = jnp.int32(0)
+    for tile in range(TILES):
+        owner = rank_ref[tile * TILE] >> 10
+        crosses = ((owner ^ device) & 1) * ((owner != above) & (owner != below)).astype(jnp.int32)
+        flag = flag | crosses
+    return flag
 
 
 def write_notes(scenes, flag, notes):
@@ -282,12 +304,14 @@
 
 
 def first_kernel(
-    me_ref, flag_ref, rank_ref, x, scenes, gains, w_qkv, w_proj, w_up, w_down,
+    me_ref, rank_ref, other_rank_ref, x, scenes, gains, w_qkv, w_proj, w_up, w_down,
     send, send_other, up, down, local, empty, result, fill_sem, *scratch,
 ):
     s = Scratch(scratch)
     copies = start_weights(0, (w_qkv, w_proj, w_up, w_down), s)
-    write_notes(scenes, flag_ref[0], Notes(empty, result))
+    me = me_ref[0]
+    flag = crossings(me, rank_ref) | crossings(me ^ 1, other_rank_ref)
+    write_notes(scenes, flag, Notes(empty, result))
     fills = []
     for index, target in enumerate((send, send_other, up, down, local)):
         count = target.shape[0]
@@ -304,7 +328,7 @@
 
     @pl.when(quick)
     def _():
-        attend_bounded(ROWS, lambda index: 0, scenes, s)
+        attend_bounded((ROWS,), lambda index: (0, 0), scenes, s)
 
     @pl.when(jnp.logical_not(quick))
     def _():
@@ -312,16 +336,15 @@
 
     for copy in copies[1:] + fills:
         copy.wait()
-    me = me_ref[0]
     above, below = neighbours(me)
     slots = (jnp.int32(0), jnp.int32(0))
-    for start in range(0, ROWS, ROW_BLOCK):
-        rows = mlp_rows(slice(start, start + ROW_BLOCK), x, gains[0, 1:2], s)
-        tiles = slice(start // TILE, (start + ROW_BLOCK) // TILE)
-        result[tiles, 0:TILE, :] = rows.reshape(ROW_BLOCK // TILE, TILE, C)
+    for start in range(0, ROWS, MLP_BLOCK):
+        rows = mlp_rows(slice(start, start + MLP_BLOCK), x, gains[0, 1:2], s)
+        tiles = slice(start // TILE, (start + MLP_BLOCK) // TILE)
+        result[tiles, 0:TILE, :] = rows.reshape(MLP_BLOCK // TILE, TILE, C)
 
         def one_tile(tile, slots):
-            owner = rank_ref[tile * TILE] // ROWS
+            owner = rank_ref[tile * TILE] >> 10
 
             def put(target, index):
                 pltpu.make_async_copy(result.at[tile], target.at[index], s.out_sem).start()
@@ -353,7 +376,7 @@
 
             return (slots[0] + is_up.astype(jnp.int32), slots[1] + is_down.astype(jnp.int32))
 
-        slots = lax.fori_loop(start // TILE, (start + ROW_BLOCK) // TILE, one_tile, slots)
+        slots = lax.fori_loop(start // TILE, (start + MLP_BLOCK) // TILE, one_tile, slots)
     pltpu.make_async_copy(result, local, s.out_sem).wait()
 
 
@@ -407,27 +430,32 @@
     bound, largest = project(x, gains[1, 0:1], s)
     quick = (bound <= SCORE_LIMIT) & (largest <= VALUE_LIMIT)
 
-    def window_start(index):
+    def window(index, count):
         first = plan[index * (QUERY_BLOCK // TILE), 0]
+        last = plan[(index + 1) * (QUERY_BLOCK // TILE) - 1, TILE - 1]
         start = jnp.int32(0)
-        for piece in range(1, (ROWS - WINDOW) // 128 + 1):
+        for piece in range(1, (ROWS - count) // 128 + 1):
             start = start + (plan[4 * piece - 1, TILE - 1] < first).astype(jnp.int32)
-        return pl.multiple_of(start * 128, 128)
+        end = start * 128 + count
+        fits = (end >= ROWS) | (plan[jnp.minimum(end // TILE, TILES - 1), 0] > last)
+        return pl.multiple_of(start * 128, 128), fits
+
+    def choose(index):
+        short, enough = window(index, WINDOWS[0])
+        wide, _ = window(index, WINDOWS[1])
+        return jnp.where(enough, 0, 1), pl.multiple_of(jnp.where(enough, short, wide), 128)
 
     fits = quick
     for index in range(ROWS // QUERY_BLOCK):
-        last = plan[(index + 1) * (QUERY_BLOCK // TILE) - 1, TILE - 1]
-        end = window_start(index) + WINDOW
-        after = plan[jnp.minimum(end // TILE, TILES - 1), 0]
-        fits = fits & ((end >= ROWS) | (after > last))
+        fits = fits & window(index, WINDOWS[1])[1]
 
     @pl.when(fits)
     def _():
-        attend_bounded(WINDOW, window_start, scenes, s)
+        attend_bounded(WINDOWS, choose, scenes, s)
 
     @pl.when(quick & jnp.logical_not(fits))
     def _():
-        attend_bounded(ROWS, lambda index: 0, scenes, s)
+        attend_bounded((ROWS,), lambda index: (0, 0), scenes, s)
 
     @pl.when(jnp.logical_not(quick))
     def _():
@@ -435,8 +463,8 @@
 
     for copy in copies[1:]:
         copy.wait()
-    for start in range(0, ROWS, ROW_BLOCK):
-        result[start : start + ROW_BLOCK] = mlp_rows(slice(start, start + ROW_BLOCK), x, gains[1, 1:2], s)
+    for start in range(0, ROWS, MLP_BLOCK):
+        result[start : start + MLP_BLOCK] = mlp_rows(slice(start, start + MLP_BLOCK), x, gains[1, 1:2], s)
 
         def one_tile(index, carry):
             source = result.at[pl.ds(pl.multiple_of(index * TILE, TILE), TILE)]
@@ -445,7 +473,7 @@
             pltpu.make_async_copy(source, target, s.out_sem).start()
             return carry
 
-        lax.fori_loop(start // TILE, (start + ROW_BLOCK) // TILE, one_tile, 0)
+        lax.fori_loop(start // TILE, (start + MLP_BLOCK) // TILE, one_tile, 0)
     pltpu.make_async_copy(result, out, s.out_sem).wait()
 
 
@@ -476,10 +504,7 @@
             array, "seq", split_axis=0, concat_axis=0, tiled=True, axis_index_groups=cores
         )
 
-    owner = hilbert_rank // ROWS
-    beside = (owner == (me + 1) % devices) | (owner == (me + devices - 1) % devices)
-    crosses = jnp.max(jnp.where(beside, 0, (owner ^ me) & 1)).reshape(1)
-    crosses = jnp.maximum(crosses, lax.ppermute(crosses, "seq", to_other))
+    other_rank = lax.ppermute(hilbert_rank, "seq", to_other)
 
     send, send_other, up, down, local = pl.pallas_call(
         first_kernel,
@@ -494,7 +519,7 @@
         + scratch_shapes(),
         compiler_params=params,
         name="first_block",
-    )(me_array, crosses, hilbert_rank, point_feats, scenes, norm_gains, *weights)
+    )(me_array, hilbert_rank, other_rank, point_feats, scenes, norm_gains, *weights)
 
     received = among_chips(send)
     from_below = lax.ppermute(up, "seq", to_above)
@@ -505,7 +530,7 @@
         return pl.pallas_call(
             functools.partial(second_kernel, sources=len(arrays)),
             in_specs=[SMEM, VMEM] + [HBM] * (len(arrays) + 4),
-            out_specs=HBM,
+            out_specs=pl.BlockSpec(memory_space=pltpu.HBM),
             out_shape=rows,
             scratch_shapes=[
                 pltpu.VMEM((ROWS, C), BF16),

time: 147 us -> 140 us (0.952)
  Pallas kernels: 106 us -> 102 us
    pallas_call x1, Pallas kernels: 52.4 us -> 50 us  [shards(): pl.pallas_call(first_kernel, in_specs=[SMEM, SMEM, SMEM, VMEM, VMEM, VMEM...]
    pallas_call x1, Pallas kernels: 53.9 us -> 51.5 us  [second(): pl.pallas_call(functools.partial(second_kernel, sources=len(arrays)), in_...]
where the time goes in v5:
time: 140 us
  Pallas kernels  102 us (73%)
  starting transfers between devices  18.9 us (13%)
  waiting for transfers between devices  16 us (11%)
    pallas_call x1, Pallas kernels, second(): pl.pallas_call(functools.partial(second_kernel, sources=len(arrays)), in_...  51.5 us
    pallas_call x1, Pallas kernels, shards(): pl.pallas_call(first_kernel, in_specs=[SMEM, SMEM, SMEM, VMEM, VMEM, VMEM...  50 us
    all_to_all x1, waiting for transfers between devices, among_chips(): lax.all_to_all(array, 'seq', split_axis=0, concat_axis=0, tiled=True, axi...  14.6 us
    all_to_all x1, starting transfers between devices, among_chips(): lax.all_to_all(array, 'seq', split_axis=0, concat_axis=0, tiled=True, axi...  11.6 us
    ppermute x1, starting transfers between devices, shards(): from_above = lax.ppermute(down, 'seq', to_below)  7.16 us
  transfers between devices with their start and end apart: 4, of which 2 were waited for; matrix products, arithmetic and copies ran while one was open for 1% of the time, Pallas kernels for 0%

profile of v5, /device:TPU:0, one launch (start us, length us, event | category | flops | bytes accessed | tf_op | source)
XLA Modules:
  0.0 139.8 jit_solution(11448239312781277706)
XLA Ops:
  0.0 0.0 collective-permute-start.1
  0.0 1.4 collective-permute-done.1.other_rank_ref
  1.4 0.0 copy-start.7
  1.4 0.6 copy-done.7
  2.0 50.0 %first_block.1 = (bf16[64,40,256]{2,1,0:T(8,128)(2,1)}, bf16[64,40,256]{2,1,0:T(8,128)(2,1)}, bf16[3,40,256]{2,1,0:T(8,128)(2,1)}, bf16[3,40,256]{2,1,0:T(8,128)(2,1)}, bf16[32,40,256]{2,1,0:T(8,128)(2,1)}) custom-call(s32[1]{0:T(128)} %bitcast.me_ref, s32[1024]{0:T(1024)} %rank_ref.1, s32[1024]{0:T(1024)} %copy-done.7, bf16[1024,256]{1,0:T(8,128)(2,1)} %x.1, ...), custom_call_target="tpu_custom_call" | custom-call | tf_op jit(solution)/shard_map/first_block/pallas_call | solution.py:509
  52.0 0.0 copy-start
  52.0 0.0 copy-start.1
  52.0 0.0 copy-start.6
  52.0 11.6 %all-to-all-start.1 = ((bf16[64,40,256]{2,1,0:T(8,128)(2,1)}), bf16[64,40,256]{2,1,0:T(8,128)(2,1)S(1)}, u32[]{:S(2)}, u32[]{:S(2)}) async-start(bf16[64,40,256]{2,1,0:T(8,128)(2,1)} %get-tuple-element.76), calls=%async_computation.1 | async-start | bytes 2621440 | tf_op jit(solution)/shard_map/all_to_all | solution.py:503
  63.7 0.1 collective-permute-start.2
  63.7 7.2 %collective-permute-start.3 = (bf16[3,40,256]{2,1,0:T(8,128)(2,1)}, bf16[3,40,256]{2,1,0:T(8,128)(2,1)S(1)}, u32[]{:S(2)}, u32[]{:S(2)}) collective-permute-start(bf16[3,40,256]{2,1,0:T(8,128)(2,1)} %get-tuple-element.78), channel_id=1, source_target_pairs={{0,127},{1,0},{2,1},{3,2},{4,3},{5,4},{6,5},{7,6},{8,7},{9,8},{10,... | collective-permute-start | bytes 184328 | tf_op jit(solution)/shard_map/ppermute | solution.py:526
  70.9 14.6 %all-to-all-done.1 = bf16[64,40,256]{2,1,0:T(8,128)(2,1)S(1)} async-done(((bf16[64,40,256]{2,1,0:T(8,128)(2,1)}), bf16[64,40,256]{2,1,0:T(8,128)(2,1)S(1)}, u32[]{:S(2)}, u32[]{:S(2)}) %all-to-all-start.1) | async-done | bytes 1310752 | tf_op jit(solution)/shard_map/all_to_all | solution.py:503
  85.5 0.8 slice_reduce_fusion
  86.9 0.0 collective-permute-done.2
  86.9 0.0 collective-permute-done.3
  87.0 0.0 copy-done
  87.0 0.0 copy-done.1
  87.0 0.0 copy-done.6
  87.0 52.0 %conditional.1 = (bf16[1024,256]{1,0:T(8,128)(2,1)S(1)}) conditional(s32[]{:T(128)} %convert_element_type.3, (s32[1]{0:T(128)}, f32[2,2,256]{2,1,0:T(2,128)S(1)}, bf16[64,40,256]{2,1,0:T(8,128)(2,1)S(1)}, bf16[3,40,256]{2,1,0:T(8,128)(2,1)S(1)}, bf16[3,40,256]{2,1,0:T(8,128)(2,1)S(1)}, /*index=5*/bf16[32,40,256]{2,1,0:T(8,128)(2,1)}, ...), branch_computations={%region_1.0_spmd, %region_2.0_spmd} | conditional | bytes 14680196 | solution.py:556
  87.2 51.5 %second_block.2 = bf16[1024,256]{1,0:T(8,128)(2,1)S(1)} custom-call(s32[1]{0:T(128)} %get-tuple-element.50.me_ref, f32[2,2,256]{2,1,0:T(2,128)S(1)} %get-tuple-element.51.gains, bf16[64,40,256]{2,1,0:T(8,128)(2,1)S(1)} %get-tuple-element.52.refs_0_, bf16[3,40,256]{2,1,0:T(8,128)(2,1)S(1)} %get-tuple-element.53.refs_1_, ...), custom_call_target="tpu_custom_call" | custom-call | tf_op jit(solution)/shard_map/cond/branch_0_fun/second_block/pallas_call | solution.py:530
  139.0 0.0 copy-start.5
  139.0 0.8 copy-done.5
Async XLA Ops:
  0.0 1.4 collective-permute-start.1
  1.4 0.6 copy-start.7
  52.0 35.0 %copy-start = (bf16[2,256,1024]{2,1,0:T(8,128)(2,1)S(1)}, bf16[2,256,1024]{2,1,0:T(8,128)(2,1)}, u32[]{:S(2)}) copy-start(bf16[2,256,1024]{2,1,0:T(8,128)(2,1)} %w_up.1) | copy-start | bytes 3145732
  52.0 35.0 %copy-start.1 = (bf16[2,1024,256]{2,1,0:T(8,128)(2,1)S(1)}, bf16[2,1024,256]{2,1,0:T(8,128)(2,1)}, u32[]{:S(2)}) copy-start(bf16[2,1024,256]{2,1,0:T(8,128)(2,1)} %w_down.1) | copy-start | bytes 3145732
  52.0 35.0 %copy-start.6 = (f32[2,2,256]{2,1,0:T(2,128)S(1)}, f32[2,2,256]{2,1,0:T(2,128)}, u32[]{:S(2)}) copy-start(f32[2,2,256]{2,1,0:T(2,128)} %gains.1) | copy-start | bytes 12292
  52.0 33.5 %all-to-all-start.1 = ((bf16[64,40,256]{2,1,0:T(8,128)(2,1)}), bf16[64,40,256]{2,1,0:T(8,128)(2,1)S(1)}, u32[]{:S(2)}, u32[]{:S(2)}) async-start(bf16[64,40,256]{2,1,0:T(8,128)(2,1)} %get-tuple-element.76), calls=%async_computation.1 | async-start | bytes 2621440 | tf_op jit(solution)/shard_map/all_to_all | solution.py:503
  63.7 23.3 %collective-permute-start.2 = (bf16[3,40,256]{2,1,0:T(8,128)(2,1)}, bf16[3,40,256]{2,1,0:T(8,128)(2,1)S(1)}, u32[]{:S(2)}, u32[]{:S(2)}) collective-permute-start(bf16[3,40,256]{2,1,0:T(8,128)(2,1)} %get-tuple-element.77), channel_id=1, source_target_pairs={{0,1},{1,2},{2,3},{3,4},{4,5},{5,6},{6,7},{7,8},{8,9},{9,10},{10,1... | collective-permute-start | bytes 184328 | tf_op jit(solution)/shard_map/ppermute | solution.py:525
  63.7 23.2 %collective-permute-start.3 = (bf16[3,40,256]{2,1,0:T(8,128)(2,1)}, bf16[3,40,256]{2,1,0:T(8,128)(2,1)S(1)}, u32[]{:S(2)}, u32[]{:S(2)}) collective-permute-start(bf16[3,40,256]{2,1,0:T(8,128)(2,1)} %get-tuple-element.78), channel_id=1, source_target_pairs={{0,127},{1,0},{2,1},{3,2},{4,3},{5,4},{6,5},{7,6},{8,7},{9,8},{10,... | collective-permute-start | bytes 184328 | tf_op jit(solution)/shard_map/ppermute | solution.py:526
  139.0 0.8 copy-start.5

commit v6 on v5

--- a/solution.py
+++ b/solution.py
@@ -87,25 +87,23 @@
     ]
 
 
-def start_weights(block, weights, s):
+def start_weights(block, weights, targets, s):
     copies = [
         pltpu.make_async_copy(source.at[block], target, s.sems.at[i])
-        for i, (source, target) in enumerate(
-            zip(weights, (s.w_qkv, s.w_proj, s.w_up, s.w_down), strict=True)
-        )
+        for i, (source, target) in enumerate(zip(weights, targets, strict=True))
     ]
     for copy in copies:
         copy.start()
     return copies
 
 
-def project(x, gain, s):
+def project(x, gain, w_qkv, s):
     for start in range(0, ROWS, ROW_BLOCK):
         rows = slice(start, start + ROW_BLOCK)
         s.normed[rows] = layer_norm(x[rows].astype(F32), gain)
     normed = s.normed[...]
-    query = dot(s.w_qkv[:, 0:C], normed, 0, 1).astype(BF16)
-    value = dot(s.w_qkv[:, 2 * C : 3 * C], normed, 0, 1).astype(BF16)
+    query = dot(w_qkv[:, 0:C], normed, 0, 1).astype(BF16)
+    value = dot(w_qkv[:, 2 * C : 3 * C], normed, 0, 1).astype(BF16)
     for head in range(HEADS):
         s.value[head, 0:HEAD, :] = value[HEAD * head : HEAD * (head + 1)]
         s.value[head, HEAD:, :] = jnp.ones((HEAD, ROWS), BF16)
@@ -136,7 +134,7 @@
     key_high = jnp.zeros((1, C), F32)
     for start in range(0, ROWS, ROW_BLOCK):
         rows = slice(start, start + ROW_BLOCK)
-        key = dot(s.normed[rows], s.w_qkv[:, C : 2 * C]).astype(BF16)
+        key = dot(s.normed[rows], w_qkv[:, C : 2 * C]).astype(BF16)
         s.key[0, rows] = key[:, 0:128]
         s.key[1, rows] = key[:, 128:256]
         wide = key.astype(F32)
@@ -304,14 +302,13 @@
 
 
 def first_kernel(
-    me_ref, rank_ref, other_rank_ref, x, scenes, gains, w_qkv, w_proj, w_up, w_down,
+    me_ref, rank_ref, x, scenes, gains, w_qkv, w_proj, w_up, w_down,
     send, send_other, up, down, local, empty, result, fill_sem, *scratch,
 ):
     s = Scratch(scratch)
-    copies = start_weights(0, (w_qkv, w_proj, w_up, w_down), s)
+    copies = start_weights(0, (w_proj, w_up, w_down), (s.w_proj, s.w_up, s.w_down), s)
     me = me_ref[0]
-    flag = crossings(me, rank_ref) | crossings(me ^ 1, other_rank_ref)
-    write_notes(scenes, flag, Notes(empty, result))
+    write_notes(scenes, crossings(me, rank_ref), Notes(empty, result))
     fills = []
     for index, target in enumerate((send, send_other, up, down, local)):
         count = target.shape[0]
@@ -322,8 +319,7 @@
         )
         fills[-1].start()
     scene_columns(scenes, s)
-    copies[0].wait()
-    bound, largest = project(x, gains[0, 0:1], s)
+    bound, largest = project(x, gains[0, 0:1], w_qkv.at[0], s)
     quick = (bound <= SCORE_LIMIT) & (largest <= VALUE_LIMIT)
 
     @pl.when(quick)
@@ -334,7 +330,7 @@
     def _():
         attend_any(scenes, s)
 
-    for copy in copies[1:] + fills:
+    for copy in copies + fills:
         copy.wait()
     above, below = neighbours(me)
     slots = (jnp.int32(0), jnp.int32(0))
@@ -402,7 +398,9 @@
         )
         fetches[-1].start()
         start += count
-    copies = start_weights(1, (w_qkv, w_proj, w_up, w_down), s)
+    copies = start_weights(
+        1, (w_qkv, w_proj, w_up, w_down), (s.w_qkv, s.w_proj, s.w_up, s.w_down), s
+    )
     for fetch in fetches:
         fetch.wait()
     ends = starts[1:] + [start]
@@ -427,7 +425,7 @@
     scene_columns(scenes, s)
     pltpu.make_async_copy(result, x, in_sem).wait()
     copies[0].wait()
-    bound, largest = project(x, gains[1, 0:1], s)
+    bound, largest = project(x, gains[1, 0:1], s.w_qkv, s)
     quick = (bound <= SCORE_LIMIT) & (largest <= VALUE_LIMIT)
 
     def window(index, count):
@@ -504,11 +502,9 @@
             array, "seq", split_axis=0, concat_axis=0, tiled=True, axis_index_groups=cores
         )
 
-    other_rank = lax.ppermute(hilbert_rank, "seq", to_other)
-
     send, send_other, up, down, local = pl.pallas_call(
         first_kernel,
-        in_specs=[SMEM, SMEM, SMEM, VMEM, VMEM, VMEM, HBM, HBM, HBM, HBM],
+        in_specs=[SMEM, SMEM, VMEM, VMEM, VMEM, VMEM, HBM, HBM, HBM],
         out_specs=[HBM] * 5,
         out_shape=[bins, bins, few, few, own],
         scratch_shapes=[
@@ -519,7 +515,7 @@
         + scratch_shapes(),
         compiler_params=params,
         name="first_block",
-    )(me_array, hilbert_rank, other_rank, point_feats, scenes, norm_gains, *weights)
+    )(me_array, hilbert_rank, point_feats, scenes, norm_gains, *weights)
 
     received = among_chips(send)
     from_below = lax.ppermute(up, "seq", to_above)
@@ -530,8 +526,8 @@
         return pl.pallas_call(
             functools.partial(second_kernel, sources=len(arrays)),
             in_specs=[SMEM, VMEM] + [HBM] * (len(arrays) + 4),
-            out_specs=pl.BlockSpec(memory_space=pltpu.HBM),
-            out_shape=rows,
+            out_specs=HBM,
+            out_shape=pltpu.HBM((ROWS, C), BF16),
             scratch_shapes=[
                 pltpu.VMEM((ROWS, C), BF16),
                 pltpu.VMEM((noted, NOTE, 128), BF16),
@@ -547,15 +543,19 @@
             name="second_block",
         )(me_array, norm_gains, *arrays, *weights)
 
-    def with_crossing(tiles, received, *rest):
+    crossing = jnp.max(received[:, TILE, TILE + 1].astype(jnp.int32)).reshape(1)
+    crossing_other = lax.ppermute(crossing, "seq", to_other)
+    out = second(received, from_below, from_above, local)
+
+    def with_crossing(out, tiles, received, *rest):
         return second(received, among_chips(lax.ppermute(tiles, "seq", to_other)), *rest)
 
-    def without_crossing(tiles, received, *rest):
-        return second(received, *rest)
+    def without_crossing(out, *rest):
+        return out
 
     return lax.cond(
-        jnp.max(received[:, TILE, TILE + 1]) > 0, with_crossing, without_crossing,
-        send_other, received, from_below, from_above, local,
+        jnp.maximum(crossing, crossing_other)[0] > 0, with_crossing, without_crossing,
+        out, send_other, received, from_below, from_above, local,
     )
 
 

time: 140 us -> 138 us (0.986)
  waiting for transfers between devices: 16 us -> 14.4 us
  transfers between devices with their start and end apart: 4 -> 4, of which waited for: 2 -> 1; matrix products, arithmetic and copies ran while one was open for 1% -> 1% of each run, Pallas kernels for 0% -> 38%
where the time goes in v6:
time: 138 us; the launch traced here: 136 us
  Pallas kernels  101 us (73%)
  starting transfers between devices  18.9 us (14%)
  waiting for transfers between devices  14.4 us (10%)
  between operations  1.44 us (1%)
    pallas_call x1, Pallas kernels, second(): pl.pallas_call(functools.partial(second_kernel, sources=len(arrays)), in_...  51.5 us
    pallas_call x1, Pallas kernels, shards(): pl.pallas_call(first_kernel, in_specs=[SMEM, SMEM, VMEM, VMEM, VMEM, VMEM...  49.3 us
    all_to_all x1, waiting for transfers between devices, among_chips(): lax.all_to_all(array, 'seq', split_axis=0, concat_axis=0, tiled=True, axi...  14.4 us
    all_to_all x1, starting transfers between devices, among_chips(): lax.all_to_all(array, 'seq', split_axis=0, concat_axis=0, tiled=True, axi...  11.6 us
    ppermute x1, starting transfers between devices, shards(): from_above = lax.ppermute(down, 'seq', to_below)  7.16 us
  transfers between devices with their start and end apart: 4, of which 1 were waited for; matrix products, arithmetic and copies ran while one was open for 1% of the time, Pallas kernels for 38%

profile of v6, /device:TPU:0, one launch (start us, length us, event | category | flops | bytes accessed | tf_op | source)
XLA Modules:
  0.0 136.4 jit_solution(8095978319539825868)
XLA Ops:
  0.0 49.3 %first_block.1 = (bf16[64,40,256]{2,1,0:T(8,128)(2,1)}, bf16[64,40,256]{2,1,0:T(8,128)(2,1)}, bf16[3,40,256]{2,1,0:T(8,128)(2,1)}, bf16[3,40,256]{2,1,0:T(8,128)(2,1)}, bf16[32,40,256]{2,1,0:T(8,128)(2,1)}) custom-call(s32[1]{0:T(128)} %bitcast.me_ref, s32[1024]{0:T(1024)} %rank_ref.1, bf16[1024,256]{1,0:T(8,128)(2,1)} %x.1, s32[8,128]{1,0:T(8,128)} %bitcast.4, ...), custom_call_target="tpu_custom_call" | custom-call | tf_op jit(solution)/shard_map/first_block/pallas_call | solution.py:505
  49.3 0.0 copy-start
  49.3 0.0 copy-start.1
  49.3 0.0 copy-start.5
  49.4 11.6 %all-to-all-start.1 = ((bf16[64,40,256]{2,1,0:T(8,128)(2,1)}), bf16[64,40,256]{2,1,0:T(8,128)(2,1)S(1)}, u32[]{:S(2)}, u32[]{:S(2)}) async-start(bf16[64,40,256]{2,1,0:T(8,128)(2,1)} %get-tuple-element.47), calls=%async_computation.1 | async-start | bytes 2621440 | tf_op jit(solution)/shard_map/all_to_all | solution.py:501
  61.0 0.1 collective-permute-start.2
  61.1 7.2 %collective-permute-start.3 = (bf16[3,40,256]{2,1,0:T(8,128)(2,1)}, bf16[3,40,256]{2,1,0:T(8,128)(2,1)S(1)}, u32[]{:S(2)}, u32[]{:S(2)}) collective-permute-start(bf16[3,40,256]{2,1,0:T(8,128)(2,1)} %get-tuple-element.49), channel_id=1, source_target_pairs={{0,127},{1,0},{2,1},{3,2},{4,3},{5,4},{6,5},{7,6},{8,7},{9,8},{10,... | collective-permute-start | bytes 184328 | tf_op jit(solution)/shard_map/ppermute | solution.py:522
  68.2 14.4 %all-to-all-done.1.refs_0_ = bf16[64,40,256]{2,1,0:T(8,128)(2,1)S(1)} async-done(((bf16[64,40,256]{2,1,0:T(8,128)(2,1)}), bf16[64,40,256]{2,1,0:T(8,128)(2,1)S(1)}, u32[]{:S(2)}, u32[]{:S(2)}) %all-to-all-start.1) | async-done | bytes 1310752 | tf_op jit(solution)/shard_map/all_to_all | solution.py:501
  82.6 0.8 fusion
  83.4 0.0 collective-permute-start.1
  83.4 0.0 collective-permute-done.2.refs_1_
  83.4 0.0 collective-permute-done.3.refs_2_
  83.4 0.0 copy-done
  83.4 0.0 copy-done.1
  83.5 0.0 copy-done.5
  83.5 0.0 copy-start.2
  83.5 0.0 copy-start.3
  83.5 0.0 copy-start.4
  83.5 0.0 copy-start.6
  83.5 51.5 %second_block.3 = bf16[1024,256]{1,0:T(8,128)(2,1)} custom-call(s32[1]{0:T(128)} %bitcast.me_ref, f32[2,2,256]{2,1,0:T(2,128)S(1)} %copy-done.5, bf16[64,40,256]{2,1,0:T(8,128)(2,1)S(1)} %all-to-all-done.1.refs_0_, bf16[3,40,256]{2,1,0:T(8,128)(2,1)S(1)} %collective-permute-done.2.refs_1_, bf16[3,40,256]{2,1,0:T(8,128)(2,1)S(1)} %collective-permute-done.3.refs_2_, ...), custom_call_target="tpu_custom_call" | custom-call | tf_op jit(solution)/shard_map/second_block/pallas_call | solution.py:526
  135.1 0.0 collective-permute-done.1
  136.2 0.0 copy-done.2
  136.2 0.0 copy-done.3
  136.2 0.0 copy-done.4
  136.2 0.0 copy-done.6
  (1 shorter events, 0.0 us)
Async XLA Ops:
  49.3 34.1 %copy-start = (bf16[2,256,1024]{2,1,0:T(8,128)(2,1)S(1)}, bf16[2,256,1024]{2,1,0:T(8,128)(2,1)}, u32[]{:S(2)}) copy-start(bf16[2,256,1024]{2,1,0:T(8,128)(2,1)} %refs_6_.1) | copy-start | bytes 3145732
  49.3 34.1 %copy-start.1 = (bf16[2,1024,256]{2,1,0:T(8,128)(2,1)S(1)}, bf16[2,1024,256]{2,1,0:T(8,128)(2,1)}, u32[]{:S(2)}) copy-start(bf16[2,1024,256]{2,1,0:T(8,128)(2,1)} %refs_7_.1) | copy-start | bytes 3145732
  49.3 34.1 %copy-start.5 = (f32[2,2,256]{2,1,0:T(2,128)S(1)}, f32[2,2,256]{2,1,0:T(2,128)}, u32[]{:S(2)}) copy-start(f32[2,2,256]{2,1,0:T(2,128)} %gains.3) | copy-start | bytes 12292
  49.4 33.3 %all-to-all-start.1 = ((bf16[64,40,256]{2,1,0:T(8,128)(2,1)}), bf16[64,40,256]{2,1,0:T(8,128)(2,1)S(1)}, u32[]{:S(2)}, u32[]{:S(2)}) async-start(bf16[64,40,256]{2,1,0:T(8,128)(2,1)} %get-tuple-element.47), calls=%async_computation.1 | async-start | bytes 2621440 | tf_op jit(solution)/shard_map/all_to_all | solution.py:501
  61.0 22.4 %collective-permute-start.2 = (bf16[3,40,256]{2,1,0:T(8,128)(2,1)}, bf16[3,40,256]{2,1,0:T(8,128)(2,1)S(1)}, u32[]{:S(2)}, u32[]{:S(2)}) collective-permute-start(bf16[3,40,256]{2,1,0:T(8,128)(2,1)} %get-tuple-element.48), channel_id=1, source_target_pairs={{0,1},{1,2},{2,3},{3,4},{4,5},{5,6},{6,7},{7,8},{8,9},{9,10},{10,1... | collective-permute-start | bytes 184328 | tf_op jit(solution)/shard_map/ppermute | solution.py:521
  61.1 22.3 %collective-permute-start.3 = (bf16[3,40,256]{2,1,0:T(8,128)(2,1)}, bf16[3,40,256]{2,1,0:T(8,128)(2,1)S(1)}, u32[]{:S(2)}, u32[]{:S(2)}) collective-permute-start(bf16[3,40,256]{2,1,0:T(8,128)(2,1)} %get-tuple-element.49), channel_id=1, source_target_pairs={{0,127},{1,0},{2,1},{3,2},{4,3},{5,4},{6,5},{7,6},{8,7},{9,8},{10,... | collective-permute-start | bytes 184328 | tf_op jit(solution)/shard_map/ppermute | solution.py:522
  83.4 51.6 %collective-permute-start.1 = (s32[1]{0:T(128)}, s32[1]{0:T(128)}, u32[]{:S(2)}, u32[]{:S(2)}) collective-permute-start(s32[1]{0:T(128)} %bitcast.2), channel_id=1, source_target_pairs={{0,1},{1,0},{2,3},{3,2},{4,5},{5,4},{6,7},{7,6},{8,9},{9,8},{10,11... | collective-permute-start | bytes 20 | tf_op jit(solution)/shard_map/ppermute | solution.py:547
  83.5 52.7 %copy-start.2 = (bf16[2,256,768]{2,1,0:T(8,128)(2,1)S(1)}, bf16[2,256,768]{2,1,0:T(8,128)(2,1)}, u32[]{:S(2)}) copy-start(bf16[2,256,768]{2,1,0:T(8,128)(2,1)} %refs_4_.1) | copy-start | bytes 2359300
  83.5 52.7 %copy-start.3 = (bf16[32,40,256]{2,1,0:T(8,128)(2,1)S(1)}, bf16[32,40,256]{2,1,0:T(8,128)(2,1)}, u32[]{:S(2)}) copy-start(bf16[32,40,256]{2,1,0:T(8,128)(2,1)} %get-tuple-element.50.refs_3_) | copy-start | bytes 1966084
  83.5 52.7 %copy-start.4 = (bf16[2,256,256]{2,1,0:T(8,128)(2,1)S(1)}, bf16[2,256,256]{2,1,0:T(8,128)(2,1)}, u32[]{:S(2)}) copy-start(bf16[2,256,256]{2,1,0:T(8,128)(2,1)} %refs_5_.1) | copy-start | bytes 786436
  83.5 52.7 %copy-start.6 = (bf16[64,40,256]{2,1,0:T(8,128)(2,1)S(1)}, bf16[64,40,256]{2,1,0:T(8,128)(2,1)}, u32[]{:S(2)}) copy-start(bf16[64,40,256]{2,1,0:T(8,128)(2,1)} %get-tuple-element.51) | copy-start | bytes 3932164

commit v7 on v6

--- a/solution.py
+++ b/solution.py
@@ -17,7 +17,10 @@
 TILE = 32
 MOST_TILES = 3
 CHIPS = 64
-NOTE = 8
+GROUPS = 4
+GROUP_ROWS = TILE // GROUPS
+NOTE = GROUPS * C
+LANES = NOTE + 128
 EPSILON = 1e-05
 QUERY_BLOCK = 256
 WINDOWS = (384, 512)
@@ -226,7 +229,7 @@
     middle = (x[rows].astype(F32) + dot(attended, s.w_proj[...])).astype(BF16)
     normed = layer_norm(middle.astype(F32), gain)
     hidden = gelu(dot(normed, s.w_up[...])).astype(BF16)
-    return (middle.astype(F32) + dot(hidden, s.w_down[...])).astype(BF16)
+    return middle.astype(F32) + dot(hidden, s.w_down[...])
 
 
 def neighbours(me):
@@ -246,24 +249,21 @@
 def write_notes(scenes, flag, notes):
     lane = lax.broadcasted_iota(jnp.int32, (1, 128), 1)
     flags = jnp.where(lane == TILE + 1, flag, 0)
-    empty = jnp.broadcast_to(flags, (NOTE, 128)).astype(F32).astype(BF16)
-    notes.empty[:, :, 0:128] = jnp.broadcast_to(empty[None], (CHIPS, NOTE, 128))
-    notes.empty[:, :, 128:256] = jnp.zeros((CHIPS, NOTE, 128), BF16)
+    notes.empty[...] = jnp.broadcast_to(flags, notes.empty.shape).astype(F32).astype(BF16)
     for tile in range(TILES):
         row = scenes[tile // 4 : tile // 4 + 1, (tile % 4) * TILE : (tile % 4 + 1) * TILE]
         row = jnp.concatenate([row] * 4, axis=1)
         row = jnp.where(lane < TILE, row, jnp.where(lane == TILE, tile + 1, flags))
-        row = jnp.broadcast_to(row, (NOTE, 128)).astype(F32).astype(BF16)
-        notes.result[tile, TILE:, 0:128] = row
-        notes.result[tile, TILE:, 128:256] = jnp.zeros((NOTE, 128), BF16)
-
-
-def sort_tiles(me, entries, plan_out, scene_out):
+        row = jnp.broadcast_to(row, (GROUP_ROWS, 128)).astype(F32).astype(BF16)
+        notes.result[tile, :, NOTE:LANES] = row
+
+
+def sort_tiles(entries, plan_out, scene_out):
     count = sum(notes.shape[0] for notes, _, _ in entries)
     total = -(-count // 128) * 128
     tables, sources = [], []
     for notes, first, step in entries:
-        tables.append(notes[:, 0:1, :].astype(F32).reshape(notes.shape[0], 128))
+        tables.append(notes[:, 0:1, NOTE:LANES].astype(F32).reshape(notes.shape[0], 128))
         index = lax.broadcasted_iota(jnp.int32, (notes.shape[0], 1), 0)
         sources.append(first + step * index)
     if total > count:
@@ -314,7 +314,7 @@
         count = target.shape[0]
         fills.append(
             pltpu.make_async_copy(
-                empty.at[0:count], target.at[:, TILE : TILE + NOTE], fill_sem.at[index]
+                empty.at[0:count], target.at[:, :, NOTE:LANES], fill_sem.at[index]
             )
         )
         fills[-1].start()
@@ -337,7 +337,9 @@
     for start in range(0, ROWS, MLP_BLOCK):
         rows = mlp_rows(slice(start, start + MLP_BLOCK), x, gains[0, 1:2], s)
         tiles = slice(start // TILE, (start + MLP_BLOCK) // TILE)
-        result[tiles, 0:TILE, :] = rows.reshape(MLP_BLOCK // TILE, TILE, C)
+        rows = rows.reshape(MLP_BLOCK // TILE, GROUPS, GROUP_ROWS, C)
+        for group in range(GROUPS):
+            result[tiles, :, C * group : C * (group + 1)] = rows[:, group].astype(BF16)
 
         def one_tile(tile, slots):
             owner = rank_ref[tile * TILE] >> 10
@@ -380,50 +382,38 @@
     me_ref, gains, *refs, sources,
 ):
     arrays, refs = refs[:sources], refs[sources:]
-    w_qkv, w_proj, w_up, w_down, out, x, notes, plan_vmem, scenes, result, plan, note_sems, in_sem = refs[:13]
-    s = Scratch(refs[13:])
+    w_qkv, w_proj, w_up, w_down, out, x, plan_vmem, scenes, result, plan, plan_sem = refs[:11]
+    s = Scratch(refs[11:])
     me = me_ref[0]
     core = lax.rem(me, 2)
     above, below = neighbours(me)
     firsts = ((core, 2), (1 - core, 2))[: sources - 3] + ((below, 0), (above, 0), (me, 0))
-    starts, fetches = [], []
-    start = 0
-    for index, array in enumerate(arrays):
-        count = array.shape[0]
-        starts.append(start)
-        fetches.append(
-            pltpu.make_async_copy(
-                array.at[:, TILE : TILE + NOTE, 0:128], notes.at[start : start + count], note_sems.at[index]
-            )
-        )
-        fetches[-1].start()
-        start += count
     copies = start_weights(
         1, (w_qkv, w_proj, w_up, w_down), (s.w_qkv, s.w_proj, s.w_up, s.w_down), s
     )
-    for fetch in fetches:
-        fetch.wait()
-    ends = starts[1:] + [start]
-    entries = [(notes[a:b], *first) for a, b, first in zip(starts, ends, firsts, strict=True)]
-    sort_tiles(me, entries, plan_vmem, scenes)
-    to_scalars = pltpu.make_async_copy(plan_vmem, plan, note_sems.at[0])
+    entries = [(array, *first) for array, first in zip(arrays, firsts, strict=True)]
+    sort_tiles(entries, plan_vmem, scenes)
+    to_scalars = pltpu.make_async_copy(plan_vmem, plan, plan_sem)
     to_scalars.start()
+    scene_columns(scenes, s)
     to_scalars.wait()
 
     def fetch(index, carry):
         entry = plan[index, TILE + 2] + 128 * plan[index, TILE + 3]
-        target = x.at[pl.ds(pl.multiple_of(index * TILE, TILE), TILE)]
-        for array, first, end in zip(arrays, starts, ends, strict=True):
+        first = 0
+        for array in arrays:
+            end = first + array.shape[0]
 
             @pl.when((entry >= first) & (entry < end))
             def _(array=array, first=first):
-                pltpu.make_async_copy(array.at[entry - first, 0:TILE], target, in_sem).start()
-
+                for group in range(GROUPS):
+                    target = pl.ds(pl.multiple_of(index * TILE + group * GROUP_ROWS, GROUP_ROWS), GROUP_ROWS)
+                    x[target, :] = array[entry - first, :, C * group : C * (group + 1)].astype(F32)
+
+            first = end
         return carry
 
     lax.fori_loop(0, TILES, fetch, 0)
-    scene_columns(scenes, s)
-    pltpu.make_async_copy(result, x, in_sem).wait()
     copies[0].wait()
     bound, largest = project(x, gains[1, 0:1], s.w_qkv, s)
     quick = (bound <= SCORE_LIMIT) & (largest <= VALUE_LIMIT)
@@ -462,7 +452,8 @@
     for copy in copies[1:]:
         copy.wait()
     for start in range(0, ROWS, MLP_BLOCK):
-        result[start : start + MLP_BLOCK] = mlp_rows(slice(start, start + MLP_BLOCK), x, gains[1, 1:2], s)
+        rows = mlp_rows(slice(start, start + MLP_BLOCK), x, gains[1, 1:2], s)
+        result[start : start + MLP_BLOCK] = rows.astype(BF16)
 
         def one_tile(index, carry):
             source = result.at[pl.ds(pl.multiple_of(index * TILE, TILE), TILE)]
@@ -488,9 +479,9 @@
     scenes = scene_id.reshape(ROWS // 128, 128)
     params = pltpu.CompilerParams(vmem_limit_bytes=VMEM_BYTES)
     rows = jax.ShapeDtypeStruct((ROWS, C), BF16)
-    few = jax.ShapeDtypeStruct((MOST_TILES, TILE + NOTE, C), BF16)
-    bins = jax.ShapeDtypeStruct((CHIPS, TILE + NOTE, C), BF16)
-    own = jax.ShapeDtypeStruct((TILES, TILE + NOTE, C), BF16)
+    few = jax.ShapeDtypeStruct((MOST_TILES, GROUP_ROWS, LANES), BF16)
+    bins = jax.ShapeDtypeStruct((CHIPS, GROUP_ROWS, LANES), BF16)
+    own = jax.ShapeDtypeStruct((TILES, GROUP_ROWS, LANES), BF16)
     ring = range(devices)
     to_above = [(i, (i + 1) % devices) for i in ring]
     to_below = [(i, (i - 1) % devices) for i in ring]
@@ -508,8 +499,8 @@
         out_specs=[HBM] * 5,
         out_shape=[bins, bins, few, few, own],
         scratch_shapes=[
-            pltpu.VMEM((CHIPS, NOTE, C), BF16),
-            pltpu.VMEM((TILES, TILE + NOTE, C), BF16),
+            pltpu.VMEM((CHIPS, GROUP_ROWS, 128), BF16),
+            pltpu.VMEM((TILES, GROUP_ROWS, LANES), BF16),
             pltpu.SemaphoreType.DMA((5,)),
         ]
         + scratch_shapes(),
@@ -522,20 +513,17 @@
     from_above = lax.ppermute(down, "seq", to_below)
 
     def second(*arrays):
-        noted = sum(array.shape[0] for array in arrays)
         return pl.pallas_call(
             functools.partial(second_kernel, sources=len(arrays)),
-            in_specs=[SMEM, VMEM] + [HBM] * (len(arrays) + 4),
+            in_specs=[SMEM, VMEM] + [VMEM] * len(arrays) + [HBM] * 4,
             out_specs=HBM,
             out_shape=pltpu.HBM((ROWS, C), BF16),
             scratch_shapes=[
-                pltpu.VMEM((ROWS, C), BF16),
-                pltpu.VMEM((noted, NOTE, 128), BF16),
+                pltpu.VMEM((ROWS, C), F32),
                 pltpu.VMEM((TILES, 128), jnp.int32),
                 pltpu.VMEM((ROWS // 128, 128), jnp.int32),
                 pltpu.VMEM((ROWS, C), BF16),
                 pltpu.SMEM((TILES, 128), jnp.int32),
-                pltpu.SemaphoreType.DMA((5,)),
                 pltpu.SemaphoreType.DMA,
             ]
             + scratch_shapes(),
@@ -543,7 +531,7 @@
             name="second_block",
         )(me_array, norm_gains, *arrays, *weights)
 
-    crossing = jnp.max(received[:, TILE, TILE + 1].astype(jnp.int32)).reshape(1)
+    crossing = jnp.max(received[:, 0, NOTE + TILE + 1].astype(jnp.int32)).reshape(1)
     crossing_other = lax.ppermute(crossing, "seq", to_other)
     out = second(received, from_below, from_above, local)
 

time: 138 us -> 136 us (0.986)
  waiting for transfers between devices: 14.4 us -> 13 us
    all_to_all x1, waiting for transfers between devices: 14.4 us -> 13 us  [among_chips(): lax.all_to_all(array, 'seq', split_axis=0, concat_axis=0, tiled=True, axi...]
where the time goes in v7:
time: 136 us; the launch traced here: 135 us
  Pallas kernels  101 us (74%)
  starting transfers between devices  18.9 us (14%)
  waiting for transfers between devices  13 us (10%)
  between operations  1.54 us (1%)
    pallas_call x1, Pallas kernels, second(): pl.pallas_call(functools.partial(second_kernel, sources=len(arrays)), in_...  51.4 us
    pallas_call x1, Pallas kernels, shards(): pl.pallas_call(first_kernel, in_specs=[SMEM, SMEM, VMEM, VMEM, VMEM, VMEM...  49.3 us
    all_to_all x1, waiting for transfers between devices, among_chips(): lax.all_to_all(array, 'seq', split_axis=0, concat_axis=0, tiled=True, axi...  13 us
    all_to_all x1, starting transfers between devices, among_chips(): lax.all_to_all(array, 'seq', split_axis=0, concat_axis=0, tiled=True, axi...  11.6 us
    ppermute x1, starting transfers between devices, shards(): from_above = lax.ppermute(down, 'seq', to_below)  7.16 us
  transfers between devices with their start and end apart: 4, of which 1 were waited for; matrix products, arithmetic and copies ran while one was open for 1% of the time, Pallas kernels for 38%

profile of v7, /device:TPU:0, one launch (start us, length us, event | category | flops | bytes accessed | tf_op | source)
XLA Modules:
  0.0 134.8 jit_solution(15483016880971214804)
XLA Ops:
  0.0 49.3 %first_block.1 = (bf16[64,8,1152]{2,1,0:T(8,128)(2,1)}, bf16[64,8,1152]{2,1,0:T(8,128)(2,1)}, bf16[3,8,1152]{2,1,0:T(8,128)(2,1)}, bf16[3,8,1152]{2,1,0:T(8,128)(2,1)}, bf16[32,8,1152]{2,1,0:T(8,128)(2,1)}) custom-call(s32[1]{0:T(128)} %bitcast.me_ref, s32[1024]{0:T(1024)} %rank_ref.1, bf16[1024,256]{1,0:T(8,128)(2,1)} %x.1, s32[8,128]{1,0:T(8,128)} %bitcast.4, ...), custom_call_target="tpu_custom_call" | custom-call | tf_op jit(solution)/shard_map/first_block/pallas_call | solution.py:496
  49.3 0.0 copy-start
  49.3 0.0 copy-start.1
  49.3 0.0 copy-start.4
  49.3 0.0 copy-start.5
  49.3 11.6 %all-to-all-start.1 = ((bf16[64,8,1152]{2,1,0:T(8,128)(2,1)}), bf16[64,8,1152]{2,1,0:T(8,128)(2,1)S(1)}, u32[]{:S(2)}, u32[]{:S(2)}) async-start(bf16[64,8,1152]{2,1,0:T(8,128)(2,1)} %get-tuple-element.47), calls=%async_computation.1 | async-start | bytes 2359296 | tf_op jit(solution)/shard_map/all_to_all | solution.py:492
  61.0 0.1 collective-permute-start.2
  61.1 7.2 %collective-permute-start.3 = (bf16[3,8,1152]{2,1,0:T(8,128)(2,1)}, bf16[3,8,1152]{2,1,0:T(8,128)(2,1)}, u32[]{:S(2)}, u32[]{:S(2)}) collective-permute-start(bf16[3,8,1152]{2,1,0:T(8,128)(2,1)} %get-tuple-element.49), channel_id=1, source_target_pairs={{0,127},{1,0},{2,1},{3,2},{4,3},{5,4},{6,5},{7,6},{8,7},{9,8},{10,... | collective-permute-start | bytes 165896 | tf_op jit(solution)/shard_map/ppermute | solution.py:513
  68.2 13.0 %all-to-all-done.1.refs_0_ = bf16[64,8,1152]{2,1,0:T(8,128)(2,1)S(1)} async-done(((bf16[64,8,1152]{2,1,0:T(8,128)(2,1)}), bf16[64,8,1152]{2,1,0:T(8,128)(2,1)S(1)}, u32[]{:S(2)}, u32[]{:S(2)}) %all-to-all-start.1) | async-done | bytes 1179680 | tf_op jit(solution)/shard_map/all_to_all | solution.py:492
  81.2 0.7 fusion
  82.0 0.0 collective-permute-start.1
  82.0 0.0 collective-permute-done.2.refs_1_
  82.0 0.0 collective-permute-done.3.refs_2_
  82.0 0.0 copy-done
  82.0 0.0 copy-done.1
  82.0 0.0 copy-done.4
  82.0 0.0 copy-done.5
  82.0 0.0 copy-start.2
  82.0 0.0 copy-start.3
  82.0 0.0 copy-start.6
  82.0 51.4 %second_block.3 = bf16[1024,256]{1,0:T(8,128)(2,1)} custom-call(s32[1]{0:T(128)} %bitcast.me_ref, f32[2,2,256]{2,1,0:T(2,128)S(1)} %copy-done.5, bf16[64,8,1152]{2,1,0:T(8,128)(2,1)S(1)} %all-to-all-done.1.refs_0_, bf16[3,8,1152]{2,1,0:T(8,128)(2,1)} %collective-permute-done.2.refs_1_, bf16[3,8,1152]{2,1,0:T(8,128)(2,1)} %collective-permute-done.3.refs_2_, ...), custom_call_target="tpu_custom_call" | custom-call | tf_op jit(solution)/shard_map/second_block/pallas_call | solution.py:516
  133.4 0.0 collective-permute-done.1
  134.6 0.0 copy-done.2
  134.7 0.0 copy-done.3
  134.7 0.0 copy-done.6
  (1 shorter events, 0.0 us)
Async XLA Ops:
  49.3 32.7 %copy-start = (bf16[2,256,1024]{2,1,0:T(8,128)(2,1)S(1)}, bf16[2,256,1024]{2,1,0:T(8,128)(2,1)}, u32[]{:S(2)}) copy-start(bf16[2,256,1024]{2,1,0:T(8,128)(2,1)} %refs_6_.1) | copy-start | bytes 3145732
  49.3 32.7 %copy-start.1 = (bf16[2,1024,256]{2,1,0:T(8,128)(2,1)S(1)}, bf16[2,1024,256]{2,1,0:T(8,128)(2,1)}, u32[]{:S(2)}) copy-start(bf16[2,1024,256]{2,1,0:T(8,128)(2,1)} %refs_7_.1) | copy-start | bytes 3145732
  49.3 32.7 %copy-start.4 = (bf16[2,256,256]{2,1,0:T(8,128)(2,1)S(1)}, bf16[2,256,256]{2,1,0:T(8,128)(2,1)}, u32[]{:S(2)}) copy-start(bf16[2,256,256]{2,1,0:T(8,128)(2,1)} %refs_5_.1) | copy-start | bytes 786436
  49.3 32.7 %copy-start.5 = (f32[2,2,256]{2,1,0:T(2,128)S(1)}, f32[2,2,256]{2,1,0:T(2,128)}, u32[]{:S(2)}) copy-start(f32[2,2,256]{2,1,0:T(2,128)} %gains.3) | copy-start | bytes 12292
  49.3 31.9 %all-to-all-start.1 = ((bf16[64,8,1152]{2,1,0:T(8,128)(2,1)}), bf16[64,8,1152]{2,1,0:T(8,128)(2,1)S(1)}, u32[]{:S(2)}, u32[]{:S(2)}) async-start(bf16[64,8,1152]{2,1,0:T(8,128)(2,1)} %get-tuple-element.47), calls=%async_computation.1 | async-start | bytes 2359296 | tf_op jit(solution)/shard_map/all_to_all | solution.py:492
  61.0 21.0 %collective-permute-start.2 = (bf16[3,8,1152]{2,1,0:T(8,128)(2,1)}, bf16[3,8,1152]{2,1,0:T(8,128)(2,1)}, u32[]{:S(2)}, u32[]{:S(2)}) collective-permute-start(bf16[3,8,1152]{2,1,0:T(8,128)(2,1)} %get-tuple-element.48), channel_id=1, source_target_pairs={{0,1},{1,2},{2,3},{3,4},{4,5},{5,6},{6,7},{7,8},{8,9},{9,10},{10,1... | collective-permute-start | bytes 165896 | tf_op jit(solution)/shard_map/ppermute | solution.py:512
  61.1 20.9 %collective-permute-start.3 = (bf16[3,8,1152]{2,1,0:T(8,128)(2,1)}, bf16[3,8,1152]{2,1,0:T(8,128)(2,1)}, u32[]{:S(2)}, u32[]{:S(2)}) collective-permute-start(bf16[3,8,1152]{2,1,0:T(8,128)(2,1)} %get-tuple-element.49), channel_id=1, source_target_pairs={{0,127},{1,0},{2,1},{3,2},{4,3},{5,4},{6,5},{7,6},{8,7},{9,8},{10,... | collective-permute-start | bytes 165896 | tf_op jit(solution)/shard_map/ppermute | solution.py:513
  82.0 51.5 %collective-permute-start.1 = (s32[1]{0:T(128)}, s32[1]{0:T(128)}, u32[]{:S(2)}, u32[]{:S(2)}) collective-permute-start(s32[1]{0:T(128)} %bitcast.2), channel_id=1, source_target_pairs={{0,1},{1,0},{2,3},{3,2},{4,5},{5,4},{6,7},{7,6},{8,9},{9,8},{10,11... | collective-permute-start | bytes 20 | tf_op jit(solution)/shard_map/ppermute | solution.py:535
  82.0 52.6 %copy-start.2 = (bf16[2,256,768]{2,1,0:T(8,128)(2,1)S(1)}, bf16[2,256,768]{2,1,0:T(8,128)(2,1)}, u32[]{:S(2)}) copy-start(bf16[2,256,768]{2,1,0:T(8,128)(2,1)} %refs_4_.1) | copy-start | bytes 2359300
  82.0 52.6 %copy-start.3 = (bf16[32,8,1152]{2,1,0:T(8,128)(2,1)S(1)}, bf16[32,8,1152]{2,1,0:T(8,128)(2,1)}, u32[]{:S(2)}) copy-start(bf16[32,8,1152]{2,1,0:T(8,128)(2,1)} %get-tuple-element.50.refs_3_) | copy-start | bytes 1769476
  82.0 52.6 %copy-start.6 = (bf16[64,8,1152]{2,1,0:T(8,128)(2,1)S(1)}, bf16[64,8,1152]{2,1,0:T(8,128)(2,1)}, u32[]{:S(2)}) copy-start(bf16[64,8,1152]{2,1,0:T(8,128)(2,1)} %get-tuple-element.51) | copy-start | bytes 3538948

commit v8 on v7

--- a/solution.py
+++ b/solution.py
@@ -120,8 +120,6 @@
         s.query_split[head, own : own + 32, :] = both
         s.query_split[head, own + 32 : own + 64, :] = both
         s.query_split[head, other : other + 64, :] = jnp.zeros((64, ROWS), F8)
-    squares = query.astype(F32) * query.astype(F32)
-    query_norm = jnp.max(jnp.sum(squares.reshape(HEADS, HEAD, ROWS), axis=1), axis=1, keepdims=True)
 
     row = lax.broadcasted_iota(jnp.int32, (64, 256), 0)
     lane = lax.broadcasted_iota(jnp.int32, (64, 256), 1)
@@ -133,16 +131,13 @@
     column = lax.broadcasted_iota(jnp.int32, (C, 128), 1)
     head_sum = jnp.where(channel // HEAD == column, 1.0, 0.0).astype(BF16)
     key_norm = jnp.zeros((1, 128), F32)
-    highest = jnp.max(jnp.abs(query.astype(F32)))
-    key_high = jnp.zeros((1, C), F32)
+    query_norm = dot(head_sum, query * query, 0, 0)
     for start in range(0, ROWS, ROW_BLOCK):
         rows = slice(start, start + ROW_BLOCK)
         key = dot(s.normed[rows], w_qkv[:, C : 2 * C]).astype(BF16)
         s.key[0, rows] = key[:, 0:128]
         s.key[1, rows] = key[:, 128:256]
-        wide = key.astype(F32)
-        key_high = jnp.maximum(key_high, jnp.max(jnp.abs(wide), axis=0, keepdims=True))
-        norms = dot((wide * wide).astype(BF16), head_sum)
+        norms = dot(key * key, head_sum)
         key_norm = jnp.maximum(key_norm, jnp.max(norms, axis=0, keepdims=True))
         high, low = split(key)
         for quarter in range(4):
@@ -151,9 +146,9 @@
             expanded = dot(pair, spread).astype(F8)
             s.key_split[2 * quarter, rows] = expanded[:, 0:128]
             s.key_split[2 * quarter + 1, rows] = expanded[:, 128:256]
-    largest = jnp.maximum(highest, jnp.max(key_high))
-    bound = 0.25 * 1.02 * jnp.sqrt(jnp.max(query_norm) * jnp.max(key_norm))
-    return bound, largest
+    query_norm, key_norm = jnp.max(query_norm), jnp.max(key_norm)
+    bound = 0.25 * 1.02 * jnp.sqrt(query_norm * key_norm)
+    return bound, 1.02 * jnp.sqrt(jnp.maximum(query_norm, key_norm))
 
 
 def make_mask(keys, count, index, scenes, s):
@@ -542,7 +537,7 @@
         return out
 
     return lax.cond(
-        jnp.maximum(crossing, crossing_other)[0] > 0, with_crossing, without_crossing,
+        jnp.max(jnp.concatenate([crossing, crossing_other])) > 0, with_crossing, without_crossing,
         out, send_other, received, from_below, from_above, local,
     )
 

time: 136 us -> 136 us (level)
  no operation moved by 1% of the time
where the time goes in v8:
time: 136 us; the launch traced here: 135 us
  Pallas kernels  101 us (74%)
  starting transfers between devices  18.9 us (14%)
  waiting for transfers between devices  13 us (10%)
  between operations  1.45 us (1%)
    pallas_call x1, Pallas kernels, second(): pl.pallas_call(functools.partial(second_kernel, sources=len(arrays)), in_...  51.5 us
    pallas_call x1, Pallas kernels, shards(): pl.pallas_call(first_kernel, in_specs=[SMEM, SMEM, VMEM, VMEM, VMEM, VMEM...  49 us
    all_to_all x1, waiting for transfers between devices, among_chips(): lax.all_to_all(array, 'seq', split_axis=0, concat_axis=0, tiled=True, axi...  13 us
    all_to_all x1, starting transfers between devices, among_chips(): lax.all_to_all(array, 'seq', split_axis=0, concat_axis=0, tiled=True, axi...  11.6 us
    ppermute x1, starting transfers between devices, shards(): from_above = lax.ppermute(down, 'seq', to_below)  7.16 us
  transfers between devices with their start and end apart: 4, of which 1 were waited for; matrix products, arithmetic and copies ran while one was open for 1% of the time, Pallas kernels for 38%

profile of v8, /device:TPU:0, one launch (start us, length us, event | category | flops | bytes accessed | tf_op | source)
XLA Modules:
  0.0 134.7 jit_solution(58118870797965632)
XLA Ops:
  0.0 49.0 %first_block.1 = (bf16[64,8,1152]{2,1,0:T(8,128)(2,1)}, bf16[64,8,1152]{2,1,0:T(8,128)(2,1)}, bf16[3,8,1152]{2,1,0:T(8,128)(2,1)}, bf16[3,8,1152]{2,1,0:T(8,128)(2,1)}, bf16[32,8,1152]{2,1,0:T(8,128)(2,1)}) custom-call(s32[1]{0:T(128)} %bitcast.me_ref, s32[1024]{0:T(1024)} %rank_ref.1, bf16[1024,256]{1,0:T(8,128)(2,1)} %x.1, s32[8,128]{1,0:T(8,128)} %bitcast.4, ...), custom_call_target="tpu_custom_call" | custom-call | tf_op jit(solution)/shard_map/first_block/pallas_call | solution.py:491
  49.1 0.0 copy-start
  49.1 0.0 copy-start.1
  49.1 0.0 copy-start.4
  49.1 0.0 copy-start.5
  49.1 11.6 %all-to-all-start.1 = ((bf16[64,8,1152]{2,1,0:T(8,128)(2,1)}), bf16[64,8,1152]{2,1,0:T(8,128)(2,1)S(1)}, u32[]{:S(2)}, u32[]{:S(2)}) async-start(bf16[64,8,1152]{2,1,0:T(8,128)(2,1)} %get-tuple-element.47), calls=%async_computation.1 | async-start | bytes 2359296 | tf_op jit(solution)/shard_map/all_to_all | solution.py:487
  60.7 0.1 collective-permute-start.2
  60.8 7.2 %collective-permute-start.3 = (bf16[3,8,1152]{2,1,0:T(8,128)(2,1)}, bf16[3,8,1152]{2,1,0:T(8,128)(2,1)}, u32[]{:S(2)}, u32[]{:S(2)}) collective-permute-start(bf16[3,8,1152]{2,1,0:T(8,128)(2,1)} %get-tuple-element.49), channel_id=1, source_target_pairs={{0,127},{1,0},{2,1},{3,2},{4,3},{5,4},{6,5},{7,6},{8,7},{9,8},{10,... | collective-permute-start | bytes 165896 | tf_op jit(solution)/shard_map/ppermute | solution.py:508
  68.0 13.0 %all-to-all-done.1.refs_0_ = bf16[64,8,1152]{2,1,0:T(8,128)(2,1)S(1)} async-done(((bf16[64,8,1152]{2,1,0:T(8,128)(2,1)}), bf16[64,8,1152]{2,1,0:T(8,128)(2,1)S(1)}, u32[]{:S(2)}, u32[]{:S(2)}) %all-to-all-start.1) | async-done | bytes 1179680 | tf_op jit(solution)/shard_map/all_to_all | solution.py:487
  81.0 0.8 fusion
  81.8 0.0 collective-permute-start.1
  81.8 0.0 collective-permute-done.2.refs_1_
  81.8 0.0 collective-permute-done.3.refs_2_
  81.8 0.0 copy-done
  81.8 0.0 copy-done.1
  81.8 0.0 copy-done.4
  81.8 0.0 copy-done.5
  81.9 51.5 %second_block.3 = bf16[1024,256]{1,0:T(8,128)(2,1)} custom-call(s32[1]{0:T(128)} %bitcast.me_ref, f32[2,2,256]{2,1,0:T(2,128)S(1)} %copy-done.5, bf16[64,8,1152]{2,1,0:T(8,128)(2,1)S(1)} %all-to-all-done.1.refs_0_, bf16[3,8,1152]{2,1,0:T(8,128)(2,1)} %collective-permute-done.2.refs_1_, bf16[3,8,1152]{2,1,0:T(8,128)(2,1)} %collective-permute-done.3.refs_2_, ...), custom_call_target="tpu_custom_call" | custom-call | tf_op jit(solution)/shard_map/second_block/pallas_call | solution.py:511
  133.4 0.0 collective-permute-done.1
  (1 shorter events, 0.0 us)
Async XLA Ops:
  49.1 32.8 %copy-start = (bf16[2,256,1024]{2,1,0:T(8,128)(2,1)S(1)}, bf16[2,256,1024]{2,1,0:T(8,128)(2,1)}, u32[]{:S(2)}) copy-start(bf16[2,256,1024]{2,1,0:T(8,128)(2,1)} %refs_6_.1) | copy-start | bytes 3145732
  49.1 32.8 %copy-start.1 = (bf16[2,1024,256]{2,1,0:T(8,128)(2,1)S(1)}, bf16[2,1024,256]{2,1,0:T(8,128)(2,1)}, u32[]{:S(2)}) copy-start(bf16[2,1024,256]{2,1,0:T(8,128)(2,1)} %refs_7_.1) | copy-start | bytes 3145732
  49.1 32.8 %copy-start.4 = (bf16[2,256,256]{2,1,0:T(8,128)(2,1)S(1)}, bf16[2,256,256]{2,1,0:T(8,128)(2,1)}, u32[]{:S(2)}) copy-start(bf16[2,256,256]{2,1,0:T(8,128)(2,1)} %refs_5_.1) | copy-start | bytes 786436
  49.1 32.8 %copy-start.5 = (f32[2,2,256]{2,1,0:T(2,128)S(1)}, f32[2,2,256]{2,1,0:T(2,128)}, u32[]{:S(2)}) copy-start(f32[2,2,256]{2,1,0:T(2,128)} %gains.3) | copy-start | bytes 12292
  49.1 31.9 %all-to-all-start.1 = ((bf16[64,8,1152]{2,1,0:T(8,128)(2,1)}), bf16[64,8,1152]{2,1,0:T(8,128)(2,1)S(1)}, u32[]{:S(2)}, u32[]{:S(2)}) async-start(bf16[64,8,1152]{2,1,0:T(8,128)(2,1)} %get-tuple-element.47), calls=%async_computation.1 | async-start | bytes 2359296 | tf_op jit(solution)/shard_map/all_to_all | solution.py:487
  60.7 21.1 %collective-permute-start.2 = (bf16[3,8,1152]{2,1,0:T(8,128)(2,1)}, bf16[3,8,1152]{2,1,0:T(8,128)(2,1)}, u32[]{:S(2)}, u32[]{:S(2)}) collective-permute-start(bf16[3,8,1152]{2,1,0:T(8,128)(2,1)} %get-tuple-element.48), channel_id=1, source_target_pairs={{0,1},{1,2},{2,3},{3,4},{4,5},{5,6},{6,7},{7,8},{8,9},{9,10},{10,1... | collective-permute-start | bytes 165896 | tf_op jit(solution)/shard_map/ppermute | solution.py:507
  60.8 21.0 %collective-permute-start.3 = (bf16[3,8,1152]{2,1,0:T(8,128)(2,1)}, bf16[3,8,1152]{2,1,0:T(8,128)(2,1)}, u32[]{:S(2)}, u32[]{:S(2)}) collective-permute-start(bf16[3,8,1152]{2,1,0:T(8,128)(2,1)} %get-tuple-element.49), channel_id=1, source_target_pairs={{0,127},{1,0},{2,1},{3,2},{4,3},{5,4},{6,5},{7,6},{8,7},{9,8},{10,... | collective-permute-start | bytes 165896 | tf_op jit(solution)/shard_map/ppermute | solution.py:508
  81.8 51.6 %collective-permute-start.1 = (s32[1]{0:T(128)}, s32[1]{0:T(128)}, u32[]{:S(2)}, u32[]{:S(2)}) collective-permute-start(s32[1]{0:T(128)} %bitcast.2), channel_id=1, source_target_pairs={{0,1},{1,0},{2,3},{3,2},{4,5},{5,4},{6,7},{7,6},{8,9},{9,8},{10,11... | collective-permute-start | bytes 20 | tf_op jit(solution)/shard_map/ppermute | solution.py:530

commit v9 on v7

--- a/solution.py
+++ b/solution.py
@@ -286,7 +286,7 @@
     entry = lax.broadcasted_iota(jnp.int32, (total, 128), 0)
     table = jnp.where(lane == TILE + 2, entry % 128, jnp.where(lane == TILE + 3, entry // 128, table.astype(jnp.int32)))
     ordered = dot(chosen, table.astype(F32).astype(BF16)).astype(jnp.int32)
-    plan_out[...] = ordered
+    plan_out[0:TILES] = ordered
     group = lax.broadcasted_iota(jnp.int32, (1, 128), 1) // TILE
     lines = jnp.zeros((ROWS // 128, 128), jnp.int32)
     for part in range(4):
@@ -393,7 +393,7 @@
     )
     entries = [(array, *first) for array, first in zip(arrays, firsts, strict=True)]
     sort_tiles(entries, plan_vmem, scenes)
-    to_scalars = pltpu.make_async_copy(plan_vmem, plan, plan_sem)
+    to_scalars = pltpu.make_async_copy(plan_vmem.at[0:TILES], plan, plan_sem)
     to_scalars.start()
     scene_columns(scenes, s)
     to_scalars.wait()
@@ -520,7 +520,7 @@
             out_shape=pltpu.HBM((ROWS, C), BF16),
             scratch_shapes=[
                 pltpu.VMEM((ROWS, C), F32),
-                pltpu.VMEM((TILES, 128), jnp.int32),
+                pltpu.VMEM((TILES + 8, 128), jnp.int32),
                 pltpu.VMEM((ROWS // 128, 128), jnp.int32),
                 pltpu.VMEM((ROWS, C), BF16),
                 pltpu.SMEM((TILES, 128), jnp.int32),

time: 136 us -> 137 us (level)
  no operation moved by 1% of the time
where the time goes in v9:
time: 137 us; the launch traced here: 135 us
  Pallas kernels  101 us (74%)
  starting transfers between devices  18.9 us (14%)
  waiting for transfers between devices  13 us (9%)
  between operations  1.54 us (1%)
    pallas_call x1, Pallas kernels, second(): pl.pallas_call(functools.partial(second_kernel, sources=len(arrays)), in_...  51.4 us
    pallas_call x1, Pallas kernels, shards(): pl.pallas_call(first_kernel, in_specs=[SMEM, SMEM, VMEM, VMEM, VMEM, VMEM...  49.3 us
    all_to_all x1, waiting for transfers between devices, among_chips(): lax.all_to_all(array, 'seq', split_axis=0, concat_axis=0, tiled=True, axi...  13 us
    all_to_all x1, starting transfers between devices, among_chips(): lax.all_to_all(array, 'seq', split_axis=0, concat_axis=0, tiled=True, axi...  11.6 us
    ppermute x1, starting transfers between devices, shards(): from_above = lax.ppermute(down, 'seq', to_below)  7.16 us
  transfers between devices with their start and end apart: 4, of which 1 were waited for; matrix products, arithmetic and copies ran while one was open for 1% of the time, Pallas kernels for 38%

profile of v9, /device:TPU:0, one launch (start us, length us, event | category | flops | bytes accessed | tf_op | source)
XLA Modules:
  0.0 134.9 jit_solution(6976720732060707958)
XLA Ops:
  0.0 49.3 %first_block.1 = (bf16[64,8,1152]{2,1,0:T(8,128)(2,1)}, bf16[64,8,1152]{2,1,0:T(8,128)(2,1)}, bf16[3,8,1152]{2,1,0:T(8,128)(2,1)}, bf16[3,8,1152]{2,1,0:T(8,128)(2,1)}, bf16[32,8,1152]{2,1,0:T(8,128)(2,1)}) custom-call(s32[1]{0:T(128)} %bitcast.me_ref, s32[1024]{0:T(1024)} %rank_ref.1, bf16[1024,256]{1,0:T(8,128)(2,1)} %x.1, s32[8,128]{1,0:T(8,128)} %bitcast.4, ...), custom_call_target="tpu_custom_call" | custom-call | tf_op jit(solution)/shard_map/first_block/pallas_call | solution.py:496
  49.3 0.0 copy-start
  49.3 0.0 copy-start.1
  49.3 0.0 copy-start.4
  49.3 0.0 copy-start.5
  49.3 11.6 %all-to-all-start.1 = ((bf16[64,8,1152]{2,1,0:T(8,128)(2,1)}), bf16[64,8,1152]{2,1,0:T(8,128)(2,1)S(1)}, u32[]{:S(2)}, u32[]{:S(2)}) async-start(bf16[64,8,1152]{2,1,0:T(8,128)(2,1)} %get-tuple-element.47), calls=%async_computation.1 | async-start | bytes 2359296 | tf_op jit(solution)/shard_map/all_to_all | solution.py:492
  61.0 0.1 collective-permute-start.2
  61.1 7.2 %collective-permute-start.3 = (bf16[3,8,1152]{2,1,0:T(8,128)(2,1)}, bf16[3,8,1152]{2,1,0:T(8,128)(2,1)}, u32[]{:S(2)}, u32[]{:S(2)}) collective-permute-start(bf16[3,8,1152]{2,1,0:T(8,128)(2,1)} %get-tuple-element.49), channel_id=1, source_target_pairs={{0,127},{1,0},{2,1},{3,2},{4,3},{5,4},{6,5},{7,6},{8,7},{9,8},{10,... | collective-permute-start | bytes 165896 | tf_op jit(solution)/shard_map/ppermute | solution.py:513
  68.2 13.0 %all-to-all-done.1.refs_0_ = bf16[64,8,1152]{2,1,0:T(8,128)(2,1)S(1)} async-done(((bf16[64,8,1152]{2,1,0:T(8,128)(2,1)}), bf16[64,8,1152]{2,1,0:T(8,128)(2,1)S(1)}, u32[]{:S(2)}, u32[]{:S(2)}) %all-to-all-start.1) | async-done | bytes 1179680 | tf_op jit(solution)/shard_map/all_to_all | solution.py:492
  81.2 0.7 fusion
  82.0 0.0 collective-permute-start.1
  82.0 0.0 collective-permute-done.2.refs_1_
  82.0 0.0 collective-permute-done.3.refs_2_
  82.0 0.0 copy-done
  82.0 0.0 copy-done.1
  82.0 0.0 copy-done.4
  82.0 0.0 copy-done.5
  82.0 0.0 copy-start.2
  82.0 0.0 copy-start.3
  82.0 0.0 copy-start.6
  82.0 51.4 %second_block.3 = bf16[1024,256]{1,0:T(8,128)(2,1)} custom-call(s32[1]{0:T(128)} %bitcast.me_ref, f32[2,2,256]{2,1,0:T(2,128)S(1)} %copy-done.5, bf16[64,8,1152]{2,1,0:T(8,128)(2,1)S(1)} %all-to-all-done.1.refs_0_, bf16[3,8,1152]{2,1,0:T(8,128)(2,1)} %collective-permute-done.2.refs_1_, bf16[3,8,1152]{2,1,0:T(8,128)(2,1)} %collective-permute-done.3.refs_2_, ...), custom_call_target="tpu_custom_call" | custom-call | tf_op jit(solution)/shard_map/second_block/pallas_call | solution.py:516
  133.5 0.0 collective-permute-done.1
  134.7 0.0 copy-done.2
  134.7 0.0 copy-done.3
  134.7 0.0 copy-done.6
  (1 shorter events, 0.0 us)
Async XLA Ops:
  49.3 32.7 %copy-start = (bf16[2,256,1024]{2,1,0:T(8,128)(2,1)S(1)}, bf16[2,256,1024]{2,1,0:T(8,128)(2,1)}, u32[]{:S(2)}) copy-start(bf16[2,256,1024]{2,1,0:T(8,128)(2,1)} %refs_6_.1) | copy-start | bytes 3145732
  49.3 32.7 %copy-start.1 = (bf16[2,1024,256]{2,1,0:T(8,128)(2,1)S(1)}, bf16[2,1024,256]{2,1,0:T(8,128)(2,1)}, u32[]{:S(2)}) copy-start(bf16[2,1024,256]{2,1,0:T(8,128)(2,1)} %refs_7_.1) | copy-start | bytes 3145732
  49.3 32.7 %copy-start.4 = (bf16[2,256,256]{2,1,0:T(8,128)(2,1)S(1)}, bf16[2,256,256]{2,1,0:T(8,128)(2,1)}, u32[]{:S(2)}) copy-start(bf16[2,256,256]{2,1,0:T(8,128)(2,1)} %refs_5_.1) | copy-start | bytes 786436
  49.3 32.7 %copy-start.5 = (f32[2,2,256]{2,1,0:T(2,128)S(1)}, f32[2,2,256]{2,1,0:T(2,128)}, u32[]{:S(2)}) copy-start(f32[2,2,256]{2,1,0:T(2,128)} %gains.3) | copy-start | bytes 12292
  49.3 31.9 %all-to-all-start.1 = ((bf16[64,8,1152]{2,1,0:T(8,128)(2,1)}), bf16[64,8,1152]{2,1,0:T(8,128)(2,1)S(1)}, u32[]{:S(2)}, u32[]{:S(2)}) async-start(bf16[64,8,1152]{2,1,0:T(8,128)(2,1)} %get-tuple-element.47), calls=%async_computation.1 | async-start | bytes 2359296 | tf_op jit(solution)/shard_map/all_to_all | solution.py:492
  61.0 21.0 %collective-permute-start.2 = (bf16[3,8,1152]{2,1,0:T(8,128)(2,1)}, bf16[3,8,1152]{2,1,0:T(8,128)(2,1)}, u32[]{:S(2)}, u32[]{:S(2)}) collective-permute-start(bf16[3,8,1152]{2,1,0:T(8,128)(2,1)} %get-tuple-element.48), channel_id=1, source_target_pairs={{0,1},{1,2},{2,3},{3,4},{4,5},{5,6},{6,7},{7,8},{8,9},{9,10},{10,1... | collective-permute-start | bytes 165896 | tf_op jit(solution)/shard_map/ppermute | solution.py:512
  61.1 20.9 %collective-permute-start.3 = (bf16[3,8,1152]{2,1,0:T(8,128)(2,1)}, bf16[3,8,1152]{2,1,0:T(8,128)(2,1)}, u32[]{:S(2)}, u32[]{:S(2)}) collective-permute-start(bf16[3,8,1152]{2,1,0:T(8,128)(2,1)} %get-tuple-element.49), channel_id=1, source_target_pairs={{0,127},{1,0},{2,1},{3,2},{4,3},{5,4},{6,5},{7,6},{8,7},{9,8},{10,... | collective-permute-start | bytes 165896 | tf_op jit(solution)/shard_map/ppermute | solution.py:513
  82.0 51.5 %collective-permute-start.1 = (s32[1]{0:T(128)}, s32[1]{0:T(128)}, u32[]{:S(2)}, u32[]{:S(2)}) collective-permute-start(s32[1]{0:T(128)} %bitcast.2), channel_id=1, source_target_pairs={{0,1},{1,0},{2,3},{3,2},{4,5},{5,4},{6,7},{7,6},{8,9},{9,8},{10,11... | collective-permute-start | bytes 20 | tf_op jit(solution)/shard_map/ppermute | solution.py:535
  82.0 52.7 %copy-start.2 = (bf16[2,256,768]{2,1,0:T(8,128)(2,1)S(1)}, bf16[2,256,768]{2,1,0:T(8,128)(2,1)}, u32[]{:S(2)}) copy-start(bf16[2,256,768]{2,1,0:T(8,128)(2,1)} %refs_4_.1) | copy-start | bytes 2359300
  82.0 52.7 %copy-start.3 = (bf16[32,8,1152]{2,1,0:T(8,128)(2,1)S(1)}, bf16[32,8,1152]{2,1,0:T(8,128)(2,1)}, u32[]{:S(2)}) copy-start(bf16[32,8,1152]{2,1,0:T(8,128)(2,1)} %get-tuple-element.50.refs_3_) | copy-start | bytes 1769476
  82.0 52.7 %copy-start.6 = (bf16[64,8,1152]{2,1,0:T(8,128)(2,1)S(1)}, bf16[64,8,1152]{2,1,0:T(8,128)(2,1)}, u32[]{:S(2)}) copy-start(bf16[64,8,1152]{2,1,0:T(8,128)(2,1)} %get-tuple-element.51) | copy-start | bytes 3538948
